TPU v7x, 32 devices: a whole 2x2x4 slice. The times are simulated.
32 devices in a mesh: span: 4 (over z), stream: 8 (over y, x, core).
Axes of the slice: x: 2, y: 2, z: 4, core: 2. Of those that a mesh axis runs over, the one named last changes fastest.
Arguments:
- right_side: float32 [64, 65536], P(None, ('span', 'stream')), may hold values from -6 to 6
- start_guess: float32 [64, 65536], P(None, ('span', 'stream')), may hold values from -6 to 6
- fine_matrix: bfloat16 [512, 5, 128, 128], P(('span', 'stream'))
- fine_columns: int32 [512, 5], P(('span', 'stream')), may hold values from 0 to 31, as said below
- send_lists: int32 [32, 16], P(('span', 'stream')), may hold values from 0 to 15
- aggregates: int32 [65536], P(('span', 'stream')), may hold values from 0 to 127
- coarse_matrix: float32 [32, 5, 128, 128], P(('span', 'stream'))
Outputs:
- solution: float32 [64, 65536], P(None, ('span', 'stream'))
- coarse_correction: float32 [64, 4096], P(None, ('span', 'stream'))
Inputs may be any that keep to these rules, and one draw needn't show every extreme that they name: `fine_columns`: entry 0 of each block row is the row block itself (its local index); the entries of one block row are distinct; entries below 16 name local blocks, entry 16 + d * 4 + h names received slot h from neighbour d; on every device every received slot is named by some block row.
All inputs are finite; a program needn't handle non-finite values.
Results may differ from a plain program's by a relative error of at most 0.0003.
Values sent between devices are 32-bit elements; how exact they have to be, the bound alone decides.
No kernel may reach another device: no remote copies, remote signals or barrier semaphores. Data moves between devices by JAX's collectives and lax.ppermute only.
A program may use at most 64 MiB of HBM per device.

v0:
```python
import jax
import jax.numpy as jnp
from jax import lax
from jax.sharding import PartitionSpec as P

center_value = 1.1
radius_value = 0.9
highest = lax.Precision.HIGHEST


def extended_2(block, sides, width):
    for axis, dim in sides:
        count = lax.axis_size(axis)
        forward = [(i, i + 1) for i in range(count - 1)]
        backward = [(target, source) for source, target in forward]
        low = lax.ppermute(
            lax.slice_in_dim(block, block.shape[dim] - width, None, axis=dim), axis, forward
        )
        high = lax.ppermute(lax.slice_in_dim(block, 0, width, axis=dim), axis, backward)
        block = jnp.concatenate([low, block, high], axis=dim)
    return block


def smooth(operator, inverse, target, start):
    if start is None:
        residual = target
        iterate = jnp.zeros_like(target)
    else:
        residual = target - operator(start)
        iterate = start
    update = inverse * residual / center_value
    iterate = iterate + update
    weight_old = radius_value / center_value
    for sweep in range(2):
        residual = residual - operator(update)
        weight_now = 1.0 / (2.0 * center_value / radius_value - weight_old)
        update = (
            weight_now * weight_old * update + 2.0 * weight_now / radius_value * inverse * residual
        )
        iterate = iterate + update
        weight_old = weight_now
    return iterate


def span_rim(to_lower, to_upper):
    stacked = jnp.stack([to_lower, to_upper], 0)
    padded = extended_2(stacked, (("span", 0),), 1)
    return (padded[0], padded[3])


def stream_rim(to_lower, to_upper):
    stacked = jnp.stack([to_lower, to_upper], 0)
    padded = extended_2(stacked, (("stream", 0),), 1)
    return (padded[0], padded[3])


def local(
    right_side, start_guess, fine_matrix, fine_columns, send_lists, aggregates, coarse_matrix
):
    vec_count = right_side.shape[0]
    blk_count = fine_matrix.shape[0]
    nnz_count = fine_matrix.shape[1]
    block_size = fine_matrix.shape[2]
    slot_count = send_lists.shape[1] // 4
    lists = send_lists[0]
    flat_cols = fine_columns.reshape(-1)
    fine_inverse = 1.0 / jnp.diagonal(fine_matrix[:, 0], axis1=1, axis2=2).astype(
        jnp.float32
    ).reshape(-1)

    def receive(blocks):
        sends = jnp.take(blocks, lists, axis=1).reshape(vec_count, 4, slot_count, block_size)
        span_low, span_high = span_rim(sends[:, 0], sends[:, 1])
        stream_low, stream_high = stream_rim(sends[:, 2], sends[:, 3])
        return jnp.concatenate([span_low, span_high, stream_low, stream_high], axis=1)

    def block_product(picked):
        return jnp.einsum(
            "rkij,vrkj->vri", fine_matrix.astype(jnp.float32), picked, precision=highest
        )

    def fine_apply(vector):
        blocks = vector.reshape(vec_count, blk_count, block_size)
        received = receive(blocks)
        extended = jnp.concatenate([blocks, received], axis=1)
        picked = jnp.take(extended, flat_cols, axis=1).reshape(
            vec_count, blk_count, nnz_count, block_size
        )
        return block_product(picked).reshape(vec_count, blk_count * block_size)

    first = smooth(fine_apply, fine_inverse, right_side, start_guess)
    leftover = right_side - fine_apply(first)
    one_hot = (aggregates[:, None] == jnp.arange(block_size, dtype=jnp.int32)[None, :]).astype(
        jnp.float32
    )
    coarse_rhs = jnp.dot(leftover, one_hot, precision=highest)
    coarse_inverse = 1.0 / jnp.diagonal(coarse_matrix[0, 0])

    def coarse_apply(vector):
        span_low, span_high = span_rim(vector, vector)
        stream_low, stream_high = stream_rim(vector, vector)
        extended = jnp.stack([vector, span_low, span_high, stream_low, stream_high], 1)
        return jnp.einsum("kij,vkj->vi", coarse_matrix[0], extended, precision=highest)

    correction = smooth(coarse_apply, coarse_inverse, coarse_rhs, None)
    second = first + jnp.dot(correction, one_hot.T, precision=highest)
    solution = smooth(fine_apply, fine_inverse, right_side, second)
    return (solution, correction)


def solution(mesh):
    placed = (
        P(None, ("span", "stream")),
        P(None, ("span", "stream")),
        P(("span", "stream"), None, None, None),
        P(("span", "stream"), None),
        P(("span", "stream"), None),
        P(("span", "stream")),
        P(("span", "stream"), None, None, None),
    )
    return jax.shard_map(
        local,
        mesh=mesh,
        in_specs=placed,
        out_specs=(P(None, ("span", "stream")), P(None, ("span", "stream"))),
        check_vma=False,
    )
```

profile of v0, /device:TPU:0, one launch (start us, length us, event | category | flops | bytes accessed | tf_op | source)
XLA Modules:
  0.0 256.2 jit_solution(17101525419107659535)
XLA Ops:
  10.2 5.6 %collective-permute-start = (f32[1,64,4,128]{3,1,2,0:T(8,128)}, f32[1,64,4,128]{3,1,2,0:T(8,128)S(1)}, u32[]{:S(2)}, u32[]{:S(2)}) collective-permute-start(f32[1,64,4,128]{3,1,2,0:T(8,128)} %get-tuple-element.33), channel_id=1, source_target_pairs={{0,8},{8,16},{16,24},{1,9},{9,17},{17,25},{2,10},{10,18},{18,26},{... | collective-permute-start | bytes 393224 | tf_op jit(solution)/shard_map/ppermute | solution.py:16
  36.0 3.9 %collective-permute-start.4 = (f32[1,64,4,128]{3,1,2,0:T(8,128)S(1)}, f32[1,64,4,128]{3,1,2,0:T(8,128)S(1)}, u32[]{:S(2)}, u32[]{:S(2)}) collective-permute-start(f32[1,64,4,128]{3,1,2,0:T(8,128)S(1)} %get-tuple-element.29), channel_id=1, source_target_pairs={{0,8},{8,16},{16,24},{1,9},{9,17},{17,25},{2,10},{10,18},{18,26},{... | collective-permute-start | bytes 393224 | tf_op jit(solution)/shard_map/ppermute | solution.py:16
  48.2 5.8 %collective-permute-done.5 = f32[1,64,4,128]{3,1,2,0:T(8,128)S(1)} collective-permute-done((f32[1,64,4,128]{3,1,2,0:T(8,128)S(1)}, f32[1,64,4,128]{3,1,2,0:T(8,128)S(1)}, u32[]{:S(2)}, u32[]{:S(2)}) %collective-permute-start.5) | collective-permute-done | bytes 131104 | tf_op jit(solution)/shard_map/ppermute | solution.py:19
  56.0 3.4 %gather_fusion.5 = f32[80,64,128]{2,1,0:T(8,128)} fusion(f32[64,32,128]{2,0,1:T(8,128)} %bitcast_dynamic-update-slice_fusion.20, s32[1024]{0:T(1024)S(1)} %pad_clamp_fusion), kind=kCustom, calls=%fused_computation.8.clone | custom fusion | bytes 5243200 | tf_op jit(solution)/shard_map/jit(_take)/gather | solution.py:86
  61.4 3.3 %convolution_bitcast_fusion.5 = f32[16,8,8,128]{3,2,1,0:T(8,128)S(1)} fusion(f32[64,16,5,128]{3,0,2,1:T(8,128)S(1)} %bitcast.384, bf16[16,5,128,128]{3,2,1,0:T(8,128)(2,1)S(1)} %copy-done), kind=kOutput, calls=%fused_computation.29 | convolution fusion | flops 1006632960 | bytes 5767168 | tf_op jit(solution)/shard_map/rkij,vrkj->vri/dot_general | solution.py:78
  75.8 4.7 %collective-permute-start.8 = (f32[1,64,4,128]{3,1,2,0:T(8,128)S(1)}, f32[1,64,4,128]{3,1,2,0:T(8,128)S(1)}, u32[]{:S(2)}, u32[]{:S(2)}) collective-permute-start(f32[1,64,4,128]{3,1,2,0:T(8,128)S(1)} %get-tuple-element.25), channel_id=1, source_target_pairs={{0,8},{8,16},{16,24},{1,9},{9,17},{17,25},{2,10},{10,18},{18,26},{... | collective-permute-start | bytes 393224 | tf_op jit(solution)/shard_map/ppermute | solution.py:16
  86.6 3.4 %gather_fusion.7 = f32[80,64,128]{2,1,0:T(8,128)} fusion(f32[64,32,128]{2,0,1:T(8,128)} %bitcast_dynamic-update-slice_fusion.16, s32[1024]{0:T(1024)S(1)} %pad_clamp_fusion), kind=kCustom, calls=%fused_computation.9.clone | custom fusion | bytes 5243200 | tf_op jit(solution)/shard_map/jit(_take)/gather | solution.py:86
  92.1 3.3 %convolution_bitcast_fusion.4 = f32[16,8,8,128]{3,2,1,0:T(8,128)S(1)} fusion(f32[64,16,5,128]{3,0,2,1:T(8,128)S(1)} %bitcast.385, bf16[16,5,128,128]{3,2,1,0:T(8,128)(2,1)S(1)} %copy-done), kind=kOutput, calls=%fused_computation.28 | convolution fusion | flops 1006632960 | bytes 5767168 | tf_op jit(solution)/shard_map/rkij,vrkj->vri/dot_general | solution.py:78
  106.5 5.0 %collective-permute-start.12 = (f32[1,64,4,128]{3,1,2,0:T(8,128)S(1)}, f32[1,64,4,128]{3,1,2,0:T(8,128)S(1)}, u32[]{:S(2)}, u32[]{:S(2)}) collective-permute-start(f32[1,64,4,128]{3,1,2,0:T(8,128)S(1)} %get-tuple-element.21), channel_id=1, source_target_pairs={{0,8},{8,16},{16,24},{1,9},{9,17},{17,25},{2,10},{10,18},{18,26},{... | collective-permute-start | bytes 393224 | tf_op jit(solution)/shard_map/ppermute | solution.py:16
  117.8 3.4 %gather_fusion.9 = f32[80,64,128]{2,1,0:T(8,128)} fusion(f32[64,32,128]{2,0,1:T(8,128)} %bitcast_dynamic-update-slice_fusion.12, s32[1024]{0:T(1024)S(1)} %pad_clamp_fusion), kind=kCustom, calls=%fused_computation.10.clone | custom fusion | bytes 5243200 | tf_op jit(solution)/shard_map/jit(_take)/gather | solution.py:86
  127.2 4.4 %collective-permute-start.16 = (f32[1,64,128]{2,1,0:T(8,128)S(1)}, f32[1,64,128]{2,1,0:T(8,128)S(1)}, u32[]{:S(2)}, u32[]{:S(2)}) collective-permute-start(f32[1,64,128]{2,1,0:T(8,128)S(1)} %fusion.19), channel_id=1, source_target_pairs={{0,8},{8,16},{16,24},{1,9},{9,17},{17,25},{2,10},{10,18},{18,26},{... | collective-permute-start | bytes 98312 | tf_op jit(solution)/shard_map/ppermute | solution.py:16
  137.2 4.7 %collective-permute-done.17 = f32[1,64,128]{2,1,0:T(8,128)S(1)} collective-permute-done((f32[1,64,128]{2,1,0:T(8,128)S(1)}, f32[1,64,128]{2,1,0:T(8,128)S(1)}, u32[]{:S(2)}, u32[]{:S(2)}) %collective-permute-start.17) | collective-permute-done | bytes 32800 | tf_op jit(solution)/shard_map/ppermute | solution.py:19
  142.5 4.2 %collective-permute-start.20 = (f32[1,64,128]{2,1,0:T(8,128)S(1)}, f32[1,64,128]{2,1,0:T(8,128)S(1)}, u32[]{:S(2)}, u32[]{:S(2)}) collective-permute-start(f32[1,64,128]{2,1,0:T(8,128)S(1)} %fusion.20), channel_id=1, source_target_pairs={{0,8},{8,16},{16,24},{1,9},{9,17},{17,25},{2,10},{10,18},{18,26},{... | collective-permute-start | bytes 98312 | tf_op jit(solution)/shard_map/ppermute | solution.py:16
  152.3 4.7 %collective-permute-done.21 = f32[1,64,128]{2,1,0:T(8,128)S(1)} collective-permute-done((f32[1,64,128]{2,1,0:T(8,128)S(1)}, f32[1,64,128]{2,1,0:T(8,128)S(1)}, u32[]{:S(2)}, u32[]{:S(2)}) %collective-permute-start.21) | collective-permute-done | bytes 32800 | tf_op jit(solution)/shard_map/ppermute | solution.py:19
  169.7 4.6 %collective-permute-start.24 = (f32[1,64,4,128]{3,1,2,0:T(8,128)S(1)}, f32[1,64,4,128]{3,1,2,0:T(8,128)S(1)}, u32[]{:S(2)}, u32[]{:S(2)}) collective-permute-start(f32[1,64,4,128]{3,1,2,0:T(8,128)S(1)} %get-tuple-element.17), channel_id=1, source_target_pairs={{0,8},{8,16},{16,24},{1,9},{9,17},{17,25},{2,10},{10,18},{18,26},{... | collective-permute-start | bytes 393224 | tf_op jit(solution)/shard_map/ppermute | solution.py:16
  180.7 3.4 %gather_fusion.11 = f32[80,64,128]{2,1,0:T(8,128)} fusion(f32[64,32,128]{2,0,1:T(8,128)} %bitcast_dynamic-update-slice_fusion.8, s32[1024]{0:T(1024)S(1)} %pad_clamp_fusion), kind=kCustom, calls=%fused_computation.11.clone | custom fusion | bytes 5243200 | tf_op jit(solution)/shard_map/jit(_take)/gather | solution.py:86
  186.1 3.3 %convolution_bitcast_fusion.2 = f32[16,8,8,128]{3,2,1,0:T(8,128)S(1)} fusion(f32[64,16,5,128]{3,0,2,1:T(8,128)S(1)} %bitcast.387, bf16[16,5,128,128]{3,2,1,0:T(8,128)(2,1)S(1)} %copy-done), kind=kOutput, calls=%fused_computation.26 | convolution fusion | flops 1006632960 | bytes 5767168 | tf_op jit(solution)/shard_map/rkij,vrkj->vri/dot_general | solution.py:78
  194.6 4.6 %collective-permute-start.28 = (f32[1,64,4,128]{3,1,2,0:T(8,128)S(1)}, f32[1,64,4,128]{3,1,2,0:T(8,128)S(1)}, u32[]{:S(2)}, u32[]{:S(2)}) collective-permute-start(f32[1,64,4,128]{3,1,2,0:T(8,128)S(1)} %get-tuple-element.13), channel_id=1, source_target_pairs={{0,8},{8,16},{16,24},{1,9},{9,17},{17,25},{2,10},{10,18},{18,26},{... | collective-permute-start | bytes 393224 | tf_op jit(solution)/shard_map/ppermute | solution.py:16
  207.5 6.2 %collective-permute-done.29 = f32[1,64,4,128]{3,1,2,0:T(8,128)S(1)} collective-permute-done((f32[1,64,4,128]{3,1,2,0:T(8,128)S(1)}, f32[1,64,4,128]{3,1,2,0:T(8,128)S(1)}, u32[]{:S(2)}, u32[]{:S(2)}) %collective-permute-start.29) | collective-permute-done | bytes 131104 | tf_op jit(solution)/shard_map/ppermute | solution.py:19
  215.7 3.4 %gather_fusion.13 = f32[80,64,128]{2,1,0:T(8,128)} fusion(f32[64,32,128]{2,0,1:T(8,128)} %bitcast_dynamic-update-slice_fusion.4, s32[1024]{0:T(1024)S(1)} %pad_clamp_fusion), kind=kCustom, calls=%fused_computation.12.clone | custom fusion | bytes 5243200 | tf_op jit(solution)/shard_map/jit(_take)/gather | solution.py:86
  221.1 3.3 %convolution_bitcast_fusion.1 = f32[16,8,8,128]{3,2,1,0:T(8,128)S(1)} fusion(f32[64,16,5,128]{3,0,2,1:T(8,128)S(1)} %bitcast.388, bf16[16,5,128,128]{3,2,1,0:T(8,128)(2,1)S(1)} %copy-done), kind=kOutput, calls=%fused_computation.25 | convolution fusion | flops 1006632960 | bytes 5767168 | tf_op jit(solution)/shard_map/rkij,vrkj->vri/dot_general | solution.py:78
  235.5 4.6 %collective-permute-start.32 = (f32[1,64,4,128]{3,1,2,0:T(8,128)S(1)}, f32[1,64,4,128]{3,1,2,0:T(8,128)S(1)}, u32[]{:S(2)}, u32[]{:S(2)}) collective-permute-start(f32[1,64,4,128]{3,1,2,0:T(8,128)S(1)} %get-tuple-element.9), channel_id=1, source_target_pairs={{0,8},{8,16},{16,24},{1,9},{9,17},{17,25},{2,10},{10,18},{18,26},{... | collective-permute-start | bytes 393224 | tf_op jit(solution)/shard_map/ppermute | solution.py:16
  246.5 3.4 %gather_fusion.15 = f32[80,64,128]{2,1,0:T(8,128)} fusion(f32[64,32,128]{2,0,1:T(8,128)} %bitcast_dynamic-update-slice_fusion, s32[1024]{0:T(1024)S(1)} %pad_clamp_fusion), kind=kCustom, calls=%fused_computation.13.clone | custom fusion | bytes 5243200 | tf_op jit(solution)/shard_map/jit(_take)/gather | solution.py:86
  251.9 3.3 %convolution_bitcast_fusion = f32[16,8,8,128]{3,2,1,0:T(8,128)S(1)} fusion(f32[64,16,5,128]{3,0,2,1:T(8,128)S(1)} %bitcast.382, bf16[16,5,128,128]{3,2,1,0:T(8,128)(2,1)S(1)} %copy-done), kind=kOutput, calls=%fused_computation.24 | convolution fusion | flops 1006632960 | bytes 5767168 | tf_op jit(solution)/shard_map/rkij,vrkj->vri/dot_general | solution.py:78
  (218 shorter events, 154.8 us)
Async XLA Ops:
  4.6 18.1 %collective-permute-start.3 = (f32[1,64,4,128]{3,1,2,0:T(8,128)S(1)}, f32[1,64,4,128]{3,1,2,0:T(8,128)S(1)}, u32[]{:S(2)}, u32[]{:S(2)}) collective-permute-start(f32[1,64,4,128]{3,1,2,0:T(8,128)S(1)} %get-tuple-element.30), channel_id=1, source_target_pairs={{1,0},{2,1},{3,2},{4,3},{5,4},{6,5},{7,6},{9,8},{10,9},{11,10},{12... | collective-permute-start | bytes 393224 | tf_op jit(solution)/shard_map/ppermute | solution.py:19
  5.9 16.8 %collective-permute-start.2 = (f32[1,64,4,128]{3,1,2,0:T(8,128)S(1)}, f32[1,64,4,128]{3,1,2,0:T(8,128)S(1)}, u32[]{:S(2)}, u32[]{:S(2)}) collective-permute-start(f32[1,64,4,128]{3,1,2,0:T(8,128)S(1)} %get-tuple-element.31), channel_id=1, source_target_pairs={{0,1},{1,2},{2,3},{3,4},{4,5},{5,6},{6,7},{8,9},{9,10},{10,11},{11... | collective-permute-start | bytes 393224 | tf_op jit(solution)/shard_map/ppermute | solution.py:16
  8.9 13.7 %collective-permute-start.1 = (f32[1,64,4,128]{3,1,2,0:T(8,128)S(1)}, f32[1,64,4,128]{3,1,2,0:T(8,128)S(1)}, u32[]{:S(2)}, u32[]{:S(2)}) collective-permute-start(f32[1,64,4,128]{3,1,2,0:T(8,128)S(1)} %get-tuple-element.32), channel_id=1, source_target_pairs={{8,0},{16,8},{24,16},{9,1},{17,9},{25,17},{10,2},{18,10},{26,18},{... | collective-permute-start | bytes 393224 | tf_op jit(solution)/shard_map/ppermute | solution.py:19
  10.2 12.4 %collective-permute-start = (f32[1,64,4,128]{3,1,2,0:T(8,128)}, f32[1,64,4,128]{3,1,2,0:T(8,128)S(1)}, u32[]{:S(2)}, u32[]{:S(2)}) collective-permute-start(f32[1,64,4,128]{3,1,2,0:T(8,128)} %get-tuple-element.33), channel_id=1, source_target_pairs={{0,8},{8,16},{16,24},{1,9},{9,17},{17,25},{2,10},{10,18},{18,26},{... | collective-permute-start | bytes 393224 | tf_op jit(solution)/shard_map/ppermute | solution.py:16
  36.0 11.5 %collective-permute-start.4 = (f32[1,64,4,128]{3,1,2,0:T(8,128)S(1)}, f32[1,64,4,128]{3,1,2,0:T(8,128)S(1)}, u32[]{:S(2)}, u32[]{:S(2)}) collective-permute-start(f32[1,64,4,128]{3,1,2,0:T(8,128)S(1)} %get-tuple-element.29), channel_id=1, source_target_pairs={{0,8},{8,16},{16,24},{1,9},{9,17},{17,25},{2,10},{10,18},{18,26},{... | collective-permute-start | bytes 393224 | tf_op jit(solution)/shard_map/ppermute | solution.py:16
  41.9 13.5 %collective-permute-start.7 = (f32[1,64,4,128]{3,1,2,0:T(8,128)S(1)}, f32[1,64,4,128]{3,1,2,0:T(8,128)S(1)}, u32[]{:S(2)}, u32[]{:S(2)}) collective-permute-start(f32[1,64,4,128]{3,1,2,0:T(8,128)S(1)} %get-tuple-element.26), channel_id=1, source_target_pairs={{1,0},{2,1},{3,2},{4,3},{5,4},{6,5},{7,6},{9,8},{10,9},{11,10},{12... | collective-permute-start | bytes 393224 | tf_op jit(solution)/shard_map/ppermute | solution.py:19
  43.1 11.5 %collective-permute-start.6 = (f32[1,64,4,128]{3,1,2,0:T(8,128)S(1)}, f32[1,64,4,128]{3,1,2,0:T(8,128)S(1)}, u32[]{:S(2)}, u32[]{:S(2)}) collective-permute-start(f32[1,64,4,128]{3,1,2,0:T(8,128)S(1)} %get-tuple-element.27), channel_id=1, source_target_pairs={{0,1},{1,2},{2,3},{3,4},{4,5},{5,6},{6,7},{8,9},{9,10},{10,11},{11... | collective-permute-start | bytes 393224 | tf_op jit(solution)/shard_map/ppermute | solution.py:16
  70.1 15.8 %collective-permute-start.11 = (f32[1,64,4,128]{3,1,2,0:T(8,128)S(1)}, f32[1,64,4,128]{3,1,2,0:T(8,128)S(1)}, u32[]{:S(2)}, u32[]{:S(2)}) collective-permute-start(f32[1,64,4,128]{3,1,2,0:T(8,128)S(1)} %get-tuple-element.22), channel_id=1, source_target_pairs={{1,0},{2,1},{3,2},{4,3},{5,4},{6,5},{7,6},{9,8},{10,9},{11,10},{12... | collective-permute-start | bytes 393224 | tf_op jit(solution)/shard_map/ppermute | solution.py:19
  71.4 13.8 %collective-permute-start.10 = (f32[1,64,4,128]{3,1,2,0:T(8,128)S(1)}, f32[1,64,4,128]{3,1,2,0:T(8,128)S(1)}, u32[]{:S(2)}, u32[]{:S(2)}) collective-permute-start(f32[1,64,4,128]{3,1,2,0:T(8,128)S(1)} %get-tuple-element.23), channel_id=1, source_target_pairs={{0,1},{1,2},{2,3},{3,4},{4,5},{5,6},{6,7},{8,9},{9,10},{10,11},{11... | collective-permute-start | bytes 393224 | tf_op jit(solution)/shard_map/ppermute | solution.py:16
  74.5 10.1 %collective-permute-start.9 = (f32[1,64,4,128]{3,1,2,0:T(8,128)S(1)}, f32[1,64,4,128]{3,1,2,0:T(8,128)S(1)}, u32[]{:S(2)}, u32[]{:S(2)}) collective-permute-start(f32[1,64,4,128]{3,1,2,0:T(8,128)S(1)} %get-tuple-element.24), channel_id=1, source_target_pairs={{8,0},{16,8},{24,16},{9,1},{17,9},{25,17},{10,2},{18,10},{26,18},{... | collective-permute-start | bytes 393224 | tf_op jit(solution)/shard_map/ppermute | solution.py:19
  100.9 16.3 %collective-permute-start.15 = (f32[1,64,4,128]{3,1,2,0:T(8,128)S(1)}, f32[1,64,4,128]{3,1,2,0:T(8,128)S(1)}, u32[]{:S(2)}, u32[]{:S(2)}) collective-permute-start(f32[1,64,4,128]{3,1,2,0:T(8,128)S(1)} %get-tuple-element.18), channel_id=1, source_target_pairs={{1,0},{2,1},{3,2},{4,3},{5,4},{6,5},{7,6},{9,8},{10,9},{11,10},{12... | collective-permute-start | bytes 393224 | tf_op jit(solution)/shard_map/ppermute | solution.py:19
  102.2 14.3 %collective-permute-start.14 = (f32[1,64,4,128]{3,1,2,0:T(8,128)S(1)}, f32[1,64,4,128]{3,1,2,0:T(8,128)S(1)}, u32[]{:S(2)}, u32[]{:S(2)}) collective-permute-start(f32[1,64,4,128]{3,1,2,0:T(8,128)S(1)} %get-tuple-element.19), channel_id=1, source_target_pairs={{0,1},{1,2},{2,3},{3,4},{4,5},{5,6},{6,7},{8,9},{9,10},{10,11},{11... | collective-permute-start | bytes 393224 | tf_op jit(solution)/shard_map/ppermute | solution.py:16
  105.2 10.6 %collective-permute-start.13 = (f32[1,64,4,128]{3,1,2,0:T(8,128)S(1)}, f32[1,64,4,128]{3,1,2,0:T(8,128)S(1)}, u32[]{:S(2)}, u32[]{:S(2)}) collective-permute-start(f32[1,64,4,128]{3,1,2,0:T(8,128)S(1)} %get-tuple-element.20), channel_id=1, source_target_pairs={{8,0},{16,8},{24,16},{9,1},{17,9},{25,17},{10,2},{18,10},{26,18},{... | collective-permute-start | bytes 393224 | tf_op jit(solution)/shard_map/ppermute | solution.py:19
  131.6 10.4 %collective-permute-start.19 = (f32[1,64,128]{2,1,0:T(8,128)S(1)}, f32[1,64,128]{2,1,0:T(8,128)S(1)}, u32[]{:S(2)}, u32[]{:S(2)}) collective-permute-start(f32[1,64,128]{2,1,0:T(8,128)S(1)} %fusion.19), channel_id=1, source_target_pairs={{1,0},{2,1},{3,2},{4,3},{5,4},{6,5},{7,6},{9,8},{10,9},{11,10},{12... | collective-permute-start | bytes 98312 | tf_op jit(solution)/shard_map/ppermute | solution.py:19
  146.7 10.4 %collective-permute-start.23 = (f32[1,64,128]{2,1,0:T(8,128)S(1)}, f32[1,64,128]{2,1,0:T(8,128)S(1)}, u32[]{:S(2)}, u32[]{:S(2)}) collective-permute-start(f32[1,64,128]{2,1,0:T(8,128)S(1)} %fusion.20), channel_id=1, source_target_pairs={{1,0},{2,1},{3,2},{4,3},{5,4},{6,5},{7,6},{9,8},{10,9},{11,10},{12... | collective-permute-start | bytes 98312 | tf_op jit(solution)/shard_map/ppermute | solution.py:19
  164.0 16.0 %collective-permute-start.27 = (f32[1,64,4,128]{3,1,2,0:T(8,128)S(1)}, f32[1,64,4,128]{3,1,2,0:T(8,128)S(1)}, u32[]{:S(2)}, u32[]{:S(2)}) collective-permute-start(f32[1,64,4,128]{3,1,2,0:T(8,128)S(1)} %get-tuple-element.14), channel_id=1, source_target_pairs={{1,0},{2,1},{3,2},{4,3},{5,4},{6,5},{7,6},{9,8},{10,9},{11,10},{12... | collective-permute-start | bytes 393224 | tf_op jit(solution)/shard_map/ppermute | solution.py:19
  165.3 14.0 %collective-permute-start.26 = (f32[1,64,4,128]{3,1,2,0:T(8,128)S(1)}, f32[1,64,4,128]{3,1,2,0:T(8,128)S(1)}, u32[]{:S(2)}, u32[]{:S(2)}) collective-permute-start(f32[1,64,4,128]{3,1,2,0:T(8,128)S(1)} %get-tuple-element.15), channel_id=1, source_target_pairs={{0,1},{1,2},{2,3},{3,4},{4,5},{5,6},{6,7},{8,9},{9,10},{10,11},{11... | collective-permute-start | bytes 393224 | tf_op jit(solution)/shard_map/ppermute | solution.py:16
  168.4 10.3 %collective-permute-start.25 = (f32[1,64,4,128]{3,1,2,0:T(8,128)S(1)}, f32[1,64,4,128]{3,1,2,0:T(8,128)S(1)}, u32[]{:S(2)}, u32[]{:S(2)}) collective-permute-start(f32[1,64,4,128]{3,1,2,0:T(8,128)S(1)} %get-tuple-element.16), channel_id=1, source_target_pairs={{8,0},{16,8},{24,16},{9,1},{17,9},{25,17},{10,2},{18,10},{26,18},{... | collective-permute-start | bytes 393224 | tf_op jit(solution)/shard_map/ppermute | solution.py:19
  194.6 12.2 %collective-permute-start.28 = (f32[1,64,4,128]{3,1,2,0:T(8,128)S(1)}, f32[1,64,4,128]{3,1,2,0:T(8,128)S(1)}, u32[]{:S(2)}, u32[]{:S(2)}) collective-permute-start(f32[1,64,4,128]{3,1,2,0:T(8,128)S(1)} %get-tuple-element.13), channel_id=1, source_target_pairs={{0,8},{8,16},{16,24},{1,9},{9,17},{17,25},{2,10},{10,18},{18,26},{... | collective-permute-start | bytes 393224 | tf_op jit(solution)/shard_map/ppermute | solution.py:16
  201.2 13.8 %collective-permute-start.31 = (f32[1,64,4,128]{3,1,2,0:T(8,128)S(1)}, f32[1,64,4,128]{3,1,2,0:T(8,128)S(1)}, u32[]{:S(2)}, u32[]{:S(2)}) collective-permute-start(f32[1,64,4,128]{3,1,2,0:T(8,128)S(1)} %get-tuple-element.10), channel_id=1, source_target_pairs={{1,0},{2,1},{3,2},{4,3},{5,4},{6,5},{7,6},{9,8},{10,9},{11,10},{12... | collective-permute-start | bytes 393224 | tf_op jit(solution)/shard_map/ppermute | solution.py:19
  202.4 11.9 %collective-permute-start.30 = (f32[1,64,4,128]{3,1,2,0:T(8,128)S(1)}, f32[1,64,4,128]{3,1,2,0:T(8,128)S(1)}, u32[]{:S(2)}, u32[]{:S(2)}) collective-permute-start(f32[1,64,4,128]{3,1,2,0:T(8,128)S(1)} %get-tuple-element.11), channel_id=1, source_target_pairs={{0,1},{1,2},{2,3},{3,4},{4,5},{5,6},{6,7},{8,9},{9,10},{10,11},{11... | collective-permute-start | bytes 393224 | tf_op jit(solution)/shard_map/ppermute | solution.py:16
  229.8 16.0 %collective-permute-start.35 = (f32[1,64,4,128]{3,1,2,0:T(8,128)S(1)}, f32[1,64,4,128]{3,1,2,0:T(8,128)S(1)}, u32[]{:S(2)}, u32[]{:S(2)}) collective-permute-start(f32[1,64,4,128]{3,1,2,0:T(8,128)S(1)} %get-tuple-element.6), channel_id=1, source_target_pairs={{1,0},{2,1},{3,2},{4,3},{5,4},{6,5},{7,6},{9,8},{10,9},{11,10},{12... | collective-permute-start | bytes 393224 | tf_op jit(solution)/shard_map/ppermute | solution.py:19
  231.1 14.0 %collective-permute-start.34 = (f32[1,64,4,128]{3,1,2,0:T(8,128)S(1)}, f32[1,64,4,128]{3,1,2,0:T(8,128)S(1)}, u32[]{:S(2)}, u32[]{:S(2)}) collective-permute-start(f32[1,64,4,128]{3,1,2,0:T(8,128)S(1)} %get-tuple-element.7), channel_id=1, source_target_pairs={{0,1},{1,2},{2,3},{3,4},{4,5},{5,6},{6,7},{8,9},{9,10},{10,11},{11... | collective-permute-start | bytes 393224 | tf_op jit(solution)/shard_map/ppermute | solution.py:16
  234.2 10.3 %collective-permute-start.33 = (f32[1,64,4,128]{3,1,2,0:T(8,128)S(1)}, f32[1,64,4,128]{3,1,2,0:T(8,128)S(1)}, u32[]{:S(2)}, u32[]{:S(2)}) collective-permute-start(f32[1,64,4,128]{3,1,2,0:T(8,128)S(1)} %get-tuple-element.8), channel_id=1, source_target_pairs={{8,0},{16,8},{24,16},{9,1},{17,9},{25,17},{10,2},{18,10},{26,18},{... | collective-permute-start | bytes 393224 | tf_op jit(solution)/shard_map/ppermute | solution.py:19
  (37 other events, 238.5 us)
where the time goes:
time: 259 us; the launch traced here: 256 us
  starting transfers between devices  92.1 us (36%)
  local copies, waits for them, and re-layouts  78.8 us (30%)
  other arithmetic  29.5 us (11%)
  waiting for transfers between devices  28.5 us (11%)
  matrix products  25.6 us (10%)
    ppermute x18, starting transfers between devices, extended_2(): lax.ppermute(lax.slice_in_dim(block, block.shape[dim] - width, None, axis...  68.8 us
    unnamed x82, local copies, waits for them, and re-layouts  28.1 us
    ppermute x18, starting transfers between devices, extended_2(): lax.ppermute(lax.slice_in_dim(block, 0, width, axis=dim), axis, backward)  23.2 us
    dot_general x7, matrix products, block_product(): jnp.einsum('rkij,vrkj->vri', fine_matrix.astype(jnp.float32), picked, pre...  22.9 us
    gather x7, local copies, waits for them, and re-layouts, fine_apply(): jnp.take(extended, flat_cols, axis=1)  22.7 us
    ppermute x18, waiting for transfers between devices, extended_2(): lax.ppermute(lax.slice_in_dim(block, 0, width, axis=dim), axis, backward)  21.5 us
    gather x7, local copies, waits for them, and re-layouts, receive(): jnp.take(blocks, lists, axis=1)  15.1 us
    select_n x8, other arithmetic, fine_apply(): jnp.take(extended, flat_cols, axis=1)  14 us
  transfers between devices with their start and end apart: 36, of which 8 were waited for; matrix products, arithmetic and copies ran while one was open for 12% of the time, Pallas kernels for 0%

commit v1 on v0

v1 whole, which is shorter than its diff:
```python
import functools

import jax
import jax.numpy as jnp
from jax import lax
from jax.experimental import pallas as pl
from jax.experimental.pallas import tpu as pltpu
from jax.sharding import PartitionSpec as P

center_value = 1.1
radius_value = 0.9
AXES = ("span", "stream")
CHUNK = 16
f32 = jnp.float32
bf16 = jnp.bfloat16


def chebyshev_weights():
    weights = []
    old = radius_value / center_value
    for _ in range(2):
        now = 1.0 / (2.0 * center_value / radius_value - old)
        weights.append((now * old, 2.0 * now / radius_value))
        old = now
    return weights


def even_partner(i, n):
    return i ^ 1 if (i ^ 1) < n else None


def odd_partner(i, n):
    j = ((i + 1) ^ 1) - 1
    return j if 0 <= j < n else None


def exchanges(n_span, n_stream):
    def flat(rule):
        return [
            (s * n_stream + t, rule(s, t)) for s in range(n_span) for t in range(n_stream)
        ]

    def along_span(rule):
        def pick(s, t):
            other = rule(s, n_span)
            if other is not None:
                return other * n_stream + t
            spare = even_partner(t, n_stream)
            return s * n_stream + (t if spare is None else spare)

        return pick

    def along_stream(rule):
        def pick(s, t):
            other = rule(t, n_stream)
            if other is not None:
                return s * n_stream + other
            spare = even_partner(s, n_span)
            return (s if spare is None else spare) * n_stream + t

        return pick

    return [
        flat(along_span(even_partner)),
        flat(along_span(odd_partner)),
        flat(along_stream(even_partner)),
        flat(along_stream(odd_partner)),
    ]


def dot_nt(a, b):
    return lax.dot_general(a, b, (((1,), (1,)), ((), ())), preferred_element_type=f32)


def dot_nn(a, b):
    return lax.dot_general(a, b, (((1,), (0,)), ((), ())), preferred_element_type=f32)


def high_low(x):
    high = x.astype(bf16)
    return high, (x - high.astype(f32)).astype(bf16)


def block(index, size):
    return pl.ds(pl.multiple_of(index * size, size), size)


def direction_of(meta, buffer):
    return buffer ^ meta[buffer // 2]


def pack(meta, lists, field, outs, size):
    slots = lists.shape[0] // 4
    rows = field.shape[0]
    for buffer in range(4):
        direction = direction_of(meta, buffer)
        for h in range(slots):
            source = lists[direction * slots + h]
            outs[buffer][0:rows, h * size : (h + 1) * size] = field[:, block(source, size)]


def pack_kernel(meta, lists, field, groups, *outs, size):
    slots = lists.shape[0] // 4
    rows = field.shape[0]
    pack(meta, lists, field, outs, size)
    for buffer in range(4):
        direction = direction_of(meta, buffer)
        for h in range(slots):
            source = lists[direction * slots + h]
            names = groups[:, block(source, size)].astype(f32)
            outs[buffer][rows : rows + 8, h * size : (h + 1) * size] = jnp.broadcast_to(
                names, (8, size)
            )


def split_field(field, wide, size):
    rows, width = field.shape
    high, low = high_low(field[...])
    wide[0:rows, 0:width] = high
    wide[rows : 2 * rows, 0:width] = low
    wide[:, width : width + size] = jnp.zeros((2 * rows, size), bf16)


def local_product(columns, matrix, wide, out, size):
    blocks, count = matrix.shape[0], matrix.shape[1]
    rows = out.shape[0]
    for g in range(blocks):
        parts = [wide[:, g * size : (g + 1) * size]]
        for k in range(1, count):
            column = jnp.minimum(columns[g * count + k], blocks)
            parts.append(wide[:, block(column, size)])
        product = dot_nt(
            jnp.concatenate(parts, axis=1),
            jnp.concatenate([matrix[g, k] for k in range(count)], axis=1),
        )
        out[:, g * size : (g + 1) * size] = product[:rows] + product[rows:]


def local_kernel(columns, field, matrix, out, wide, *, size):
    split_field(field, wide, size)
    local_product(columns, matrix, wide, out, size)


def prepare_kernel(
    meta, columns, field, matrix, groups, coarse, out, entries, inverse, onehot, coarse_high, coarse_low, coarse_inverse, wide, *, size, halo_slots
):
    blocks, count = matrix.shape[0], matrix.shape[1]
    limit = entries.shape[0] - 1

    def clear(i, carry):
        entries[i] = halo_slots
        return carry

    lax.fori_loop(0, limit, clear, 0)
    per = halo_slots // 4

    def scan(g, found):
        for k in range(1, count):
            column = columns[g * count + k]
            slot = jnp.maximum(column - blocks, 0)
            direction = lax.div(slot, per)
            flip = jnp.where(direction < 2, meta[0], meta[1])
            place = (direction ^ flip) * per + lax.rem(slot, per)
            use = jnp.where(column >= blocks, meta[2 + direction], 0)
            entries[found] = jnp.where(
                use > 0, (g * count + k) * (2 * halo_slots) + place, halo_slots
            )
            found = found + use
        return found

    total = lax.fori_loop(0, blocks, scan, 0)
    entries[limit] = total
    same = (
        lax.broadcasted_iota(jnp.int32, (size, size), 0)
        == lax.broadcasted_iota(jnp.int32, (size, size), 1)
    )
    for g in range(blocks):
        diagonal = jnp.sum(
            jnp.where(same, matrix[g, 0].astype(f32), 0.0), axis=0, keepdims=True
        )
        inverse[:, g * size : (g + 1) * size] = jnp.broadcast_to(1.0 / diagonal, (8, size))
    diagonal = jnp.sum(jnp.where(same, coarse[0], 0.0), axis=0, keepdims=True)
    coarse_inverse[...] = jnp.broadcast_to(1.0 / diagonal, (8, size))
    cells = lax.broadcasted_iota(jnp.int32, (size, groups.shape[1]), 0)
    onehot[...] = jnp.where(cells == groups[...], 1.0, 0.0).astype(bf16)
    for k in range(5):
        if k == 0:
            piece = coarse[0]
        else:
            direction = direction_of(meta, k - 1)
            piece = jnp.where(meta[2 + direction] > 0, coarse[1 + direction], 0.0)
        high, low = high_low(piece)
        coarse_high[:, k * size : (k + 1) * size] = high
        coarse_low[:, k * size : (k + 1) * size] = low
    split_field(field, wide, size)
    local_product(columns, matrix, wide, out, size)


def split_halos(halos, wide, size):
    rows = wide.shape[0] // 2
    width = halos[0].shape[1]
    for buffer in range(4):
        high, low = high_low(halos[buffer][0:rows, :])
        wide[0:rows, buffer * width : (buffer + 1) * width] = high
        wide[rows : 2 * rows, buffer * width : (buffer + 1) * width] = low
    wide[:, 4 * width : 4 * width + size] = jnp.zeros((2 * rows, size), bf16)


def subtract_halo(entries, matrix, wide, products, residual, size):
    blocks, count = matrix.shape[0], matrix.shape[1]
    rows = residual.shape[0]
    slots = wide.shape[1] // size - 1
    limit = entries.shape[0] - 1

    def chunk(c, carry):
        for i in range(CHUNK):
            code = entries[c * CHUNK + i]
            which, place = lax.div(code, 2 * slots), lax.rem(code, 2 * slots)
            product = dot_nt(
                wide[:, block(place, size)], matrix[lax.div(which, count), lax.rem(which, count)]
            )
            products[i] = product[:rows] + product[rows:]
        for i in range(CHUNK):
            row = lax.div(entries[c * CHUNK + i], 2 * slots * count)
            at = block(row, size)
            residual[:, at] = residual[:, at] - products[i]
        return carry

    lax.fori_loop(0, (entries[limit] + CHUNK - 1) // CHUNK, chunk, 0)


def halo_kernel(
    *refs, size, weights, first, mode
):
    refs = list(refs)
    meta, lists, entries = refs[:3]
    halos = refs[3:7]
    local, residual, update, iterate, inverse, matrix = refs[7:13]
    refs = refs[13:]
    rows = local.shape[0]
    if mode == "restrict":
        onehot, coarse_inverse, left_out, start_out, coarse_out, wide, products = refs
        residual_out = left_out
    elif mode == "last":
        iterate_out, residual_out, wide, products = refs
    else:
        residual_out, update_out, iterate_out = refs[:3]
        outs = refs[3:7]
        wide, products = refs[7:]
    split_halos(halos, wide, size)
    residual_out[...] = residual[...] - local[...]
    subtract_halo(entries, matrix, wide, products, residual_out, size)
    if mode == "restrict":
        high, low = high_low(residual_out[...])
        total = dot_nt(jnp.concatenate([high, low], axis=0), onehot[...])
        total = total[:rows] + total[rows:]
        coarse_out[...] = total
        start_out[...] = coarse_inverse[0:1, :] * total / center_value
        return
    if first:
        new = inverse[0:1, :] * residual_out[...] / center_value
    else:
        new = weights[0] * update[...] + weights[1] * inverse[0:1, :] * residual_out[...]
    iterate_out[...] = iterate[...] + new
    if mode == "send":
        update_out[...] = new
        pack(meta, lists, update_out, outs, size)


def coarse_product(c, halos, coarse_high, coarse_low):
    rows = c.shape[0]
    high, low = high_low(jnp.concatenate([c] + [h[...] for h in halos], axis=1))
    big = dot_nt(jnp.concatenate([high, low], axis=0), coarse_high[...])
    return big[:rows] + big[rows:] + dot_nt(high, coarse_low[...])


def coarse_kernel(
    h0, h1, h2, h3, residual, update, iterate, coarse_high, coarse_low, coarse_inverse, *outs, weights, last
):
    c = update[...]
    left = residual[...] - coarse_product(c, (h0, h1, h2, h3), coarse_high, coarse_low)
    new = weights[0] * c + weights[1] * coarse_inverse[0:1, :] * left
    if last:
        outs[0][...] = iterate[...] + new
    else:
        residual_out, update_out, iterate_out = outs
        residual_out[...] = left
        update_out[...] = new
        iterate_out[...] = iterate[...] + new


def spread_kernel(columns, correction, onehot, iterate, matrix, second, out, field, wide, *, size):
    rows = correction.shape[0]
    high, low = high_low(correction[...])
    spread = dot_nn(jnp.concatenate([high, low], axis=0), onehot[...])
    field[...] = spread[:rows] + spread[rows:]
    second[...] = iterate[...] + field[...]
    split_field(field, wide, size)
    local_product(columns, matrix, wide, out, size)


def names_kernel(n0, n1, n2, n3, out, *, size):
    width = n0.shape[1]
    for buffer, names in enumerate((n0, n1, n2, n3)):
        cells = lax.broadcasted_iota(jnp.int32, (size, width), 0).astype(f32)
        out[:, buffer * width : (buffer + 1) * width] = jnp.where(
            cells == names[0:1, :], 1.0, 0.0
        ).astype(bf16)


def second_kernel(
    meta, lists, entries, e0, e1, e2, e3, names, local, leftover, iterate, inverse, matrix, residual_out, update_out, iterate_out, o0, o1, o2, o3, wide, products, *, size
):
    rows = local.shape[0]
    width = names.shape[1] // 4
    for buffer, e in enumerate((e0, e1, e2, e3)):
        high, low = high_low(e[...])
        spread = dot_nn(
            jnp.concatenate([high, low], axis=0),
            names[:, buffer * width : (buffer + 1) * width],
        )
        high, low = high_low(spread[:rows] + spread[rows:])
        wide[0:rows, buffer * width : (buffer + 1) * width] = high
        wide[rows : 2 * rows, buffer * width : (buffer + 1) * width] = low
    wide[:, 4 * width : 4 * width + size] = jnp.zeros((2 * rows, size), bf16)
    residual_out[...] = leftover[...] - local[...]
    subtract_halo(entries, matrix, wide, products, residual_out, size)
    new = inverse[0:1, :] * residual_out[...] / center_value
    iterate_out[...] = iterate[...] + new
    update_out[...] = new
    pack(meta, lists, update_out, (o0, o1, o2, o3), size)


def local_program(
    right_side, start_guess, fine_matrix, fine_columns, send_lists, aggregates, coarse_matrix
):
    n_span, n_stream = lax.axis_size("span"), lax.axis_size("stream")
    rows, width = right_side.shape
    blocks, count, size, _ = fine_matrix.shape
    slots = send_lists.shape[1] // 4
    halo_width = slots * size
    perms = exchanges(n_span, n_stream)
    s, t = lax.axis_index("span"), lax.axis_index("stream")
    meta = jnp.stack(
        [
            1 - s % 2,
            1 - t % 2,
            (s > 0).astype(jnp.int32),
            (s < n_span - 1).astype(jnp.int32),
            (t > 0).astype(jnp.int32),
            (t < n_stream - 1).astype(jnp.int32),
        ]
    ).astype(jnp.int32)
    lists = send_lists.reshape(-1)
    columns = fine_columns.reshape(-1)
    groups = aggregates.reshape(1, width)
    coarse = coarse_matrix.reshape(coarse_matrix.shape[1:])
    weights = chebyshev_weights()

    vmem = pl.BlockSpec(memory_space=pltpu.VMEM)
    smem = pl.BlockSpec(memory_space=pltpu.SMEM)

    def call(kernel, ins, outs, scratch=(), scalars=0, scalar_outs=(), flops=0):
        return pl.pallas_call(
            kernel,
            out_shape=[jax.ShapeDtypeStruct(shape, kind) for shape, kind in outs],
            in_specs=[smem] * scalars + [vmem] * (len(ins) - scalars),
            out_specs=[smem if i in scalar_outs else vmem for i in range(len(outs))],
            scratch_shapes=list(scratch),
            compiler_params=pltpu.CompilerParams(vmem_limit_bytes=VMEM_LIMIT),
            cost_estimate=pl.CostEstimate(
                flops=flops, bytes_accessed=4 * 1024 * 1024, transcendentals=0
            ),
        )(*ins)

    def exchange(payloads):
        return [lax.ppermute(x, AXES, perm) for x, perm in zip(payloads, perms)]

    field = ((rows, width), f32)
    halo = ((rows, halo_width), f32)
    small = ((rows, size), f32)
    wide_local = pltpu.VMEM((2 * rows, width + size), bf16)
    wide_halo = pltpu.VMEM((2 * rows, 4 * halo_width + size), bf16)
    products = pltpu.VMEM((CHUNK, rows, size), f32)
    flops = 2 * 2 * rows * blocks * count * size * size

    def apply_local(update):
        return call(
            functools.partial(local_kernel, size=size),
            [columns, update, fine_matrix], [field], [wide_local], 1, flops=flops,
        )[0]

    def sweep(halos, local, residual, update, iterate, weight, first=False, mode="send", extra=()):
        outs = {
            "send": [field, field, field] + [halo] * 4,
            "last": [field, field],
            "restrict": [field, small, small],
        }[mode]
        return call(
            functools.partial(halo_kernel, size=size, weights=weight, first=first, mode=mode),
            [meta, lists, entries] + halos + [local, residual, update, iterate, inverse, fine_matrix] + list(extra),
            outs, [wide_halo, products], 3, flops=flops // 5,
        )

    payloads = call(
        functools.partial(pack_kernel, size=size),
        [meta, lists, start_guess, groups], [((rows + 8, halo_width), f32)] * 4, (), 2,
    )
    entry_count = -(-blocks * (count - 1) // CHUNK) * CHUNK
    halos = exchange(payloads)
    local, entries, inverse, onehot, coarse_high, coarse_low, coarse_inverse = call(
        functools.partial(prepare_kernel, size=size, halo_slots=4 * slots),
        [meta, columns, start_guess, fine_matrix, groups, coarse],
        [
            field,
            ((entry_count + 1,), jnp.int32),
            ((8, width), f32),
            ((size, width), bf16),
            ((size, 5 * size), bf16),
            ((size, 5 * size), bf16),
            ((8, size), f32),
        ],
        [wide_local], 2, (1,), flops=flops,
    )
    names = [h[rows : rows + 8] for h in halos]
    residual, update, iterate, *payloads = sweep(
        halos, local, right_side, start_guess, start_guess, (0.0, 0.0), first=True
    )
    for weight in weights:
        halos = exchange(payloads)
        local = apply_local(update)
        residual, update, iterate, *payloads = sweep(
            halos, local, residual, update, iterate, weight
        )
    halos = exchange(payloads)
    local = apply_local(update)
    names = call(
        functools.partial(names_kernel, size=size), names, [((size, 4 * halo_width), bf16)]
    )[0]
    leftover, c, coarse_left = sweep(
        halos, local, residual, update, iterate, (0.0, 0.0), mode="restrict",
        extra=(onehot, coarse_inverse),
    )
    correction = c
    for i, weight in enumerate(weights):
        halos = exchange([c] * 4)
        result = call(
            functools.partial(coarse_kernel, weights=weight, last=i == 1),
            halos + [coarse_left, c, correction, coarse_high, coarse_low, coarse_inverse],
            [small] if i == 1 else [small] * 3,
        )
        if i == 1:
            correction = result[0]
        else:
            coarse_left, c, correction = result
    halos = exchange([correction] * 4)
    iterate, local = call(
        functools.partial(spread_kernel, size=size),
        [columns, correction, onehot, iterate, fine_matrix], [field, field],
        [pltpu.VMEM((rows, width), f32), wide_local], 1, flops=flops,
    )
    residual, update, iterate, *payloads = call(
        functools.partial(second_kernel, size=size),
        [meta, lists, entries] + halos + [names, local, leftover, iterate, inverse, fine_matrix],
        [field, field, field] + [halo] * 4, [wide_halo, products], 3, flops=flops // 5,
    )
    halos = exchange(payloads)
    local = apply_local(update)
    residual, update, iterate, *payloads = sweep(
        halos, local, residual, update, iterate, weights[0]
    )
    halos = exchange(payloads)
    local = apply_local(update)
    result = sweep(halos, local, residual, update, iterate, weights[1], mode="last")
    return (result[0], correction)


VMEM_LIMIT = 16 * 1024 * 1024


def solution(mesh):
    placed = (
        P(None, AXES),
        P(None, AXES),
        P(AXES, None, None, None),
        P(AXES, None),
        P(AXES, None),
        P(AXES),
        P(AXES, None, None, None),
    )
    return jax.shard_map(
        local_program,
        mesh=mesh,
        in_specs=placed,
        out_specs=(P(None, AXES), P(None, AXES)),
        check_vma=False,
    )
```

time: 259 us -> 87.5 us (0.34)
  local copies, waits for them, and re-layouts: 78.8 us -> 8.55 us
  starting transfers between devices: 92.1 us -> 36.4 us
  other arithmetic: 29.5 us -> 0 us
  Pallas kernels: 0 us -> 26.7 us
  matrix products: 25.6 us -> 0 us
  waiting for transfers between devices: 28.5 us -> 14.4 us
    ppermute x36, starting transfers between devices: 92.1 us -> 36.4 us  [exchange(): return [lax.ppermute(x, AXES, perm) for x, perm in zip(payloads, perms)]]
    gather x16 -> x0, local copies, waits for them, and re-layouts: 41 us -> none  [the longest x7 22.7 us: fine_apply(): jnp.take(extended, flat_cols, axis=1)]
    pallas_call x0 -> x18, Pallas kernels: none -> 26.7 us  [call(): pl.pallas_call(kernel, out_shape=[jax.ShapeDtypeStruct(shape, kind) for s...]
    dot_general x11 -> x0, matrix products: 25.6 us -> none  [the longest x7 22.9 us: block_product(): jnp.einsum('rkij,vrkj->vri', fine_matrix.astype(jnp.float32), picked, pre...]
    select_n x16 -> x0, other arithmetic: 21.6 us -> none  [the longest x8 14 us: fine_apply(): jnp.take(extended, flat_cols, axis=1)]
    unnamed x82 -> x23, local copies, waits for them, and re-layouts: 28.1 us -> 8.37 us
    ppermute x36, waiting for transfers between devices: 28.5 us -> 14.4 us  [exchange(): return [lax.ppermute(x, AXES, perm) for x, perm in zip(payloads, perms)]]
    reshape x6 -> x1, local copies, waits for them, and re-layouts: 4.64 us -> 0.09 us  [local_program(): columns = fine_columns.reshape(-1)]
  transfers between devices with their start and end apart: 36 -> 36, of which waited for: 8 -> 12; matrix products, arithmetic and copies ran while one was open for 12% -> 1% of each run, Pallas kernels for 0% -> 16%
where the time goes in v1:
time: 87.5 us; the launch traced here: 87 us
  starting transfers between devices  36.4 us (42%)
  Pallas kernels  26.7 us (31%)
  waiting for transfers between devices  14.4 us (16%)
  local copies, waits for them, and re-layouts  8.55 us (10%)
  between operations  0.98 us (1%)
    ppermute x36, starting transfers between devices, exchange(): return [lax.ppermute(x, AXES, perm) for x, perm in zip(payloads, perms)]  36.4 us
    pallas_call x18, Pallas kernels, call(): pl.pallas_call(kernel, out_shape=[jax.ShapeDtypeStruct(shape, kind) for s...  26.7 us
    ppermute x36, waiting for transfers between devices, exchange(): return [lax.ppermute(x, AXES, perm) for x, perm in zip(payloads, perms)]  14.4 us
    unnamed x23, local copies, waits for them, and re-layouts  8.37 us
  transfers between devices with their start and end apart: 36, of which 12 were waited for; matrix products, arithmetic and copies ran while one was open for 1% of the time, Pallas kernels for 16%

profile of v1, /device:TPU:0, one launch (start us, length us, event | category | flops | bytes accessed | tf_op | source)
XLA Modules:
  0.0 87.0 jit_solution(16918252809034721968)
XLA Ops:
  3.8 3.1 %collective-permute-start = (f32[72,512]{1,0:T(8,128)S(1)}, f32[72,512]{1,0:T(8,128)S(1)}, u32[]{:S(2)}, u32[]{:S(2)}) collective-permute-start(f32[72,512]{1,0:T(8,128)S(1)} %get-tuple-element.58), channel_id=1, source_target_pairs={{0,8},{1,9},{2,10},{3,11},{4,12},{5,13},{6,14},{7,15},{8,0},{9,1},... | collective-permute-start | bytes 442376 | tf_op jit(solution)/shard_map/ppermute | solution.py:377
  7.4 2.6 %collective-permute-start.3 = (f32[72,512]{1,0:T(8,128)S(1)}, f32[72,512]{1,0:T(8,128)S(1)}, u32[]{:S(2)}, u32[]{:S(2)}) collective-permute-start(f32[72,512]{1,0:T(8,128)S(1)} %get-tuple-element.61), channel_id=1, source_target_pairs={{0,8},{1,2},{2,1},{3,4},{4,3},{5,6},{6,5},{7,15},{8,0},{9,10},{10,... | collective-permute-start | bytes 442376 | tf_op jit(solution)/shard_map/ppermute | solution.py:377
  10.9 1.7 %copy-done = bf16[16,5,128,128]{3,2,1,0:T(8,128)(2,1)S(1)} copy-done((bf16[16,5,128,128]{3,2,1,0:T(8,128)(2,1)S(1)}, bf16[16,5,128,128]{3,2,1,0:T(8,128)(2,1)}, u32[]{:S(2)}) %copy-start) | copy-done | bytes 2621464
  15.4 3.4 %shard_map.86 = (f32[64,2048]{1,0:T(8,128)S(1)}, s32[65]{0:T(128)S(1)}, f32[8,2048]{1,0:T(8,128)S(1)}, bf16[128,2048]{1,0:T(8,128)(2,1)S(1)}, bf16[128,640]{1,0:...) custom-call(s32[6]{0:T(128)S(1)} %stack.43.meta.refs_0_, s32[80]{0:T(128)S(1)} %reshape.17.columns, ...), custom_call_target="tpu_custom_call" | custom-call | flops 335544320 | bytes 4194304 | tf_op jit(solution)/shard_map/pallas_call | solution.py:364
  22.4 1.7 %shard_map.89.refs_7_ = f32[64,2048]{1,0:T(8,128)S(1)} custom-call(s32[80]{0:T(128)S(1)} %reshape.17.columns, f32[64,2048]{1,0:T(8,128)S(1)} %get-tuple-element.68.field.refs_9_, bf16[16,5,128,128]{3,2,1,0:T(8,128)(2,1)S(1)} %copy-done.1), custom_call_target="tpu_custom_call" | custom-call | flops 335544320 | bytes 4194304 | tf_op jit(solution)/shard_map/pallas_call | solution.py:364
  30.1 1.7 %collective-permute-start.11 = (f32[64,512]{1,0:T(8,128)S(1)}, f32[64,512]{1,0:T(8,128)S(1)}, u32[]{:S(2)}, u32[]{:S(2)}) collective-permute-start(f32[64,512]{1,0:T(8,128)S(1)} %get-tuple-element.74), channel_id=1, source_target_pairs={{0,8},{1,2},{2,1},{3,4},{4,3},{5,6},{6,5},{7,15},{8,0},{9,10},{10,... | collective-permute-start | bytes 393224 | tf_op jit(solution)/shard_map/ppermute | solution.py:377
  31.9 1.7 %shard_map.91.refs_7_ = f32[64,2048]{1,0:T(8,128)S(1)} custom-call(s32[80]{0:T(128)S(1)} %reshape.17.columns, f32[64,2048]{1,0:T(8,128)S(1)} %get-tuple-element.75.field.refs_9_, bf16[16,5,128,128]{3,2,1,0:T(8,128)(2,1)S(1)} %copy-done.1), custom_call_target="tpu_custom_call" | custom-call | flops 335544320 | bytes 4194304 | tf_op jit(solution)/shard_map/pallas_call | solution.py:364
  40.5 1.7 %shard_map.93.refs_7_ = f32[64,2048]{1,0:T(8,128)S(1)} custom-call(s32[80]{0:T(128)S(1)} %reshape.17.columns, f32[64,2048]{1,0:T(8,128)S(1)} %get-tuple-element.82.field.refs_9_, bf16[16,5,128,128]{3,2,1,0:T(8,128)(2,1)S(1)} %copy-done.1), custom_call_target="tpu_custom_call" | custom-call | flops 335544320 | bytes 4194304 | tf_op jit(solution)/shard_map/pallas_call | solution.py:364
  42.2 1.6 %collective-permute-done.15.refs_6_ = f32[64,512]{1,0:T(8,128)S(1)} collective-permute-done((f32[64,512]{1,0:T(8,128)S(1)}, f32[64,512]{1,0:T(8,128)S(1)}, u32[]{:S(2)}, u32[]{:S(2)}) %collective-permute-start.15) | collective-permute-done | bytes 131104 | tf_op jit(solution)/shard_map/ppermute | solution.py:377
  45.3 1.7 %collective-permute-start.19 = (f32[64,128]{1,0:T(8,128)S(1)}, f32[64,128]{1,0:T(8,128)S(1)}, u32[]{:S(2)}, u32[]{:S(2)}) collective-permute-start(f32[64,128]{1,0:T(8,128)S(1)} %get-tuple-element.87.update.iterate), channel_id=1, source_target_pairs={{0,8},{1,2},{2,1},{3,4},{4,3},{5,6},{6,5},{7,15},{8,0},{9,10},{10,... | collective-permute-start | bytes 98312 | tf_op jit(solution)/shard_map/ppermute | solution.py:377
  47.5 1.7 %collective-permute-start.16 = (f32[64,128]{1,0:T(8,128)S(1)}, f32[64,128]{1,0:T(8,128)S(1)}, u32[]{:S(2)}, u32[]{:S(2)}) collective-permute-start(f32[64,128]{1,0:T(8,128)S(1)} %get-tuple-element.87.update.iterate), channel_id=1, source_target_pairs={{0,8},{1,9},{2,10},{3,11},{4,12},{5,13},{6,14},{7,15},{8,0},{9,1},... | collective-permute-start | bytes 98312 | tf_op jit(solution)/shard_map/ppermute | solution.py:377
  49.3 2.1 %collective-permute-done.16.h0 = f32[64,128]{1,0:T(8,128)S(1)} collective-permute-done((f32[64,128]{1,0:T(8,128)S(1)}, f32[64,128]{1,0:T(8,128)S(1)}, u32[]{:S(2)}, u32[]{:S(2)}) %collective-permute-start.16) | collective-permute-done | bytes 32800 | tf_op jit(solution)/shard_map/ppermute | solution.py:377
  51.7 1.7 %collective-permute-start.23 = (f32[64,128]{1,0:T(8,128)S(1)}, f32[64,128]{1,0:T(8,128)S(1)}, u32[]{:S(2)}, u32[]{:S(2)}) collective-permute-start(f32[64,128]{1,0:T(8,128)S(1)} %get-tuple-element.91.update), channel_id=1, source_target_pairs={{0,8},{1,2},{2,1},{3,4},{4,3},{5,6},{6,5},{7,15},{8,0},{9,10},{10,... | collective-permute-start | bytes 98312 | tf_op jit(solution)/shard_map/ppermute | solution.py:377
  54.4 3.7 %collective-permute-start.20 = (f32[64,128]{1,0:T(8,128)S(1)}, f32[64,128]{1,0:T(8,128)S(1)}, u32[]{:S(2)}, u32[]{:S(2)}) collective-permute-start(f32[64,128]{1,0:T(8,128)S(1)} %get-tuple-element.91.update), channel_id=1, source_target_pairs={{0,8},{1,9},{2,10},{3,11},{4,12},{5,13},{6,14},{7,15},{8,0},{9,1},... | collective-permute-start | bytes 98312 | tf_op jit(solution)/shard_map/ppermute | solution.py:377
  58.1 1.9 %collective-permute-done.20.h0 = f32[64,128]{1,0:T(8,128)S(1)} collective-permute-done((f32[64,128]{1,0:T(8,128)S(1)}, f32[64,128]{1,0:T(8,128)S(1)}, u32[]{:S(2)}, u32[]{:S(2)}) %collective-permute-start.20) | collective-permute-done | bytes 32800 | tf_op jit(solution)/shard_map/ppermute | solution.py:377
  60.8 2.0 %collective-permute-start.27 = (f32[64,128]{1,0:T(8,128)}, f32[64,128]{1,0:T(8,128)S(1)}, u32[]{:S(2)}, u32[]{:S(2)}) collective-permute-start(f32[64,128]{1,0:T(8,128)} %shard_map.96.correction), channel_id=1, source_target_pairs={{0,8},{1,2},{2,1},{3,4},{4,3},{5,6},{6,5},{7,15},{8,0},{9,10},{10,... | collective-permute-start | bytes 98312 | tf_op jit(solution)/shard_map/ppermute | solution.py:377
  65.0 1.9 %shard_map.98 = (f32[64,2048]{1,0:T(8,128)S(1)}, f32[64,2048]{1,0:T(8,128)S(1)}) custom-call(s32[80]{0:T(128)S(1)} %reshape.17.columns, f32[64,128]{1,0:T(8,128)S(1)} %copy-done.6, bf16[128,2048]{1,0:T(8,128)(2,1)S(1)} %get-tuple-element.85.refs_13_.onehot, f32[64,2048]{1,0:T(8,128)S(1)} %get-tuple-element.84.refs_10_.iterate, ...), custom_call_target="tpu_custom_call" | custom-call | flops 335544320 | bytes 4194304 | tf_op jit(solution)/shard_map/pallas_call | solution.py:364
  67.5 1.8 %shard_map.99 = (f32[64,2048]{1,0:T(8,128)S(1)}, f32[64,2048]{1,0:T(8,128)S(1)}, f32[64,2048]{1,0:T(8,128)S(1)}, f32[64,512]{1,0:T(8,128)S(1)}, f32[64,512]{1,0:...) custom-call(s32[6]{0:T(128)S(1)} %stack.43.meta.refs_0_, s32[16]{0:T(128)S(1)} %bitcast.17, ...), custom_call_target="tpu_custom_call" | custom-call | flops 67108864 | bytes 4194304 | tf_op jit(solution)/shard_map/pallas_call | solution.py:364
  70.6 2.2 %collective-permute-start.31 = (f32[64,512]{1,0:T(8,128)S(1)}, f32[64,512]{1,0:T(8,128)S(1)}, u32[]{:S(2)}, u32[]{:S(2)}) collective-permute-start(f32[64,512]{1,0:T(8,128)S(1)} %get-tuple-element.100), channel_id=1, source_target_pairs={{0,8},{1,2},{2,1},{3,4},{4,3},{5,6},{6,5},{7,15},{8,0},{9,10},{10,... | collective-permute-start | bytes 393224 | tf_op jit(solution)/shard_map/ppermute | solution.py:377
  72.8 1.7 %shard_map.100.refs_7_ = f32[64,2048]{1,0:T(8,128)S(1)} custom-call(s32[80]{0:T(128)S(1)} %reshape.17.columns, f32[64,2048]{1,0:T(8,128)S(1)} %get-tuple-element.101.field.refs_9_, bf16[16,5,128,128]{3,2,1,0:T(8,128)(2,1)S(1)} %copy-done.1), custom_call_target="tpu_custom_call" | custom-call | flops 335544320 | bytes 4194304 | tf_op jit(solution)/shard_map/pallas_call | solution.py:364
  77.2 2.1 %collective-permute-start.32 = (f32[64,512]{1,0:T(8,128)S(1)}, f32[64,512]{1,0:T(8,128)S(1)}, u32[]{:S(2)}, u32[]{:S(2)}) collective-permute-start(f32[64,512]{1,0:T(8,128)S(1)} %get-tuple-element.104), channel_id=1, source_target_pairs={{0,8},{1,9},{2,10},{3,11},{4,12},{5,13},{6,14},{7,15},{8,0},{9,1},... | collective-permute-start | bytes 393224 | tf_op jit(solution)/shard_map/ppermute | solution.py:377
  81.1 1.7 %shard_map.102.refs_7_ = f32[64,2048]{1,0:T(8,128)S(1)} custom-call(s32[80]{0:T(128)S(1)} %reshape.17.columns, f32[64,2048]{1,0:T(8,128)S(1)} %get-tuple-element.108.field.refs_9_, bf16[16,5,128,128]{3,2,1,0:T(8,128)(2,1)S(1)} %copy-done.1), custom_call_target="tpu_custom_call" | custom-call | flops 335544320 | bytes 4194304 | tf_op jit(solution)/shard_map/pallas_call | solution.py:364
  83.0 1.7 %collective-permute-done.35.refs_6_ = f32[64,512]{1,0:T(8,128)S(1)} collective-permute-done((f32[64,512]{1,0:T(8,128)S(1)}, f32[64,512]{1,0:T(8,128)S(1)}, u32[]{:S(2)}, u32[]{:S(2)}) %collective-permute-start.35) | collective-permute-done | bytes 131104 | tf_op jit(solution)/shard_map/ppermute | solution.py:377
  84.7 2.3 %shard_map.103 = (f32[64,2048]{1,0:T(8,128)}, f32[64,2048]{1,0:T(8,128)}) custom-call(s32[6]{0:T(128)S(1)} %stack.43.meta.refs_0_, s32[16]{0:T(128)S(1)} %bitcast.19, s32[65]{0:T(128)S(1)} %get-tuple-element.57.refs_2_.entries, f32[64,512]{1,0:T(8,128)S(1)} %collective-permute-done.32.refs_3_, f32[64,512]{1,0:T(8,128)S(1)} %collective-permute-done.33.refs_4_, ...), custom_call_target="tpu_custom_call" | custom-call | flops 67108864 | bytes 4194304 | tf_op jit(solution)/shard_map/pallas_call | solution.py:364
  (95 shorter events, 36.7 us)
Async XLA Ops:
  3.8 15.0 %collective-permute-start = (f32[72,512]{1,0:T(8,128)S(1)}, f32[72,512]{1,0:T(8,128)S(1)}, u32[]{:S(2)}, u32[]{:S(2)}) collective-permute-start(f32[72,512]{1,0:T(8,128)S(1)} %get-tuple-element.58), channel_id=1, source_target_pairs={{0,8},{1,9},{2,10},{3,11},{4,12},{5,13},{6,14},{7,15},{8,0},{9,1},... | collective-permute-start | bytes 442376 | tf_op jit(solution)/shard_map/ppermute | solution.py:377
  6.9 11.9 %collective-permute-start.1 = (f32[72,512]{1,0:T(8,128)S(1)}, f32[72,512]{1,0:T(8,128)S(1)}, u32[]{:S(2)}, u32[]{:S(2)}) collective-permute-start(f32[72,512]{1,0:T(8,128)S(1)} %get-tuple-element.59), channel_id=1, source_target_pairs={{0,1},{1,0},{2,3},{3,2},{4,5},{5,4},{6,7},{7,6},{8,16},{9,17},{10,... | collective-permute-start | bytes 442376 | tf_op jit(solution)/shard_map/ppermute | solution.py:377
  6.9 11.9 %collective-permute-start.2 = (f32[72,512]{1,0:T(8,128)S(1)}, f32[72,512]{1,0:T(8,128)S(1)}, u32[]{:S(2)}, u32[]{:S(2)}) collective-permute-start(f32[72,512]{1,0:T(8,128)S(1)} %get-tuple-element.60), channel_id=1, source_target_pairs={{0,1},{1,0},{2,3},{3,2},{4,5},{5,4},{6,7},{7,6},{8,9},{9,8},{10,11... | collective-permute-start | bytes 442376 | tf_op jit(solution)/shard_map/ppermute | solution.py:377
  7.4 11.4 %collective-permute-start.3 = (f32[72,512]{1,0:T(8,128)S(1)}, f32[72,512]{1,0:T(8,128)S(1)}, u32[]{:S(2)}, u32[]{:S(2)}) collective-permute-start(f32[72,512]{1,0:T(8,128)S(1)} %get-tuple-element.61), channel_id=1, source_target_pairs={{0,8},{1,2},{2,1},{3,4},{4,3},{5,6},{6,5},{7,15},{8,0},{9,10},{10,... | collective-permute-start | bytes 442376 | tf_op jit(solution)/shard_map/ppermute | solution.py:377
  20.3 5.3 %collective-permute-start.4 = (f32[64,512]{1,0:T(8,128)S(1)}, f32[64,512]{1,0:T(8,128)S(1)}, u32[]{:S(2)}, u32[]{:S(2)}) collective-permute-start(f32[64,512]{1,0:T(8,128)S(1)} %get-tuple-element.64), channel_id=1, source_target_pairs={{0,8},{1,9},{2,10},{3,11},{4,12},{5,13},{6,14},{7,15},{8,0},{9,1},... | collective-permute-start | bytes 393224 | tf_op jit(solution)/shard_map/ppermute | solution.py:377
  20.3 5.2 %collective-permute-start.5 = (f32[64,512]{1,0:T(8,128)S(1)}, f32[64,512]{1,0:T(8,128)S(1)}, u32[]{:S(2)}, u32[]{:S(2)}) collective-permute-start(f32[64,512]{1,0:T(8,128)S(1)} %get-tuple-element.65), channel_id=1, source_target_pairs={{0,1},{1,0},{2,3},{3,2},{4,5},{5,4},{6,7},{7,6},{8,16},{9,17},{10,... | collective-permute-start | bytes 393224 | tf_op jit(solution)/shard_map/ppermute | solution.py:377
  21.6 5.3 %collective-permute-start.7 = (f32[64,512]{1,0:T(8,128)S(1)}, f32[64,512]{1,0:T(8,128)S(1)}, u32[]{:S(2)}, u32[]{:S(2)}) collective-permute-start(f32[64,512]{1,0:T(8,128)S(1)} %get-tuple-element.67), channel_id=1, source_target_pairs={{0,8},{1,2},{2,1},{3,4},{4,3},{5,6},{6,5},{7,15},{8,0},{9,10},{10,... | collective-permute-start | bytes 393224 | tf_op jit(solution)/shard_map/ppermute | solution.py:377
  28.4 5.6 %collective-permute-start.8 = (f32[64,512]{1,0:T(8,128)S(1)}, f32[64,512]{1,0:T(8,128)S(1)}, u32[]{:S(2)}, u32[]{:S(2)}) collective-permute-start(f32[64,512]{1,0:T(8,128)S(1)} %get-tuple-element.71), channel_id=1, source_target_pairs={{0,8},{1,9},{2,10},{3,11},{4,12},{5,13},{6,14},{7,15},{8,0},{9,1},... | collective-permute-start | bytes 393224 | tf_op jit(solution)/shard_map/ppermute | solution.py:377
  29.6 4.4 %collective-permute-start.9 = (f32[64,512]{1,0:T(8,128)S(1)}, f32[64,512]{1,0:T(8,128)S(1)}, u32[]{:S(2)}, u32[]{:S(2)}) collective-permute-start(f32[64,512]{1,0:T(8,128)S(1)} %get-tuple-element.72), channel_id=1, source_target_pairs={{0,1},{1,0},{2,3},{3,2},{4,5},{5,4},{6,7},{7,6},{8,16},{9,17},{10,... | collective-permute-start | bytes 393224 | tf_op jit(solution)/shard_map/ppermute | solution.py:377
  29.6 4.4 %collective-permute-start.10 = (f32[64,512]{1,0:T(8,128)S(1)}, f32[64,512]{1,0:T(8,128)S(1)}, u32[]{:S(2)}, u32[]{:S(2)}) collective-permute-start(f32[64,512]{1,0:T(8,128)S(1)} %get-tuple-element.73), channel_id=1, source_target_pairs={{0,1},{1,0},{2,3},{3,2},{4,5},{5,4},{6,7},{7,6},{8,9},{9,8},{10,11... | collective-permute-start | bytes 393224 | tf_op jit(solution)/shard_map/ppermute | solution.py:377
  30.1 5.3 %collective-permute-start.11 = (f32[64,512]{1,0:T(8,128)S(1)}, f32[64,512]{1,0:T(8,128)S(1)}, u32[]{:S(2)}, u32[]{:S(2)}) collective-permute-start(f32[64,512]{1,0:T(8,128)S(1)} %get-tuple-element.74), channel_id=1, source_target_pairs={{0,8},{1,2},{2,1},{3,4},{4,3},{5,6},{6,5},{7,15},{8,0},{9,10},{10,... | collective-permute-start | bytes 393224 | tf_op jit(solution)/shard_map/ppermute | solution.py:377
  36.8 5.3 %collective-permute-start.12 = (f32[64,512]{1,0:T(8,128)S(1)}, f32[64,512]{1,0:T(8,128)S(1)}, u32[]{:S(2)}, u32[]{:S(2)}) collective-permute-start(f32[64,512]{1,0:T(8,128)S(1)} %get-tuple-element.78), channel_id=1, source_target_pairs={{0,8},{1,9},{2,10},{3,11},{4,12},{5,13},{6,14},{7,15},{8,0},{9,1},... | collective-permute-start | bytes 393224 | tf_op jit(solution)/shard_map/ppermute | solution.py:377
  38.8 5.0 %collective-permute-start.15 = (f32[64,512]{1,0:T(8,128)S(1)}, f32[64,512]{1,0:T(8,128)S(1)}, u32[]{:S(2)}, u32[]{:S(2)}) collective-permute-start(f32[64,512]{1,0:T(8,128)S(1)} %get-tuple-element.81), channel_id=1, source_target_pairs={{0,8},{1,2},{2,1},{3,4},{4,3},{5,6},{6,5},{7,15},{8,0},{9,10},{10,... | collective-permute-start | bytes 393224 | tf_op jit(solution)/shard_map/ppermute | solution.py:377
  51.7 6.4 %collective-permute-start.23 = (f32[64,128]{1,0:T(8,128)S(1)}, f32[64,128]{1,0:T(8,128)S(1)}, u32[]{:S(2)}, u32[]{:S(2)}) collective-permute-start(f32[64,128]{1,0:T(8,128)S(1)} %get-tuple-element.91.update), channel_id=1, source_target_pairs={{0,8},{1,2},{2,1},{3,4},{4,3},{5,6},{6,5},{7,15},{8,0},{9,10},{10,... | collective-permute-start | bytes 98312 | tf_op jit(solution)/shard_map/ppermute | solution.py:377
  53.4 4.7 %collective-permute-start.22 = (f32[64,128]{1,0:T(8,128)S(1)}, f32[64,128]{1,0:T(8,128)S(1)}, u32[]{:S(2)}, u32[]{:S(2)}) collective-permute-start(f32[64,128]{1,0:T(8,128)S(1)} %get-tuple-element.91.update), channel_id=1, source_target_pairs={{0,1},{1,0},{2,3},{3,2},{4,5},{5,4},{6,7},{7,6},{8,9},{9,8},{10,11... | collective-permute-start | bytes 98312 | tf_op jit(solution)/shard_map/ppermute | solution.py:377
  54.4 5.6 %collective-permute-start.20 = (f32[64,128]{1,0:T(8,128)S(1)}, f32[64,128]{1,0:T(8,128)S(1)}, u32[]{:S(2)}, u32[]{:S(2)}) collective-permute-start(f32[64,128]{1,0:T(8,128)S(1)} %get-tuple-element.91.update), channel_id=1, source_target_pairs={{0,8},{1,9},{2,10},{3,11},{4,12},{5,13},{6,14},{7,15},{8,0},{9,1},... | collective-permute-start | bytes 98312 | tf_op jit(solution)/shard_map/ppermute | solution.py:377
  60.8 6.0 %collective-permute-start.27 = (f32[64,128]{1,0:T(8,128)}, f32[64,128]{1,0:T(8,128)S(1)}, u32[]{:S(2)}, u32[]{:S(2)}) collective-permute-start(f32[64,128]{1,0:T(8,128)} %shard_map.96.correction), channel_id=1, source_target_pairs={{0,8},{1,2},{2,1},{3,4},{4,3},{5,6},{6,5},{7,15},{8,0},{9,10},{10,... | collective-permute-start | bytes 98312 | tf_op jit(solution)/shard_map/ppermute | solution.py:377
  63.4 4.1 %collective-permute-start.24 = (f32[64,128]{1,0:T(8,128)}, f32[64,128]{1,0:T(8,128)S(1)}, u32[]{:S(2)}, u32[]{:S(2)}) collective-permute-start(f32[64,128]{1,0:T(8,128)} %shard_map.96.correction), channel_id=1, source_target_pairs={{0,8},{1,9},{2,10},{3,11},{4,12},{5,13},{6,14},{7,15},{8,0},{9,1},... | collective-permute-start | bytes 98312 | tf_op jit(solution)/shard_map/ppermute | solution.py:377
  69.3 5.2 %collective-permute-start.28 = (f32[64,512]{1,0:T(8,128)S(1)}, f32[64,512]{1,0:T(8,128)S(1)}, u32[]{:S(2)}, u32[]{:S(2)}) collective-permute-start(f32[64,512]{1,0:T(8,128)S(1)} %get-tuple-element.97), channel_id=1, source_target_pairs={{0,8},{1,9},{2,10},{3,11},{4,12},{5,13},{6,14},{7,15},{8,0},{9,1},... | collective-permute-start | bytes 393224 | tf_op jit(solution)/shard_map/ppermute | solution.py:377
  70.1 4.4 %collective-permute-start.29 = (f32[64,512]{1,0:T(8,128)S(1)}, f32[64,512]{1,0:T(8,128)S(1)}, u32[]{:S(2)}, u32[]{:S(2)}) collective-permute-start(f32[64,512]{1,0:T(8,128)S(1)} %get-tuple-element.98), channel_id=1, source_target_pairs={{0,1},{1,0},{2,3},{3,2},{4,5},{5,4},{6,7},{7,6},{8,16},{9,17},{10,... | collective-permute-start | bytes 393224 | tf_op jit(solution)/shard_map/ppermute | solution.py:377
  70.1 4.4 %collective-permute-start.30 = (f32[64,512]{1,0:T(8,128)S(1)}, f32[64,512]{1,0:T(8,128)S(1)}, u32[]{:S(2)}, u32[]{:S(2)}) collective-permute-start(f32[64,512]{1,0:T(8,128)S(1)} %get-tuple-element.99), channel_id=1, source_target_pairs={{0,1},{1,0},{2,3},{3,2},{4,5},{5,4},{6,7},{7,6},{8,9},{9,8},{10,11... | collective-permute-start | bytes 393224 | tf_op jit(solution)/shard_map/ppermute | solution.py:377
  70.6 5.1 %collective-permute-start.31 = (f32[64,512]{1,0:T(8,128)S(1)}, f32[64,512]{1,0:T(8,128)S(1)}, u32[]{:S(2)}, u32[]{:S(2)}) collective-permute-start(f32[64,512]{1,0:T(8,128)S(1)} %get-tuple-element.100), channel_id=1, source_target_pairs={{0,8},{1,2},{2,1},{3,4},{4,3},{5,6},{6,5},{7,15},{8,0},{9,10},{10,... | collective-permute-start | bytes 393224 | tf_op jit(solution)/shard_map/ppermute | solution.py:377
  77.2 5.9 %collective-permute-start.32 = (f32[64,512]{1,0:T(8,128)S(1)}, f32[64,512]{1,0:T(8,128)S(1)}, u32[]{:S(2)}, u32[]{:S(2)}) collective-permute-start(f32[64,512]{1,0:T(8,128)S(1)} %get-tuple-element.104), channel_id=1, source_target_pairs={{0,8},{1,9},{2,10},{3,11},{4,12},{5,13},{6,14},{7,15},{8,0},{9,1},... | collective-permute-start | bytes 393224 | tf_op jit(solution)/shard_map/ppermute | solution.py:377
  79.8 5.0 %collective-permute-start.35 = (f32[64,512]{1,0:T(8,128)S(1)}, f32[64,512]{1,0:T(8,128)S(1)}, u32[]{:S(2)}, u32[]{:S(2)}) collective-permute-start(f32[64,512]{1,0:T(8,128)S(1)} %get-tuple-element.107), channel_id=1, source_target_pairs={{0,8},{1,2},{2,1},{3,4},{4,3},{5,6},{6,5},{7,15},{8,0},{9,10},{10,... | collective-permute-start | bytes 393224 | tf_op jit(solution)/shard_map/ppermute | solution.py:377
  (23 other events, 88.3 us)

commit v2 on v0

v2 whole, which is shorter than its diff:
```python
import functools

import jax
import jax.numpy as jnp
from jax import lax
from jax.experimental import pallas as pl
from jax.experimental.pallas import tpu as pltpu
from jax.sharding import PartitionSpec as P

center_value = 1.1
radius_value = 0.9
AXES = ("span", "stream")
ORDER = (2, 0, 1, 3)
EARLY = (0, 1, 2)
LAST = 3
CHUNK = 4
VMEM_LIMIT = 16 * 1024 * 1024
f32 = jnp.float32
bf16 = jnp.bfloat16
i32 = jnp.int32


def chebyshev_weights():
    weights = []
    old = radius_value / center_value
    for _ in range(2):
        now = 1.0 / (2.0 * center_value / radius_value - old)
        weights.append((now * old, 2.0 * now / radius_value))
        old = now
    return weights


def even_partner(i, n):
    return i ^ 1 if (i ^ 1) < n else None


def odd_partner(i, n):
    j = ((i + 1) ^ 1) - 1
    return j if 0 <= j < n else None


def exchanges(n_span, n_stream):
    def flat(rule):
        return [(s * n_stream + t, rule(s, t)) for s in range(n_span) for t in range(n_stream)]

    def along_span(rule):
        def pick(s, t):
            other = rule(s, n_span)
            if other is not None:
                return other * n_stream + t
            spare = even_partner(t, n_stream)
            return s * n_stream + (t if spare is None else spare)

        return pick

    def along_stream(rule):
        def pick(s, t):
            other = rule(t, n_stream)
            if other is not None:
                return s * n_stream + other
            spare = even_partner(s, n_span)
            return (s if spare is None else spare) * n_stream + t

        return pick

    return [
        flat(along_span(even_partner)),
        flat(along_span(odd_partner)),
        flat(along_stream(even_partner)),
        flat(along_stream(odd_partner)),
    ]


def place_in_mesh():
    s, t = lax.axis_index("span"), lax.axis_index("stream")
    n_span, n_stream = lax.axis_size("span"), lax.axis_size("stream")
    flips = (1 - (s & 1), 1 - (t & 1))
    valid = tuple(
        jnp.where(there, 1, 0).astype(i32)
        for there in (s > 0, s < n_span - 1, t > 0, t < n_stream - 1)
    )
    return flips, valid


def dot_nt(a, b):
    return lax.dot_general(a, b, (((1,), (1,)), ((), ())), preferred_element_type=f32)


def dot_nn(a, b):
    return lax.dot_general(a, b, (((1,), (0,)), ((), ())), preferred_element_type=f32)


def high_low(x):
    high = x.astype(bf16)
    return high, (x - high.astype(f32)).astype(bf16)


def stacked(x):
    return jnp.concatenate(high_low(x), axis=0)


def halves(x):
    rows = x.shape[0] // 2
    return x[:rows] + x[rows:]


def block(index, size):
    return pl.ds(pl.multiple_of(index * size, size), size)


class Table:
    def __init__(self, blocks, count, slots):
        self.blocks, self.count, self.slots = blocks, count, slots
        self.capacity = blocks * (count - 1) + CHUNK
        self.columns = 4 * slots
        self.home = self.columns + blocks * count
        self.counts = self.home + 5
        self.entries = self.counts + 5
        self.length = self.entries + 5 * self.capacity

    def direction(self, slot):
        if self.slots & (self.slots - 1) == 0:
            return slot >> (self.slots.bit_length() - 1)
        return lax.div(slot, self.slots)

    def code(self, which, row, slot):
        return (which << 16) | (row << 8) | slot


def pack(table, field, outs, size, slots):
    for buffer in range(4):
        for h in range(slots):
            source = table[buffer * slots + h]
            outs[buffer][:, h * size : (h + 1) * size] = field[:, block(source, size)]


def load_kernel(
    guess, lists, columns, groups, o0, o1, o2, o3, field, lists_out, columns_out, names, sems, *, size, slots
):
    copies = [
        pltpu.make_async_copy(source, target, sems.at[i])
        for i, (source, target) in enumerate(
            ((lists, lists_out), (guess, field), (groups, names), (columns, columns_out))
        )
    ]
    for copy in copies:
        copy.start()
    flips, _ = place_in_mesh()
    for copy in copies:
        copy.wait()
    rows = field.shape[0]
    for buffer, out in enumerate((o0, o1, o2, o3)):
        direction = buffer ^ flips[buffer // 2]
        for h in range(slots):
            at = block(lists_out[0, direction * slots + h], size)
            out[0:rows, h * size : (h + 1) * size] = field[:, at]
            out[rows : rows + 8, h * size : (h + 1) * size] = jnp.broadcast_to(
                names[:, at].astype(f32), (8, size)
            )


def split_field(field, wide, size):
    rows, width = field.shape
    high, low = high_low(field[...])
    wide[0:rows, 0:width] = high
    wide[rows : 2 * rows, 0:width] = low
    wide[:, width : width + size] = jnp.zeros((2 * rows, size), bf16)


def local_block(table, lay, matrix, wide, g, size):
    parts = [wide[:, g * size : (g + 1) * size]]
    for k in range(1, lay.count):
        parts.append(wide[:, block(table[lay.columns + g * lay.count + k], size)])
    pieces = [matrix[g * lay.count + k] for k in range(lay.count)]
    return halves(dot_nt(jnp.concatenate(parts, axis=1), jnp.concatenate(pieces, axis=1)))


def diagonal_row(matrix, same):
    return jnp.sum(jnp.where(same, matrix.astype(f32), 0.0), axis=0, keepdims=True)


def square_mask(size):
    return lax.broadcasted_iota(i32, (size, size), 0) == lax.broadcasted_iota(
        i32, (size, size), 1
    )


def build_table(lists, columns, table, lay):
    flips, valid = place_in_mesh()
    for direction in range(4):
        buffer = direction ^ flips[direction // 2]
        table[lay.home + direction] = jnp.where(valid[direction] > 0, buffer, 4)
        for h in range(lay.slots):
            table[buffer * lay.slots + h] = lists[0, direction * lay.slots + h]
    table[lay.home + 4] = 4
    for buffer in range(5):
        table[lay.counts + buffer] = 0
    for g in range(lay.blocks):
        table[lay.columns + g * lay.count] = columns[0, g]
        for k in range(1, lay.count):
            column = columns[k, g]
            table[lay.columns + g * lay.count + k] = jnp.minimum(column, lay.blocks)
            slot = jnp.maximum(column - lay.blocks, 0)
            direction = jnp.where(column < lay.blocks, 4, lay.direction(slot))
            buffer = table[lay.home + direction]
            found = table[lay.counts + buffer]
            table[lay.entries + buffer * lay.capacity + found] = lay.code(
                g * lay.count + k, g, slot - lay.direction(slot) * lay.slots
            )
            table[lay.counts + buffer] = found + 1
    for buffer in range(4):
        found = table[lay.counts + buffer]
        for i in range(CHUNK):
            table[lay.entries + buffer * lay.capacity + found + i] = lay.slots


def first_kernel(
    lists, columns, field, target, source, out, table, inverse, matrix, wide, right, sems, *, size, lay, parts
):
    per = matrix.shape[0] // parts
    copies = [
        pltpu.make_async_copy(
            source.at[pl.ds(i * per, per)], matrix.at[pl.ds(i * per, per)], sems.at[i]
        )
        for i in range(parts)
    ]
    copies.append(pltpu.make_async_copy(target, right, sems.at[parts]))
    for copy in copies:
        copy.start()
    split_field(field, wide, size)
    build_table(lists, columns, table, lay)
    copies[parts].wait()
    same = square_mask(size)
    for g in range(lay.blocks):
        if g % (lay.blocks // parts) == 0:
            copies[g // (lay.blocks // parts)].wait()
        at = slice(g * size, (g + 1) * size)
        out[:, at] = right[:, at] - local_block(table, lay, matrix, wide, g, size)
        inverse[:, at] = jnp.broadcast_to(
            1.0 / diagonal_row(matrix[g * lay.count], same), (8, size)
        )


def local_kernel(table, update, residual, iterate, matrix, out, iterate_out, wide, *, size, lay):
    split_field(update, wide, size)
    for g in range(lay.blocks):
        at = slice(g * size, (g + 1) * size)
        out[:, at] = residual[:, at] - local_block(table, lay, matrix, wide, g, size)
    iterate_out[...] = iterate[...] + update[...]


def local_and_coarse_kernel(
    table, update, residual, iterate, matrix, groups, coarse, h0, h1, h2, h3,
    out, iterate_out, onehot, names, coarse_high, coarse_low, coarse_inverse, wide, brought, cells, sems, *, size, lay,
):
    copies = [
        pltpu.make_async_copy(coarse, brought, sems.at[0]),
        pltpu.make_async_copy(groups, cells, sems.at[1]),
    ]
    for copy in copies:
        copy.start()
    local_kernel(
        table, update, residual, iterate, matrix, out, iterate_out, wide, size=size, lay=lay
    )
    width = lay.slots * size
    rows = update.shape[0]
    number = lax.broadcasted_iota(i32, (size, width), 0).astype(f32)
    for buffer, received in enumerate((h0, h1, h2, h3)):
        names[:, buffer * width : (buffer + 1) * width] = jnp.where(
            number == received[rows : rows + 1, :], 1.0, 0.0
        ).astype(bf16)
    for copy in copies:
        copy.wait()
    onehot[...] = jnp.where(
        lax.broadcasted_iota(i32, onehot.shape, 0) == cells[...], 1.0, 0.0
    ).astype(bf16)
    coarse_inverse[...] = jnp.broadcast_to(
        1.0 / diagonal_row(brought[0], square_mask(size)), (8, size)
    )
    flips, valid = place_in_mesh()
    for k in range(5):
        if k == 0:
            piece = brought[0]
        else:
            direction = (k - 1) ^ flips[(k - 1) // 2]
            there = jnp.where(
                direction < 2,
                jnp.where(direction == 0, valid[0], valid[1]),
                jnp.where(direction == 2, valid[2], valid[3]),
            )
            piece = jnp.where(there > 0, brought[1 + direction], 0.0)
        high, low = high_low(piece)
        coarse_high[:, k * size : (k + 1) * size] = high
        coarse_low[:, k * size : (k + 1) * size] = low


def put_halo(wide, place, x, size):
    rows, width = x.shape
    start = place * (width + size)
    high, low = high_low(x)
    wide[0:rows, start : start + width] = high
    wide[rows : 2 * rows, start : start + width] = low
    wide[:, start + width : start + width + size] = jnp.zeros((2 * rows, size), bf16)


def entry_product(code, matrix, wide, place, lay, size):
    which, row, slot = code >> 16, (code >> 8) & 255, code & 255
    at = block(place * (lay.slots + 1) + slot, size)
    return block(row, size), halves(dot_nt(wide[:, at], matrix[which]))


def for_received(table, lay, buffers, matrix, wide, size, use):
    def group(members):
        use(
            [
                entry_product(
                    table[lay.entries + buffer * lay.capacity + i], matrix, wide, place, lay, size
                )
                for place, buffer, i in members
            ]
        )

    group([(p, b, i) for p, b in enumerate(buffers) for i in range(CHUNK)])
    for place, buffer in enumerate(buffers):

        def more(c, carry, place=place, buffer=buffer):
            group([(place, buffer, c * CHUNK + i) for i in range(CHUNK)])
            return carry

        chunks = (table[lay.counts + buffer] + CHUNK - 1) // CHUNK
        lax.fori_loop(1, chunks, more, 0)


def sweep_weights(weights, inverse):
    if weights is None:
        return None, inverse[0:1, :] / center_value
    return weights[0], weights[1] * inverse[0:1, :]


def early_kernel(table, h0, h1, h2, residual, update, inverse, matrix, *refs, size, lay, weights, mode):
    refs = list(refs)
    rows = residual.shape[0]
    onehot = refs.pop(0) if mode == "restrict" else None
    names = refs.pop(0) if mode == "spread" else None
    iterate = refs.pop(0) if mode == "last" else None
    left, new, wide = refs
    for place, received in enumerate((h0, h1, h2)):
        if mode == "spread":
            width = lay.slots * size
            buffer = EARLY[place]
            chosen = names[:, buffer * width : (buffer + 1) * width]
            put_halo(wide, place, halves(dot_nn(stacked(received[...]), chosen)), size)
        else:
            put_halo(wide, place, received[0:rows, :], size)
    left[...] = residual[...]

    def use(found):
        for at, product in found:
            left[:, at] = left[:, at] - product

    for_received(table, lay, EARLY, matrix, wide, size, use)
    if mode == "restrict":
        new[...] = halves(dot_nt(stacked(left[...]), onehot[...]))
        return
    a, b = sweep_weights(weights, inverse)
    change = b * left[...] if a is None else a * update[...] + b * left[...]
    new[...] = iterate[...] + change if mode == "last" else change


def late_kernel(table, received, residual, update, inverse, matrix, *refs, size, lay, weights, mode):
    refs = list(refs)
    rows = residual.shape[0]
    names = refs.pop(0) if mode == "spread" else None
    wide, scaled = refs[-2:]
    if mode == "last":
        new = refs[0]
        new[...] = update[...]
    else:
        left, new = refs[:2]
    if mode == "spread":
        width = lay.slots * size
        chosen = names[:, LAST * width : (LAST + 1) * width]
        put_halo(wide, 0, halves(dot_nn(stacked(received[...]), chosen)), size)
    else:
        put_halo(wide, 0, received[0:rows, :], size)
    scaled[0:1, :] = sweep_weights(weights, inverse)[1]

    def use(found):
        for at, product in found:
            if mode != "last":
                left[:, at] = left[:, at] - product
            new[:, at] = new[:, at] - scaled[0:1, at] * product

    for_received(table, lay, (LAST,), matrix, wide, size, use)
    if mode != "last":
        pack(table, new, refs[2:6], size, lay.slots)


def restrict_kernel(
    table, received, residual, matrix, onehot, part, coarse_inverse, left, total, start, wide, *, size, lay
):
    rows = residual.shape[0]
    put_halo(wide, 0, received[0:rows, :], size)
    total[...] = part[...]

    def use(found):
        for at, product in found:
            left[:, at] = left[:, at] - product
        amount = sum(halves(dot_nt(stacked(product), onehot[:, at])) for at, product in found)
        total[...] = total[...] - amount

    for_received(table, lay, (LAST,), matrix, wide, size, use)
    start[...] = coarse_inverse[0:1, :] * total[...] / center_value


def coarse_kernel(
    h0, h1, h2, h3, residual, update, iterate, coarse_high, coarse_low, coarse_inverse, *outs, weights, last
):
    c = update[...]
    rows = c.shape[0]
    high, low = high_low(jnp.concatenate([c] + [h[...] for h in (h0, h1, h2, h3)], axis=1))
    product = halves(dot_nt(jnp.concatenate([high, low], axis=0), coarse_high[...]))
    left = residual[...] - (product + dot_nt(high, coarse_low[...]))
    new = weights[0] * c + weights[1] * coarse_inverse[0:1, :] * left
    outs[0][...] = iterate[...] + new
    if not last:
        outs[1][...] = left
        outs[2][...] = new


def spread_kernel(
    table, correction, onehot, iterate, leftover, matrix, second, out, correction_out, field, wide, *, size, lay
):
    field[...] = halves(dot_nn(stacked(correction[...]), onehot[...]))
    local_kernel(table, field, leftover, iterate, matrix, out, second, wide, size=size, lay=lay)
    correction_out[...] = correction[...]


def local_program(
    right_side, start_guess, fine_matrix, fine_columns, send_lists, aggregates, coarse_matrix
):
    perms = exchanges(lax.axis_size("span"), lax.axis_size("stream"))
    rows, width = right_side.shape
    blocks, count, size, _ = fine_matrix.shape
    slots = send_lists.shape[1] // 4
    halo_width = slots * size
    lay = Table(blocks, count, slots)
    groups = aggregates.reshape(1, width)
    stored = fine_matrix.reshape(blocks * count, size, size)
    coarse = coarse_matrix.reshape(coarse_matrix.shape[1:])
    weights = chebyshev_weights()
    parts = 4 if blocks % 4 == 0 else 1

    spaces = {
        "v": pl.BlockSpec(memory_space=pltpu.VMEM),
        "s": pl.BlockSpec(memory_space=pltpu.SMEM),
        "h": pl.BlockSpec(memory_space=pltpu.HBM),
    }

    def call(kernel, ins, outs, scratch=(), where="", kept="", aliases=None, flops=0, **named):
        where = where + "v" * (len(ins) - len(where))
        kept = kept + "v" * (len(outs) - len(kept))
        fixed = {"h": pltpu.HBM, "V": pltpu.VMEM}
        ins = [
            pltpu.with_memory_space_constraint(x, fixed[c]) if c in fixed else x
            for x, c in zip(ins, where)
        ]
        forms = {
            "v": jax.ShapeDtypeStruct,
            "V": pltpu.MemorySpace.VMEM,
            "s": pltpu.MemorySpace.SMEM,
        }
        return pl.pallas_call(
            functools.partial(kernel, **named),
            out_shape=[forms[c](shape, kind) for c, (shape, kind) in zip(kept, outs)],
            in_specs=[spaces[c.lower()] for c in where],
            out_specs=[spaces[c.lower()] for c in kept],
            scratch_shapes=list(scratch),
            input_output_aliases=aliases or {},
            compiler_params=pltpu.CompilerParams(vmem_limit_bytes=VMEM_LIMIT),
            cost_estimate=pl.CostEstimate(
                flops=flops, bytes_accessed=4 * 1024 * 1024, transcendentals=0
            ),
        )(*ins)

    def exchange(payloads):
        got = [None] * 4
        for buffer in ORDER:
            got[buffer] = lax.ppermute(payloads[buffer], AXES, perms[buffer])
        return got

    field = ((rows, width), f32)
    halo = ((rows, halo_width), f32)
    small = ((rows, size), f32)
    wide_local = pltpu.VMEM((2 * rows, width + size), bf16)
    wide_early = pltpu.VMEM((2 * rows, 3 * (halo_width + size)), bf16)
    wide_late = pltpu.VMEM((2 * rows, halo_width + size), bf16)
    flops = 2 * 2 * rows * blocks * count * size * size
    dims = {"size": size, "lay": lay}

    def early(halos, residual, update, weight, mode="plain", extra=()):
        return call(
            early_kernel,
            [table] + [halos[b] for b in EARLY] + [residual, update, inverse, matrix] + list(extra),
            [field, small if mode == "restrict" else field], [wide_early], "s",
            "vv" if mode == "last" else "Vv" if mode == "restrict" else "VV",
            flops=flops // 5, weights=weight, mode=mode, **dims,
        )

    def sweep(halos, residual, update, weight, mode="plain", extra=(), late_extra=()):
        residual, update = early(halos, residual, update, weight, mode, extra)
        ins = [table, halos[LAST], residual, update, inverse, matrix] + list(late_extra)
        scratch = [wide_late, pltpu.VMEM((8, width), f32)]
        named = dict(flops=flops // 10, weights=weight, mode=mode, **dims)
        if mode == "last":
            return call(late_kernel, ins, [field], scratch, "s", **named)
        return call(
            late_kernel, ins, [field, field] + [halo] * 4, scratch, "svVV", "VV",
            {2: 0, 3: 1}, **named,
        )

    def local(update, residual, iterate):
        return call(
            local_kernel, [table, update, residual, iterate, matrix], [field, field],
            [wide_local], "s", flops=flops, **dims,
        )

    *payloads, guess, lists, columns = call(
        load_kernel,
        [start_guess, send_lists, fine_columns.T, groups],
        [((rows + 8, halo_width), f32)] * 4
        + [field, (send_lists.shape, i32), (fine_columns.shape[::-1], i32)],
        [pltpu.VMEM((1, width), i32), pltpu.SemaphoreType.DMA((4,))],
        "hhhh", "vvvvvss", size=size, slots=slots,
    )
    first_halos = halos = exchange(payloads)
    residual, table, inverse, matrix = call(
        first_kernel,
        [lists, columns, guess, right_side, stored],
        [field, ((lay.length,), i32), ((8, width), f32), (stored.shape, bf16)],
        [wide_local, pltpu.VMEM(*field), pltpu.SemaphoreType.DMA((parts + 1,))],
        "ssvhh", "vs", flops=flops, parts=parts, **dims,
    )
    iterate = guess
    residual, update, *payloads = sweep(halos, residual, guess, None)
    halos = exchange(payloads)
    residual, iterate, onehot, names, coarse_high, coarse_low, coarse_inverse = call(
        local_and_coarse_kernel,
        [table, update, residual, iterate, matrix, groups, coarse] + first_halos,
        [
            field,
            field,
            ((size, width), bf16),
            ((size, 4 * halo_width), bf16),
            ((size, 5 * size), bf16),
            ((size, 5 * size), bf16),
            ((8, size), f32),
        ],
        [
            wide_local,
            pltpu.VMEM(coarse.shape, f32),
            pltpu.VMEM((1, width), i32),
            pltpu.SemaphoreType.DMA((2,)),
        ],
        "svvvvhh", flops=flops, **dims,
    )
    residual, update, *payloads = sweep(halos, residual, update, weights[0])
    halos = exchange(payloads)
    residual, iterate = local(update, residual, iterate)
    residual, update, *payloads = sweep(halos, residual, update, weights[1])
    halos = exchange(payloads)
    residual, iterate = local(update, residual, iterate)
    residual, part = early(halos, residual, update, None, "restrict", (onehot,))
    leftover, coarse_left, c = call(
        restrict_kernel,
        [table, halos[LAST], residual, matrix, onehot, part, coarse_inverse],
        [field, small, small], [wide_late], "svV", "V", {2: 0}, flops=flops // 10, **dims,
    )
    correction = c
    for i, weight in enumerate(weights):
        halos = exchange([c] * 4)
        result = call(
            coarse_kernel,
            halos + [coarse_left, c, correction, coarse_high, coarse_low, coarse_inverse],
            [small] if i == 1 else [small] * 3, weights=weight, last=i == 1,
        )
        correction = result[0]
        if i == 0:
            coarse_left, c = result[1:]
    halos = exchange([correction] * 4)
    iterate, residual, correction_out = call(
        spread_kernel,
        [table, correction, onehot, iterate, leftover, matrix], [field, field, small],
        [pltpu.VMEM(*field), wide_local], "s", flops=flops, **dims,
    )
    residual, update, *payloads = sweep(
        halos, residual, iterate, None, "spread", (names,), (names,)
    )
    halos = exchange(payloads)
    residual, iterate = local(update, residual, iterate)
    residual, update, *payloads = sweep(halos, residual, update, weights[0])
    halos = exchange(payloads)
    residual, iterate = local(update, residual, iterate)
    result = sweep(halos, residual, update, weights[1], "last", (iterate,))
    return (result[0], correction_out)


def solution(mesh):
    placed = (
        P(None, AXES),
        P(None, AXES),
        P(AXES, None, None, None),
        P(AXES, None),
        P(AXES, None),
        P(AXES),
        P(AXES, None, None, None),
    )
    return jax.shard_map(
        local_program,
        mesh=mesh,
        in_specs=placed,
        out_specs=(P(None, AXES), P(None, AXES)),
        check_vma=False,
    )
```

time: 259 us -> 72.1 us (0.28); the launches traced: 256 us -> 71.9 us
  local copies, waits for them, and re-layouts: 78.8 us -> 0 us
  starting transfers between devices: 92.1 us -> 32.9 us
  other arithmetic: 29.5 us -> 0 us
  matrix products: 25.6 us -> 0 us
  Pallas kernels: 0 us -> 21 us
  waiting for transfers between devices: 28.5 us -> 17.2 us
    ppermute x36, starting transfers between devices: 92.1 us -> 32.9 us  [exchange(): got[buffer] = lax.ppermute(payloads[buffer], AXES, perms[buffer])]
    gather x16 -> x0, local copies, waits for them, and re-layouts: 41 us -> none  [the longest x7 22.7 us: fine_apply(): jnp.take(extended, flat_cols, axis=1)]
    unnamed x82 -> x0, local copies, waits for them, and re-layouts: 28.1 us -> none
    dot_general x11 -> x0, matrix products: 25.6 us -> none  [the longest x7 22.9 us: block_product(): jnp.einsum('rkij,vrkj->vri', fine_matrix.astype(jnp.float32), picked, pre...]
    select_n x16 -> x0, other arithmetic: 21.6 us -> none  [the longest x8 14 us: fine_apply(): jnp.take(extended, flat_cols, axis=1)]
    pallas_call x0 -> x24, Pallas kernels: none -> 21 us  [call(): pl.pallas_call(functools.partial(kernel, **named), out_shape=[forms[c](sh...]
    ppermute x36, waiting for transfers between devices: 28.5 us -> 17.2 us  [exchange(): got[buffer] = lax.ppermute(payloads[buffer], AXES, perms[buffer])]
    reshape x6 -> x0, local copies, waits for them, and re-layouts: 4.64 us -> none  [the longest x5 4.55 us: fine_apply(): blocks = vector.reshape(vec_count, blk_count, block_size)]
  transfers between devices with their start and end apart: 36 -> 36, of which waited for: 8 -> 13; matrix products, arithmetic and copies ran while one was open for 12% -> 0% of each run, Pallas kernels for 0% -> 22%
where the time goes in v2:
time: 72.1 us; the launch traced here: 71.9 us
  starting transfers between devices  32.9 us (46%)
  Pallas kernels  21 us (29%)
  waiting for transfers between devices  17.2 us (24%)
  between operations  0.87 us (1%)
    ppermute x36, starting transfers between devices, exchange(): got[buffer] = lax.ppermute(payloads[buffer], AXES, perms[buffer])  32.9 us
    pallas_call x24, Pallas kernels, call(): pl.pallas_call(functools.partial(kernel, **named), out_shape=[forms[c](sh...  21 us
    ppermute x36, waiting for transfers between devices, exchange(): got[buffer] = lax.ppermute(payloads[buffer], AXES, perms[buffer])  17.2 us
  transfers between devices with their start and end apart: 36, of which 13 were waited for; matrix products, arithmetic and copies ran while one was open for 0% of the time, Pallas kernels for 22%

profile of v2, /device:TPU:0, one launch (start us, length us, event | category | flops | bytes accessed | tf_op | source)
XLA Modules:
  0.0 71.9 jit_solution(3080024037807764930)
XLA Ops:
  0.6 1.2 %shard_map.86 = (f32[72,512]{1,0:T(8,128)S(1)}, f32[72,512]{1,0:T(8,128)S(1)}, f32[72,512]{1,0:T(8,128)S(1)}, f32[72,512]{1,0:T(8,128)S(1)}, f32[64,2048]{1,0:T(...) custom-call(f32[64,2048]{1,0:T(8,128)} %guess.1, s32[1,16]{1,0:T(1,128)} %lists.1, s32[5,16]{1,0:T(8,128)} %bitcast.8, ...), custom_call_target="tpu_custom_call" | custom-call | bytes 4194304 | tf_op jit(solution)/shard_map/pallas_call | solution.py:473
  1.8 3.1 %collective-permute-start.1 = (f32[72,512]{1,0:T(8,128)S(1)}, f32[72,512]{1,0:T(8,128)S(1)}, u32[]{:S(2)}, u32[]{:S(2)}) collective-permute-start(f32[72,512]{1,0:T(8,128)S(1)} %get-tuple-element.86), channel_id=1, source_target_pairs={{0,8},{1,9},{2,10},{3,11},{4,12},{5,13},{6,14},{7,15},{8,0},{9,1},... | collective-permute-start | bytes 442376 | tf_op jit(solution)/shard_map/ppermute | solution.py:489
  5.4 2.6 %collective-permute-start = (f32[72,512]{1,0:T(8,128)S(1)}, f32[72,512]{1,0:T(8,128)S(1)}, u32[]{:S(2)}, u32[]{:S(2)}) collective-permute-start(f32[72,512]{1,0:T(8,128)S(1)} %get-tuple-element.85), channel_id=1, source_target_pairs={{0,8},{1,2},{2,1},{3,4},{4,3},{5,6},{6,5},{7,15},{8,0},{9,10},{10,... | collective-permute-start | bytes 442376 | tf_op jit(solution)/shard_map/ppermute | solution.py:489
  8.1 3.4 %shard_map.87 = (f32[64,2048]{1,0:T(8,128)S(1)}, s32[446]{0:T(512)S(4)}, f32[8,2048]{1,0:T(8,128)S(1)}, bf16[80,128,128]{2,1,0:T(8,128)(2,1)S(1)}) custom-call(s32[1,16]{1,0:T(1,128)S(4)} %get-tuple-element.81.lists, s32[5,16]{1,0:T(8,128)S(4)} %get-tuple-element.82.columns, f32[64,2048]{1,0:T(8,128)S(1)} %get-tuple-element.83.field.update.iterate, ...), custom_call_target="tpu_custom_call" | custom-call | flops 335544320 | bytes 4194304 | tf_op jit(solution)/shard_map/pallas_call | solution.py:473
  12.4 1.2 %collective-permute-start.5 = (f32[64,512]{1,0:T(8,128)S(1)}, f32[64,512]{1,0:T(8,128)S(1)}, u32[]{:S(2)}, u32[]{:S(2)}) collective-permute-start(f32[64,512]{1,0:T(8,128)S(1)} %get-tuple-element.95), channel_id=1, source_target_pairs={{0,8},{1,9},{2,10},{3,11},{4,12},{5,13},{6,14},{7,15},{8,0},{9,1},... | collective-permute-start | bytes 393224 | tf_op jit(solution)/shard_map/ppermute | solution.py:489
  15.6 2.1 %shard_map.90 = (f32[64,2048]{1,0:T(8,128)S(1)}, f32[64,2048]{1,0:T(8,128)S(1)}, bf16[128,2048]{1,0:T(8,128)(2,1)S(1)}, bf16[128,2048]{1,0:T(8,128)(2,1)S(1)}, b...) custom-call(s32[446]{0:T(512)S(4)} %get-tuple-element.84.table, ...), custom_call_target="tpu_custom_call" | custom-call | flops 335544320 | bytes 4194304 | tf_op jit(solution)/shard_map/pallas_call | solution.py:473
  20.2 1.5 %collective-permute-start.9 = (f32[64,512]{1,0:T(8,128)S(1)}, f32[64,512]{1,0:T(8,128)S(1)}, u32[]{:S(2)}, u32[]{:S(2)}) collective-permute-start(f32[64,512]{1,0:T(8,128)S(1)} %get-tuple-element.104), channel_id=1, source_target_pairs={{0,8},{1,9},{2,10},{3,11},{4,12},{5,13},{6,14},{7,15},{8,0},{9,1},... | collective-permute-start | bytes 393224 | tf_op jit(solution)/shard_map/ppermute | solution.py:489
  23.5 2.1 %collective-permute-done.9.h0 = f32[64,512]{1,0:T(8,128)S(1)} collective-permute-done((f32[64,512]{1,0:T(8,128)S(1)}, f32[64,512]{1,0:T(8,128)S(1)}, u32[]{:S(2)}, u32[]{:S(2)}) %collective-permute-start.9) | collective-permute-done | bytes 131104 | tf_op jit(solution)/shard_map/ppermute | solution.py:489
  27.5 1.6 %collective-permute-start.13 = (f32[64,512]{1,0:T(8,128)S(1)}, f32[64,512]{1,0:T(8,128)S(1)}, u32[]{:S(2)}, u32[]{:S(2)}) collective-permute-start(f32[64,512]{1,0:T(8,128)S(1)} %get-tuple-element.114), channel_id=1, source_target_pairs={{0,8},{1,9},{2,10},{3,11},{4,12},{5,13},{6,14},{7,15},{8,0},{9,1},... | collective-permute-start | bytes 393224 | tf_op jit(solution)/shard_map/ppermute | solution.py:489
  31.1 1.7 %collective-permute-done.13.h0 = f32[64,512]{1,0:T(8,128)S(1)} collective-permute-done((f32[64,512]{1,0:T(8,128)S(1)}, f32[64,512]{1,0:T(8,128)S(1)}, u32[]{:S(2)}, u32[]{:S(2)}) %collective-permute-start.13) | collective-permute-done | bytes 131104 | tf_op jit(solution)/shard_map/ppermute | solution.py:489
  36.6 2.7 %collective-permute-start.16 = (f32[64,128]{1,0:T(8,128)S(1)}, f32[64,128]{1,0:T(8,128)S(1)}, u32[]{:S(2)}, u32[]{:S(2)}) collective-permute-start(f32[64,128]{1,0:T(8,128)S(1)} %get-tuple-element.125.update.iterate), channel_id=1, source_target_pairs={{0,8},{1,9},{2,10},{3,11},{4,12},{5,13},{6,14},{7,15},{8,0},{9,1},... | collective-permute-start | bytes 98312 | tf_op jit(solution)/shard_map/ppermute | solution.py:489
  39.2 1.9 %collective-permute-done.16.h0 = f32[64,128]{1,0:T(8,128)S(1)} collective-permute-done((f32[64,128]{1,0:T(8,128)S(1)}, f32[64,128]{1,0:T(8,128)S(1)}, u32[]{:S(2)}, u32[]{:S(2)}) %collective-permute-start.16) | collective-permute-done | bytes 32800 | tf_op jit(solution)/shard_map/ppermute | solution.py:489
  41.4 2.1 %collective-permute-start.23 = (f32[64,128]{1,0:T(8,128)S(1)}, f32[64,128]{1,0:T(8,128)S(1)}, u32[]{:S(2)}, u32[]{:S(2)}) collective-permute-start(f32[64,128]{1,0:T(8,128)S(1)} %get-tuple-element.129.update), channel_id=1, source_target_pairs={{0,8},{1,2},{2,1},{3,4},{4,3},{5,6},{6,5},{7,15},{8,0},{9,10},{10,... | collective-permute-start | bytes 98312 | tf_op jit(solution)/shard_map/ppermute | solution.py:489
  44.4 2.5 %collective-permute-start.20 = (f32[64,128]{1,0:T(8,128)S(1)}, f32[64,128]{1,0:T(8,128)S(1)}, u32[]{:S(2)}, u32[]{:S(2)}) collective-permute-start(f32[64,128]{1,0:T(8,128)S(1)} %get-tuple-element.129.update), channel_id=1, source_target_pairs={{0,8},{1,9},{2,10},{3,11},{4,12},{5,13},{6,14},{7,15},{8,0},{9,1},... | collective-permute-start | bytes 98312 | tf_op jit(solution)/shard_map/ppermute | solution.py:489
  46.9 1.9 %collective-permute-done.20.h0 = f32[64,128]{1,0:T(8,128)S(1)} collective-permute-done((f32[64,128]{1,0:T(8,128)S(1)}, f32[64,128]{1,0:T(8,128)S(1)}, u32[]{:S(2)}, u32[]{:S(2)}) %collective-permute-start.20) | collective-permute-done | bytes 32800 | tf_op jit(solution)/shard_map/ppermute | solution.py:489
  49.6 3.2 %collective-permute-start.25 = (f32[64,128]{1,0:T(8,128)S(1)}, f32[64,128]{1,0:T(8,128)S(1)}, u32[]{:S(2)}, u32[]{:S(2)}) collective-permute-start(f32[64,128]{1,0:T(8,128)S(1)} %shard_map.100.correction), channel_id=1, source_target_pairs={{0,8},{1,9},{2,10},{3,11},{4,12},{5,13},{6,14},{7,15},{8,0},{9,1},... | collective-permute-start | bytes 98312 | tf_op jit(solution)/shard_map/ppermute | solution.py:489
  52.8 1.8 %shard_map.101 = (f32[64,2048]{1,0:T(8,128)S(1)}, f32[64,2048]{1,0:T(8,128)S(1)}, f32[64,128]{1,0:T(8,128)}) custom-call(s32[446]{0:T(512)S(4)} %get-tuple-element.84.table, f32[64,128]{1,0:T(8,128)S(1)} %shard_map.100.correction, bf16[128,2048]{1,0:T(8,128)(2,1)S(1)} %get-tuple-element.121.refs_0_.onehot, f32[64,2048]{1,0:T(8,128)S(1)} %get-tuple-element.132.iterate, ...), custom_call_target="tpu_custom_call" | custom-call | flops 335544320 | bytes 4194304 | tf_op jit(solution)/shard_map/pallas_call | solution.py:473
  55.4 1.3 %collective-permute-done.24.received = f32[64,128]{1,0:T(8,128)S(1)} collective-permute-done((f32[64,128]{1,0:T(8,128)S(1)}, f32[64,128]{1,0:T(8,128)S(1)}, u32[]{:S(2)}, u32[]{:S(2)}) %collective-permute-start.24) | collective-permute-done | bytes 32800 | tf_op jit(solution)/shard_map/ppermute | solution.py:489
  58.5 1.2 %collective-permute-start.28 = (f32[64,512]{1,0:T(8,128)S(1)}, f32[64,512]{1,0:T(8,128)S(1)}, u32[]{:S(2)}, u32[]{:S(2)}) collective-permute-start(f32[64,512]{1,0:T(8,128)S(1)} %get-tuple-element.139), channel_id=1, source_target_pairs={{0,8},{1,2},{2,1},{3,4},{4,3},{5,6},{6,5},{7,15},{8,0},{9,10},{10,... | collective-permute-start | bytes 393224 | tf_op jit(solution)/shard_map/ppermute | solution.py:489
  59.7 1.2 %shard_map.104 = (f32[64,2048]{1,0:T(8,128)S(1)}, f32[64,2048]{1,0:T(8,128)S(1)}) custom-call(s32[446]{0:T(512)S(4)} %get-tuple-element.84.table, f32[64,2048]{1,0:T(8,128)S(1)} %get-tuple-element.143.update, f32[64,2048]{1,0:T(8,128)S(1)} %get-tuple-element.144.residual, f32[64,2048]{1,0:T(8,128)S(1)} %get-tuple-element.135.update.iterate, ...), custom_call_target="tpu_custom_call" | custom-call | flops 335544320 | bytes 4194304 | tf_op jit(solution)/shard_map/pallas_call | solution.py:473
  60.9 1.3 %collective-permute-done.29.h0 = f32[64,512]{1,0:T(8,128)S(1)} collective-permute-done((f32[64,512]{1,0:T(8,128)S(1)}, f32[64,512]{1,0:T(8,128)S(1)}, u32[]{:S(2)}, u32[]{:S(2)}) %collective-permute-start.29) | collective-permute-done | bytes 131104 | tf_op jit(solution)/shard_map/ppermute | solution.py:489
  63.9 1.3 %collective-permute-start.33 = (f32[64,512]{1,0:T(8,128)S(1)}, f32[64,512]{1,0:T(8,128)S(1)}, u32[]{:S(2)}, u32[]{:S(2)}) collective-permute-start(f32[64,512]{1,0:T(8,128)S(1)} %get-tuple-element.149), channel_id=1, source_target_pairs={{0,8},{1,9},{2,10},{3,11},{4,12},{5,13},{6,14},{7,15},{8,0},{9,1},... | collective-permute-start | bytes 393224 | tf_op jit(solution)/shard_map/ppermute | solution.py:489
  65.7 1.2 %collective-permute-start.32 = (f32[64,512]{1,0:T(8,128)S(1)}, f32[64,512]{1,0:T(8,128)S(1)}, u32[]{:S(2)}, u32[]{:S(2)}) collective-permute-start(f32[64,512]{1,0:T(8,128)S(1)} %get-tuple-element.148), channel_id=1, source_target_pairs={{0,8},{1,2},{2,1},{3,4},{4,3},{5,6},{6,5},{7,15},{8,0},{9,10},{10,... | collective-permute-start | bytes 393224 | tf_op jit(solution)/shard_map/ppermute | solution.py:489
  68.0 1.5 %collective-permute-done.33.h0 = f32[64,512]{1,0:T(8,128)S(1)} collective-permute-done((f32[64,512]{1,0:T(8,128)S(1)}, f32[64,512]{1,0:T(8,128)S(1)}, u32[]{:S(2)}, u32[]{:S(2)}) %collective-permute-start.33) | collective-permute-done | bytes 131104 | tf_op jit(solution)/shard_map/ppermute | solution.py:489
  (72 shorter events, 25.6 us)
Async XLA Ops:
  1.8 9.7 %collective-permute-start.1 = (f32[72,512]{1,0:T(8,128)S(1)}, f32[72,512]{1,0:T(8,128)S(1)}, u32[]{:S(2)}, u32[]{:S(2)}) collective-permute-start(f32[72,512]{1,0:T(8,128)S(1)} %get-tuple-element.86), channel_id=1, source_target_pairs={{0,8},{1,9},{2,10},{3,11},{4,12},{5,13},{6,14},{7,15},{8,0},{9,1},... | collective-permute-start | bytes 442376 | tf_op jit(solution)/shard_map/ppermute | solution.py:489
  4.9 6.6 %collective-permute-start.2 = (f32[72,512]{1,0:T(8,128)S(1)}, f32[72,512]{1,0:T(8,128)S(1)}, u32[]{:S(2)}, u32[]{:S(2)}) collective-permute-start(f32[72,512]{1,0:T(8,128)S(1)} %get-tuple-element.87), channel_id=1, source_target_pairs={{0,1},{1,0},{2,3},{3,2},{4,5},{5,4},{6,7},{7,6},{8,16},{9,17},{10,... | collective-permute-start | bytes 442376 | tf_op jit(solution)/shard_map/ppermute | solution.py:489
  4.9 6.6 %collective-permute-start.3 = (f32[72,512]{1,0:T(8,128)S(1)}, f32[72,512]{1,0:T(8,128)S(1)}, u32[]{:S(2)}, u32[]{:S(2)}) collective-permute-start(f32[72,512]{1,0:T(8,128)S(1)} %get-tuple-element.88), channel_id=1, source_target_pairs={{0,1},{1,0},{2,3},{3,2},{4,5},{5,4},{6,7},{7,6},{8,9},{9,8},{10,11... | collective-permute-start | bytes 442376 | tf_op jit(solution)/shard_map/ppermute | solution.py:489
  5.4 6.6 %collective-permute-start = (f32[72,512]{1,0:T(8,128)S(1)}, f32[72,512]{1,0:T(8,128)S(1)}, u32[]{:S(2)}, u32[]{:S(2)}) collective-permute-start(f32[72,512]{1,0:T(8,128)S(1)} %get-tuple-element.85), channel_id=1, source_target_pairs={{0,8},{1,2},{2,1},{3,4},{4,3},{5,6},{6,5},{7,15},{8,0},{9,10},{10,... | collective-permute-start | bytes 442376 | tf_op jit(solution)/shard_map/ppermute | solution.py:489
  12.4 6.1 %collective-permute-start.5 = (f32[64,512]{1,0:T(8,128)S(1)}, f32[64,512]{1,0:T(8,128)S(1)}, u32[]{:S(2)}, u32[]{:S(2)}) collective-permute-start(f32[64,512]{1,0:T(8,128)S(1)} %get-tuple-element.95), channel_id=1, source_target_pairs={{0,8},{1,9},{2,10},{3,11},{4,12},{5,13},{6,14},{7,15},{8,0},{9,1},... | collective-permute-start | bytes 393224 | tf_op jit(solution)/shard_map/ppermute | solution.py:489
  13.6 4.9 %collective-permute-start.6 = (f32[64,512]{1,0:T(8,128)S(1)}, f32[64,512]{1,0:T(8,128)S(1)}, u32[]{:S(2)}, u32[]{:S(2)}) collective-permute-start(f32[64,512]{1,0:T(8,128)S(1)} %get-tuple-element.96), channel_id=1, source_target_pairs={{0,1},{1,0},{2,3},{3,2},{4,5},{5,4},{6,7},{7,6},{8,16},{9,17},{10,... | collective-permute-start | bytes 393224 | tf_op jit(solution)/shard_map/ppermute | solution.py:489
  14.5 5.3 %collective-permute-start.4 = (f32[64,512]{1,0:T(8,128)S(1)}, f32[64,512]{1,0:T(8,128)S(1)}, u32[]{:S(2)}, u32[]{:S(2)}) collective-permute-start(f32[64,512]{1,0:T(8,128)S(1)} %get-tuple-element.94), channel_id=1, source_target_pairs={{0,8},{1,2},{2,1},{3,4},{4,3},{5,6},{6,5},{7,15},{8,0},{9,10},{10,... | collective-permute-start | bytes 393224 | tf_op jit(solution)/shard_map/ppermute | solution.py:489
  20.2 5.4 %collective-permute-start.9 = (f32[64,512]{1,0:T(8,128)S(1)}, f32[64,512]{1,0:T(8,128)S(1)}, u32[]{:S(2)}, u32[]{:S(2)}) collective-permute-start(f32[64,512]{1,0:T(8,128)S(1)} %get-tuple-element.104), channel_id=1, source_target_pairs={{0,8},{1,9},{2,10},{3,11},{4,12},{5,13},{6,14},{7,15},{8,0},{9,1},... | collective-permute-start | bytes 393224 | tf_op jit(solution)/shard_map/ppermute | solution.py:489
  22.3 5.0 %collective-permute-start.8 = (f32[64,512]{1,0:T(8,128)S(1)}, f32[64,512]{1,0:T(8,128)S(1)}, u32[]{:S(2)}, u32[]{:S(2)}) collective-permute-start(f32[64,512]{1,0:T(8,128)S(1)} %get-tuple-element.103), channel_id=1, source_target_pairs={{0,8},{1,2},{2,1},{3,4},{4,3},{5,6},{6,5},{7,15},{8,0},{9,10},{10,... | collective-permute-start | bytes 393224 | tf_op jit(solution)/shard_map/ppermute | solution.py:489
  27.5 5.2 %collective-permute-start.13 = (f32[64,512]{1,0:T(8,128)S(1)}, f32[64,512]{1,0:T(8,128)S(1)}, u32[]{:S(2)}, u32[]{:S(2)}) collective-permute-start(f32[64,512]{1,0:T(8,128)S(1)} %get-tuple-element.114), channel_id=1, source_target_pairs={{0,8},{1,9},{2,10},{3,11},{4,12},{5,13},{6,14},{7,15},{8,0},{9,1},... | collective-permute-start | bytes 393224 | tf_op jit(solution)/shard_map/ppermute | solution.py:489
  29.6 5.0 %collective-permute-start.12 = (f32[64,512]{1,0:T(8,128)S(1)}, f32[64,512]{1,0:T(8,128)S(1)}, u32[]{:S(2)}, u32[]{:S(2)}) collective-permute-start(f32[64,512]{1,0:T(8,128)S(1)} %get-tuple-element.113), channel_id=1, source_target_pairs={{0,8},{1,2},{2,1},{3,4},{4,3},{5,6},{6,5},{7,15},{8,0},{9,10},{10,... | collective-permute-start | bytes 393224 | tf_op jit(solution)/shard_map/ppermute | solution.py:489
  36.6 4.5 %collective-permute-start.16 = (f32[64,128]{1,0:T(8,128)S(1)}, f32[64,128]{1,0:T(8,128)S(1)}, u32[]{:S(2)}, u32[]{:S(2)}) collective-permute-start(f32[64,128]{1,0:T(8,128)S(1)} %get-tuple-element.125.update.iterate), channel_id=1, source_target_pairs={{0,8},{1,9},{2,10},{3,11},{4,12},{5,13},{6,14},{7,15},{8,0},{9,1},... | collective-permute-start | bytes 98312 | tf_op jit(solution)/shard_map/ppermute | solution.py:489
  41.4 5.5 %collective-permute-start.23 = (f32[64,128]{1,0:T(8,128)S(1)}, f32[64,128]{1,0:T(8,128)S(1)}, u32[]{:S(2)}, u32[]{:S(2)}) collective-permute-start(f32[64,128]{1,0:T(8,128)S(1)} %get-tuple-element.129.update), channel_id=1, source_target_pairs={{0,8},{1,2},{2,1},{3,4},{4,3},{5,6},{6,5},{7,15},{8,0},{9,10},{10,... | collective-permute-start | bytes 98312 | tf_op jit(solution)/shard_map/ppermute | solution.py:489
  44.4 4.4 %collective-permute-start.20 = (f32[64,128]{1,0:T(8,128)S(1)}, f32[64,128]{1,0:T(8,128)S(1)}, u32[]{:S(2)}, u32[]{:S(2)}) collective-permute-start(f32[64,128]{1,0:T(8,128)S(1)} %get-tuple-element.129.update), channel_id=1, source_target_pairs={{0,8},{1,9},{2,10},{3,11},{4,12},{5,13},{6,14},{7,15},{8,0},{9,1},... | collective-permute-start | bytes 98312 | tf_op jit(solution)/shard_map/ppermute | solution.py:489
  49.1 5.6 %collective-permute-start.27 = (f32[64,128]{1,0:T(8,128)S(1)}, f32[64,128]{1,0:T(8,128)S(1)}, u32[]{:S(2)}, u32[]{:S(2)}) collective-permute-start(f32[64,128]{1,0:T(8,128)S(1)} %shard_map.100.correction), channel_id=1, source_target_pairs={{0,1},{1,0},{2,3},{3,2},{4,5},{5,4},{6,7},{7,6},{8,9},{9,8},{10,11... | collective-permute-start | bytes 98312 | tf_op jit(solution)/shard_map/ppermute | solution.py:489
  49.1 5.5 %collective-permute-start.26 = (f32[64,128]{1,0:T(8,128)S(1)}, f32[64,128]{1,0:T(8,128)S(1)}, u32[]{:S(2)}, u32[]{:S(2)}) collective-permute-start(f32[64,128]{1,0:T(8,128)S(1)} %shard_map.100.correction), channel_id=1, source_target_pairs={{0,1},{1,0},{2,3},{3,2},{4,5},{5,4},{6,7},{7,6},{8,16},{9,17},{10,... | collective-permute-start | bytes 98312 | tf_op jit(solution)/shard_map/ppermute | solution.py:489
  49.6 5.1 %collective-permute-start.25 = (f32[64,128]{1,0:T(8,128)S(1)}, f32[64,128]{1,0:T(8,128)S(1)}, u32[]{:S(2)}, u32[]{:S(2)}) collective-permute-start(f32[64,128]{1,0:T(8,128)S(1)} %shard_map.100.correction), channel_id=1, source_target_pairs={{0,8},{1,9},{2,10},{3,11},{4,12},{5,13},{6,14},{7,15},{8,0},{9,1},... | collective-permute-start | bytes 98312 | tf_op jit(solution)/shard_map/ppermute | solution.py:489
  57.2 5.0 %collective-permute-start.29 = (f32[64,512]{1,0:T(8,128)S(1)}, f32[64,512]{1,0:T(8,128)S(1)}, u32[]{:S(2)}, u32[]{:S(2)}) collective-permute-start(f32[64,512]{1,0:T(8,128)S(1)} %get-tuple-element.140), channel_id=1, source_target_pairs={{0,8},{1,9},{2,10},{3,11},{4,12},{5,13},{6,14},{7,15},{8,0},{9,1},... | collective-permute-start | bytes 393224 | tf_op jit(solution)/shard_map/ppermute | solution.py:489
  58.0 4.2 %collective-permute-start.30 = (f32[64,512]{1,0:T(8,128)S(1)}, f32[64,512]{1,0:T(8,128)S(1)}, u32[]{:S(2)}, u32[]{:S(2)}) collective-permute-start(f32[64,512]{1,0:T(8,128)S(1)} %get-tuple-element.141), channel_id=1, source_target_pairs={{0,1},{1,0},{2,3},{3,2},{4,5},{5,4},{6,7},{7,6},{8,16},{9,17},{10,... | collective-permute-start | bytes 393224 | tf_op jit(solution)/shard_map/ppermute | solution.py:489
  58.0 4.2 %collective-permute-start.31 = (f32[64,512]{1,0:T(8,128)S(1)}, f32[64,512]{1,0:T(8,128)S(1)}, u32[]{:S(2)}, u32[]{:S(2)}) collective-permute-start(f32[64,512]{1,0:T(8,128)S(1)} %get-tuple-element.142), channel_id=1, source_target_pairs={{0,1},{1,0},{2,3},{3,2},{4,5},{5,4},{6,7},{7,6},{8,9},{9,8},{10,11... | collective-permute-start | bytes 393224 | tf_op jit(solution)/shard_map/ppermute | solution.py:489
  58.5 5.1 %collective-permute-start.28 = (f32[64,512]{1,0:T(8,128)S(1)}, f32[64,512]{1,0:T(8,128)S(1)}, u32[]{:S(2)}, u32[]{:S(2)}) collective-permute-start(f32[64,512]{1,0:T(8,128)S(1)} %get-tuple-element.139), channel_id=1, source_target_pairs={{0,8},{1,2},{2,1},{3,4},{4,3},{5,6},{6,5},{7,15},{8,0},{9,10},{10,... | collective-permute-start | bytes 393224 | tf_op jit(solution)/shard_map/ppermute | solution.py:489
  63.9 5.6 %collective-permute-start.33 = (f32[64,512]{1,0:T(8,128)S(1)}, f32[64,512]{1,0:T(8,128)S(1)}, u32[]{:S(2)}, u32[]{:S(2)}) collective-permute-start(f32[64,512]{1,0:T(8,128)S(1)} %get-tuple-element.149), channel_id=1, source_target_pairs={{0,8},{1,9},{2,10},{3,11},{4,12},{5,13},{6,14},{7,15},{8,0},{9,1},... | collective-permute-start | bytes 393224 | tf_op jit(solution)/shard_map/ppermute | solution.py:489
  65.2 4.3 %collective-permute-start.34 = (f32[64,512]{1,0:T(8,128)S(1)}, f32[64,512]{1,0:T(8,128)S(1)}, u32[]{:S(2)}, u32[]{:S(2)}) collective-permute-start(f32[64,512]{1,0:T(8,128)S(1)} %get-tuple-element.150), channel_id=1, source_target_pairs={{0,1},{1,0},{2,3},{3,2},{4,5},{5,4},{6,7},{7,6},{8,16},{9,17},{10,... | collective-permute-start | bytes 393224 | tf_op jit(solution)/shard_map/ppermute | solution.py:489
  65.7 5.2 %collective-permute-start.32 = (f32[64,512]{1,0:T(8,128)S(1)}, f32[64,512]{1,0:T(8,128)S(1)}, u32[]{:S(2)}, u32[]{:S(2)}) collective-permute-start(f32[64,512]{1,0:T(8,128)S(1)} %get-tuple-element.148), channel_id=1, source_target_pairs={{0,8},{1,2},{2,1},{3,4},{4,3},{5,6},{6,5},{7,15},{8,0},{9,10},{10,... | collective-permute-start | bytes 393224 | tf_op jit(solution)/shard_map/ppermute | solution.py:489
  (12 other events, 42.9 us)

commit v3 on v2

v3 whole, which is shorter than its diff:
```python
import functools

import jax
import jax.numpy as jnp
import numpy as np
from jax import lax
from jax.experimental import pallas as pl
from jax.experimental.pallas import tpu as pltpu
from jax.sharding import PartitionSpec as P

center_value = 1.1
radius_value = 0.9
AXES = ("span", "stream")
STEPS = ((0,), (1, 2, 3))
AHEAD = 2
COARSE = (3, 2, 1, 0)
CHUNK = 4
VMEM_LIMIT = 16 * 1024 * 1024
f32 = jnp.float32
bf16 = jnp.bfloat16
i32 = jnp.int32


def chebyshev_weights():
    weights = []
    old = radius_value / center_value
    for _ in range(2):
        now = 1.0 / (2.0 * center_value / radius_value - old)
        weights.append((now * old, 2.0 * now / radius_value))
        old = now
    return weights


def directions(s, t, n_span, n_stream, choose):
    span_even, span_odd = choose((s & 1) == 0, 1, 0), choose((s & 1) == 0, 0, 1)
    stream_even, stream_odd = choose((t & 1) == 0, 3, 2), choose((t & 1) == 0, 2, 3)
    end_s = (s == 0) | (s == n_span - 1)
    ahead = (((t + 1) >> 1) & 1) == 0
    return (
        choose(ahead, stream_odd, span_even),
        choose(ahead, span_even, choose(end_s, stream_odd, span_odd)),
        choose(ahead | end_s, span_odd, stream_odd),
        stream_even,
    )


def exchanges(n_span, n_stream):
    steps = ((-1, 0), (1, 0), (0, -1), (0, 1))
    partners = [{} for _ in range(4)]
    for s in range(n_span):
        for t in range(n_stream):
            way = directions(
                np.int32(s), np.int32(t), n_span, n_stream, lambda c, a, b: int(a if c else b)
            )
            for number in range(4):
                other_s, other_t = s + steps[way[number]][0], t + steps[way[number]][1]
                if 0 <= other_s < n_span and 0 <= other_t < n_stream:
                    partners[number][s, t] = (other_s, other_t)
    result = []
    for found in partners:
        idle = [(s, t) for s in range(n_span) for t in range(n_stream) if (s, t) not in found]
        while idle:
            s, t = idle.pop(0)
            other = min(
                idle,
                key=lambda o: (o != (s, t ^ 1), o[0] != s, abs(o[0] - s) + abs(o[1] - t)),
                default=(s, t),
            )
            if other in idle:
                idle.remove(other)
            found[s, t], found[other] = other, (s, t)
        result.append(
            [(s * n_stream + t, o[0] * n_stream + o[1]) for (s, t), o in sorted(found.items())]
        )
    return result


def place_in_mesh():
    s, t = lax.axis_index("span"), lax.axis_index("stream")
    n_span, n_stream = lax.axis_size("span"), lax.axis_size("stream")
    ways = directions(s, t, n_span, n_stream, jnp.where)
    there = [
        jnp.where(
            way < 2,
            jnp.where(way == 0, s > 0, s < n_span - 1),
            jnp.where(way == 2, t > 0, t < n_stream - 1),
        )
        for way in ways
    ]
    return ways, there


def dot_nt(a, b):
    return lax.dot_general(a, b, (((1,), (1,)), ((), ())), preferred_element_type=f32)


def dot_nn(a, b):
    return lax.dot_general(a, b, (((1,), (0,)), ((), ())), preferred_element_type=f32)


def high_low(x):
    high = x.astype(bf16)
    return high, (x - high.astype(f32)).astype(bf16)


def stacked(x):
    return jnp.concatenate(high_low(x), axis=0)


def halves(x):
    rows = x.shape[0] // 2
    return x[:rows] + x[rows:]


def block(index, size):
    return pl.ds(pl.multiple_of(index * size, size), size)


class Table:
    def __init__(self, blocks, count, slots):
        self.blocks, self.count, self.slots = blocks, count, slots
        self.capacity = blocks * (count - 1) + CHUNK
        self.columns = 4 * slots
        self.home = self.columns + blocks * count
        self.counts = self.home + 5
        self.entries = self.counts + 5
        self.length = self.entries + 5 * self.capacity

    def direction(self, slot):
        if self.slots & (self.slots - 1) == 0:
            return slot >> (self.slots.bit_length() - 1)
        return lax.div(slot, self.slots)

    def code(self, which, row, slot):
        return (which << 16) | (row << 8) | slot


def pack(table, field, outs, size, slots):
    for buffer in range(4):
        for h in range(slots):
            source = table[buffer * slots + h]
            outs[buffer][:, h * size : (h + 1) * size] = field[:, block(source, size)]


def load_kernel(
    guess, lists, columns, groups, o0, o1, o2, o3, field, lists_out, columns_out, names, sems, *, size, slots
):
    copies = [
        pltpu.make_async_copy(source, target, sems.at[i])
        for i, (source, target) in enumerate(
            ((lists, lists_out), (guess, field), (groups, names), (columns, columns_out))
        )
    ]
    for copy in copies:
        copy.start()
    ways, _ = place_in_mesh()
    for copy in copies:
        copy.wait()
    rows = field.shape[0]
    for buffer, out in enumerate((o0, o1, o2, o3)):
        direction = ways[buffer]
        for h in range(slots):
            at = block(lists_out[0, direction * slots + h], size)
            out[0:rows, h * size : (h + 1) * size] = field[:, at]
            out[rows : rows + 8, h * size : (h + 1) * size] = jnp.broadcast_to(
                names[:, at].astype(f32), (8, size)
            )


def split_field(field, wide, size):
    rows, width = field.shape
    high, low = high_low(field[...])
    wide[0:rows, 0:width] = high
    wide[rows : 2 * rows, 0:width] = low
    wide[0 : 2 * rows, width : width + size] = jnp.zeros((2 * rows, size), bf16)


def local_rows(table, lay, matrix, wide, g, size, rows):
    parts = [wide[0:rows, g * size : (g + 1) * size]]
    for k in range(1, lay.count):
        parts.append(wide[0:rows, block(table[lay.columns + g * lay.count + k], size)])
    pieces = [matrix[g * lay.count + k] for k in range(lay.count)]
    return dot_nt(jnp.concatenate(parts, axis=1), jnp.concatenate(pieces, axis=1))


def local_block(table, lay, matrix, wide, g, size, rows):
    return halves(local_rows(table, lay, matrix, wide, g, size, 2 * rows))


def diagonal_row(matrix, same):
    return jnp.sum(jnp.where(same, matrix.astype(f32), 0.0), axis=0, keepdims=True)


def square_mask(size):
    return lax.broadcasted_iota(i32, (size, size), 0) == lax.broadcasted_iota(
        i32, (size, size), 1
    )


def build_table(lists, columns, table, lay):
    ways, there = place_in_mesh()
    for buffer in range(4):
        direction = ways[buffer]
        table[lay.home + direction] = jnp.where(there[buffer], buffer, 4)
        for h in range(lay.slots):
            table[buffer * lay.slots + h] = lists[0, direction * lay.slots + h]
    table[lay.home + 4] = 4
    for buffer in range(5):
        table[lay.counts + buffer] = 0
    for g in range(lay.blocks):
        table[lay.columns + g * lay.count] = columns[0, g]
        for k in range(1, lay.count):
            column = columns[k, g]
            table[lay.columns + g * lay.count + k] = jnp.minimum(column, lay.blocks)
            slot = jnp.maximum(column - lay.blocks, 0)
            direction = jnp.where(column < lay.blocks, 4, lay.direction(slot))
            buffer = table[lay.home + direction]
            found = table[lay.counts + buffer]
            table[lay.entries + buffer * lay.capacity + found] = lay.code(
                g * lay.count + k, g, slot - lay.direction(slot) * lay.slots
            )
            table[lay.counts + buffer] = found + 1
    for buffer in range(4):
        found = table[lay.counts + buffer]
        for i in range(CHUNK):
            table[lay.entries + buffer * lay.capacity + found + i] = lay.slots


def sweep_weights(weights, inverse):
    if weights is None:
        return None, inverse[0:1, :] / center_value
    return weights[0], weights[1] * inverse[0:1, :]


def begin_sweep(left, update, iterate, inverse, new, weights, mode, onehot=None):
    if mode == "restrict":
        new[...] = halves(dot_nt(stacked(left[...]), onehot[...]))
        return
    a, b = sweep_weights(weights, inverse)
    change = b * left[...] if a is None else a * update[...] + b * left[...]
    new[...] = iterate[...] + change if mode == "last" else change


def first_kernel(
    lists, columns, field, target, source, left, new, table, inverse, matrix, wide, right, sems, *, size, lay, parts
):
    per = matrix.shape[0] // parts
    copies = [
        pltpu.make_async_copy(
            source.at[pl.ds(i * per, per)], matrix.at[pl.ds(i * per, per)], sems.at[i]
        )
        for i in range(parts)
    ]
    copies.append(pltpu.make_async_copy(target, right, sems.at[parts]))
    copies[parts].start()
    for copy in copies[:AHEAD]:
        copy.start()
    split_field(field, wide, size)
    build_table(lists, columns, table, lay)
    copies[parts].wait()
    same = square_mask(size)
    for g in range(lay.blocks):
        if g % (lay.blocks // parts) == 0:
            part = g // (lay.blocks // parts)
            copies[part].wait()
            if part + AHEAD < parts:
                copies[part + AHEAD].start()
        at = slice(g * size, (g + 1) * size)
        left[:, at] = right[:, at] - local_block(table, lay, matrix, wide, g, size, left.shape[0])
        inverse[:, at] = jnp.broadcast_to(
            1.0 / diagonal_row(matrix[g * lay.count], same), (8, size)
        )
    begin_sweep(left, None, None, inverse, new, None, "plain")


def local_kernel(table, update, residual, iterate, inverse, matrix, *refs, size, lay, weights, mode):
    refs = list(refs)
    onehot = refs.pop(0) if mode == "restrict" else None
    left, new, iterate_out, wide = refs
    split_field(update, wide, size)
    for g in range(lay.blocks):
        at = slice(g * size, (g + 1) * size)
        left[:, at] = residual[:, at] - local_block(table, lay, matrix, wide, g, size, left.shape[0])
    iterate_out[...] = iterate[...] + update[...]
    begin_sweep(left, update, iterate_out, inverse, new, weights, mode, onehot)


def local_and_coarse_kernel(
    table, update, residual, iterate, inverse, matrix, groups, coarse, h0, h1, h2, h3,
    left, new, iterate_out, onehot, names, coarse_high, coarse_low, coarse_inverse, wide, brought, cells, sems, *, size, lay, weights,
):
    copies = [
        pltpu.make_async_copy(coarse, brought, sems.at[0]),
        pltpu.make_async_copy(groups, cells, sems.at[1]),
    ]
    for copy in copies:
        copy.start()
    local_kernel(
        table, update, residual, iterate, inverse, matrix, left, new, iterate_out, wide,
        size=size, lay=lay, weights=weights, mode="plain",
    )
    width = lay.slots * size
    rows = update.shape[0]
    number = lax.broadcasted_iota(i32, (size, width), 0).astype(f32)
    for buffer, received in enumerate((h0, h1, h2, h3)):
        names[:, buffer * width : (buffer + 1) * width] = jnp.where(
            number == received[rows : rows + 1, :], 1.0, 0.0
        ).astype(bf16)
    for copy in copies:
        copy.wait()
    onehot[...] = jnp.where(
        lax.broadcasted_iota(i32, onehot.shape, 0) == cells[...], 1.0, 0.0
    ).astype(bf16)
    coarse_inverse[...] = jnp.broadcast_to(
        1.0 / diagonal_row(brought[0], square_mask(size)), (8, size)
    )
    ways, there = place_in_mesh()
    for k in range(5):
        if k == 0:
            piece = brought[0]
        else:
            piece = jnp.where(there[k - 1], brought[1 + ways[k - 1]], 0.0)
        high, low = high_low(piece)
        coarse_high[:, k * size : (k + 1) * size] = high
        coarse_low[:, k * size : (k + 1) * size] = low


def put_halo(wide, place, x, size):
    rows, width = x.shape
    start = place * (width + size)
    high, low = high_low(x)
    wide[0:rows, start : start + width] = high
    wide[rows : 2 * rows, start : start + width] = low
    wide[:, start + width : start + width + size] = jnp.zeros((2 * rows, size), bf16)


def put_halos(wide, halos, buffers, names, rows, lay, size):
    for place, (buffer, received) in enumerate(zip(buffers, halos)):
        x = received[0:rows, :]
        if names is not None:
            width = lay.slots * size
            chosen = names[:, buffer * width : (buffer + 1) * width]
            x = halves(dot_nn(stacked(x), chosen))
        put_halo(wide, place, x, size)


def entry_product(code, matrix, wide, place, lay, size):
    which, row, slot = code >> 16, (code >> 8) & 255, code & 255
    at = block(place * (lay.slots + 1) + slot, size)
    return block(row, size), halves(dot_nt(wide[:, at], matrix[which]))


def for_received(table, lay, buffers, matrix, wide, size, use):
    def group(members):
        use(
            [
                entry_product(
                    table[lay.entries + buffer * lay.capacity + i], matrix, wide, place, lay, size
                )
                for place, buffer, i in members
            ]
        )

    group([(p, b, i) for p, b in enumerate(buffers) for i in range(CHUNK)])
    for place, buffer in enumerate(buffers):

        def more(c, carry, place=place, buffer=buffer):
            group([(place, buffer, c * CHUNK + i) for i in range(CHUNK)])
            return carry

        chunks = (table[lay.counts + buffer] + CHUNK - 1) // CHUNK
        lax.fori_loop(1, chunks, more, 0)


def received_kernel(table, left_in, new_in, inverse, matrix, *refs, size, lay, weights, mode, buffers, final):
    refs = list(refs)
    halos, refs = refs[: len(buffers)], refs[len(buffers) :]
    rows = left_in.shape[0]
    names = refs.pop(0) if mode == "spread" else None
    if mode == "restrict":
        onehot, coarse_inverse = refs[:2]
        refs = refs[2:]
    wide, scaled = refs[-2:]
    left, new = refs[:2]
    if mode == "last" and final:
        new = refs[0]
        new[...] = new_in[...]
    put_halos(wide, halos, buffers, names, rows, lay, size)
    if mode != "restrict":
        scaled[0:1, :] = sweep_weights(weights, inverse)[1]

    def use(found):
        for at, product in found:
            if mode != "last":
                left[:, at] = left[:, at] - product
            if mode != "restrict":
                new[:, at] = new[:, at] - scaled[0:1, at] * product
        if mode == "restrict":
            new[...] = new[...] - sum(
                halves(dot_nt(stacked(product), onehot[:, at])) for at, product in found
            )

    for_received(table, lay, buffers, matrix, wide, size, use)
    if not final or mode == "last":
        return
    if mode == "restrict":
        refs[2][...] = coarse_inverse[0:1, :] * new[...] / center_value
    else:
        pack(table, new, refs[2:6], size, lay.slots)


def coarse_kernel(
    h0, h1, h2, h3, residual, update, iterate, coarse_high, coarse_low, coarse_inverse, *outs, weights, last
):
    c = update[...]
    rows = c.shape[0]
    received = dict(zip(COARSE, (h0, h1, h2, h3)))
    high, low = high_low(jnp.concatenate([c] + [received[b][...] for b in range(4)], axis=1))
    product = halves(dot_nt(jnp.concatenate([high, low], axis=0), coarse_high[...]))
    left = residual[...] - (product + dot_nt(high, coarse_low[...]))
    new = weights[0] * c + weights[1] * coarse_inverse[0:1, :] * left
    outs[0][...] = iterate[...] + new
    if not last:
        outs[1][...] = left
        outs[2][...] = new


def local_and_spread_kernel(
    table, update, residual, iterate, inverse, matrix, onehot, left, new, iterate_out, high, low, wide, *, size, lay, weights
):
    local_kernel(
        table, update, residual, iterate, inverse, matrix, left, new, iterate_out, wide,
        size=size, lay=lay, weights=weights, mode="plain",
    )
    width = onehot.shape[1]
    wide[0:size, 0:width] = onehot[...]
    wide[0:size, width : width + size] = jnp.zeros((size, size), bf16)
    for g in range(lay.blocks):
        at = slice(g * size, (g + 1) * size)
        high[:, at], low[:, at] = high_low(
            local_rows(table, lay, matrix, wide, g, size, size)
        )


def spread_kernel(
    table, correction, onehot, iterate, leftover, inverse, spread_high, spread_low, left, new, second, correction_out, *, size, lay
):
    rows = correction.shape[0]
    both = stacked(correction[...])
    second[...] = iterate[...] + halves(dot_nn(both, onehot[...]))
    product = halves(dot_nn(both, spread_high[...])) + dot_nn(both[:rows], spread_low[...])
    left[...] = leftover[...] - product
    begin_sweep(left, None, None, inverse, new, None, "plain")
    correction_out[...] = correction[...]


def local_program(
    right_side, start_guess, fine_matrix, fine_columns, send_lists, aggregates, coarse_matrix
):
    perms = exchanges(lax.axis_size("span"), lax.axis_size("stream"))
    rows, width = right_side.shape
    blocks, count, size, _ = fine_matrix.shape
    slots = send_lists.shape[1] // 4
    halo_width = slots * size
    lay = Table(blocks, count, slots)
    groups = aggregates.reshape(1, width)
    stored = fine_matrix.reshape(blocks * count, size, size)
    coarse = coarse_matrix.reshape(coarse_matrix.shape[1:])
    weights = chebyshev_weights()
    parts = 4 if blocks % 4 == 0 else 1

    spaces = {
        "v": pl.BlockSpec(memory_space=pltpu.VMEM),
        "s": pl.BlockSpec(memory_space=pltpu.SMEM),
        "h": pl.BlockSpec(memory_space=pltpu.HBM),
    }

    def call(kernel, ins, outs, scratch=(), where="", kept="", aliases=None, flops=0, **named):
        where = where + "v" * (len(ins) - len(where))
        kept = kept + "v" * (len(outs) - len(kept))
        fixed = {"h": pltpu.HBM, "V": pltpu.VMEM}
        ins = [
            pltpu.with_memory_space_constraint(x, fixed[c]) if c in fixed else x
            for x, c in zip(ins, where)
        ]
        forms = {
            "v": jax.ShapeDtypeStruct,
            "V": pltpu.MemorySpace.VMEM,
            "s": pltpu.MemorySpace.SMEM,
        }
        return pl.pallas_call(
            functools.partial(kernel, **named),
            out_shape=[forms[c](shape, kind) for c, (shape, kind) in zip(kept, outs)],
            in_specs=[spaces[c.lower()] for c in where],
            out_specs=[spaces[c.lower()] for c in kept],
            scratch_shapes=list(scratch),
            input_output_aliases=aliases or {},
            compiler_params=pltpu.CompilerParams(vmem_limit_bytes=VMEM_LIMIT),
            cost_estimate=pl.CostEstimate(
                flops=flops, bytes_accessed=4 * 1024 * 1024, transcendentals=0
            ),
        )(*ins)

    def exchange(payloads):
        return [lax.ppermute(x, AXES, perm) for x, perm in zip(payloads, perms)]

    field = ((rows, width), f32)
    halo = ((rows, halo_width), f32)
    small = ((rows, size), f32)
    wide_local = pltpu.VMEM((2 * rows, width + size), bf16)
    wide_spread = pltpu.VMEM((max(2 * rows, size), width + size), bf16)
    flops = 2 * 2 * rows * blocks * count * size * size
    dims = {"size": size, "lay": lay}

    def received(halos, left, new, weight, mode="plain", extra=()):
        for step, buffers in enumerate(STEPS):
            final = step == len(STEPS) - 1
            outs, kept = [field, small if mode == "restrict" else field], "VV"
            aliases = {1: 0, 2: 1}
            if mode == "last" and final:
                outs, kept, aliases = [field], "v", None
            elif mode == "restrict" and final:
                outs.append(small)
            elif final:
                outs += [halo] * 4
            result = call(
                received_kernel,
                [table, left, new, inverse, matrix] + [halos[b] for b in buffers] + list(extra),
                outs,
                [
                    pltpu.VMEM((2 * rows, len(buffers) * (halo_width + size)), bf16),
                    pltpu.VMEM((8, width), f32),
                ],
                "sVV", kept, aliases, flops=flops * len(buffers) // 20,
                weights=weight, mode=mode, buffers=buffers, final=final, **dims,
            )
            left, new = result[0], result[1] if len(result) > 1 else None
        return result

    def local(update, residual, iterate, weight, mode="plain", extra=()):
        return call(
            local_kernel, [table, update, residual, iterate, inverse, matrix] + list(extra),
            [field, small if mode == "restrict" else field, field],
            [wide_local], "s", "VV", flops=flops, weights=weight, mode=mode, **dims,
        )

    *payloads, guess, lists, columns = call(
        load_kernel,
        [start_guess, send_lists, fine_columns.T, groups],
        [((rows + 8, halo_width), f32)] * 4
        + [field, (send_lists.shape, i32), (fine_columns.shape[::-1], i32)],
        [pltpu.VMEM((1, width), i32), pltpu.SemaphoreType.DMA((4,))],
        "hhhh", "vvvvvss", size=size, slots=slots,
    )
    first_halos = halos = exchange(payloads)
    left, new, table, inverse, matrix = call(
        first_kernel,
        [lists, columns, guess, right_side, stored],
        [field, field, ((lay.length,), i32), ((8, width), f32), (stored.shape, bf16)],
        [wide_local, pltpu.VMEM(*field), pltpu.SemaphoreType.DMA((parts + 1,))],
        "ssvhh", "VVs", flops=flops, parts=parts, **dims,
    )
    residual, update, *payloads = received(halos, left, new, None)
    halos = exchange(payloads)
    left, new, iterate, onehot, names, coarse_high, coarse_low, coarse_inverse = call(
        local_and_coarse_kernel,
        [table, update, residual, guess, inverse, matrix, groups, coarse] + first_halos,
        [
            field,
            field,
            field,
            ((size, width), bf16),
            ((size, 4 * halo_width), bf16),
            ((size, 5 * size), bf16),
            ((size, 5 * size), bf16),
            ((8, size), f32),
        ],
        [
            wide_local,
            pltpu.VMEM(coarse.shape, f32),
            pltpu.VMEM((1, width), i32),
            pltpu.SemaphoreType.DMA((2,)),
        ],
        "svvvvvhh", "VV", flops=flops, weights=weights[0], **dims,
    )
    residual, update, *payloads = received(halos, left, new, weights[0])
    halos = exchange(payloads)
    left, new, iterate, spread_high, spread_low = call(
        local_and_spread_kernel, [table, update, residual, iterate, inverse, matrix, onehot],
        [field, field, field, ((size, width), bf16), ((size, width), bf16)],
        [wide_spread], "s", "VV", flops=flops, weights=weights[1], **dims,
    )
    residual, update, *payloads = received(halos, left, new, weights[1])
    halos = exchange(payloads)
    left, new, iterate = local(update, residual, iterate, None, "restrict", (onehot,))
    leftover, coarse_left, c = received(
        halos, left, new, None, "restrict", (onehot, coarse_inverse)
    )
    correction = c
    for i, weight in enumerate(weights):
        halos = exchange([c] * 4)
        result = call(
            coarse_kernel,
            [halos[b] for b in COARSE]
            + [coarse_left, c, correction, coarse_high, coarse_low, coarse_inverse],
            [small] if i == 1 else [small] * 3, weights=weight, last=i == 1,
        )
        correction = result[0]
        if i == 0:
            coarse_left, c = result[1:]
    halos = exchange([correction] * 4)
    left, new, iterate, correction_out = call(
        spread_kernel,
        [table, correction, onehot, iterate, leftover, inverse, spread_high, spread_low],
        [field, field, field, small], (), "s", "VV", flops=flops, **dims,
    )
    residual, update, *payloads = received(halos, left, new, None, "spread", (names,))
    halos = exchange(payloads)
    left, new, iterate = local(update, residual, iterate, weights[0])
    residual, update, *payloads = received(halos, left, new, weights[0])
    halos = exchange(payloads)
    left, new, iterate = local(update, residual, iterate, weights[1], "last")
    result = received(halos, left, new, weights[1], "last")
    return (result[0], correction_out)


def solution(mesh):
    placed = (
        P(None, AXES),
        P(None, AXES),
        P(AXES, None, None, None),
        P(AXES, None),
        P(AXES, None),
        P(AXES),
        P(AXES, None, None, None),
    )
    return jax.shard_map(
        local_program,
        mesh=mesh,
        in_specs=placed,
        out_specs=(P(None, AXES), P(None, AXES)),
        check_vma=False,
    )
```

time: 72.1 us -> 66.5 us (0.922)
  waiting for transfers between devices: 17.2 us -> 6.52 us
  starting transfers between devices: 32.9 us -> 36.6 us
  Pallas kernels: 21 us -> 21.8 us
    ppermute x36, waiting for transfers between devices: 17.2 us -> 6.52 us  [exchange(): return [lax.ppermute(x, AXES, perm) for x, perm in zip(payloads, perms)]]
    ppermute x36, starting transfers between devices: 32.9 us -> 36.6 us  [exchange(): return [lax.ppermute(x, AXES, perm) for x, perm in zip(payloads, perms)]]
    pallas_call x24, Pallas kernels: 21 us -> 21.8 us  [call(): pl.pallas_call(functools.partial(kernel, **named), out_shape=[forms[c](sh...]
  transfers between devices with their start and end apart: 36 -> 36, of which waited for: 13 -> 12; matrix products, arithmetic and copies ran while one was open for 0% -> 0% of each run, Pallas kernels for 22% -> 23%
where the time goes in v3:
time: 66.5 us; the launch traced here: 65.8 us
  starting transfers between devices  36.6 us (55%)
  Pallas kernels  21.8 us (33%)
  waiting for transfers between devices  6.52 us (10%)
  between operations  0.9 us (1%)
    ppermute x36, starting transfers between devices, exchange(): return [lax.ppermute(x, AXES, perm) for x, perm in zip(payloads, perms)]  36.6 us
    pallas_call x24, Pallas kernels, call(): pl.pallas_call(functools.partial(kernel, **named), out_shape=[forms[c](sh...  21.8 us
    ppermute x36, waiting for transfers between devices, exchange(): return [lax.ppermute(x, AXES, perm) for x, perm in zip(payloads, perms)]  6.52 us
  transfers between devices with their start and end apart: 36, of which 12 were waited for; matrix products, arithmetic and copies ran while one was open for 0% of the time, Pallas kernels for 23%

profile of v3, /device:TPU:0, one launch (start us, length us, event | category | flops | bytes accessed | tf_op | source)
XLA Modules:
  0.0 65.8 jit_solution(3846891630643438296)
XLA Ops:
  0.6 1.2 %shard_map.86 = (f32[72,512]{1,0:T(8,128)S(1)}, f32[72,512]{1,0:T(8,128)S(1)}, f32[72,512]{1,0:T(8,128)S(1)}, f32[72,512]{1,0:T(8,128)S(1)}, f32[64,2048]{1,0:T(...) custom-call(f32[64,2048]{1,0:T(8,128)} %guess.1, s32[1,16]{1,0:T(1,128)} %lists.1, s32[5,16]{1,0:T(8,128)} %bitcast.8, ...), custom_call_target="tpu_custom_call" | custom-call | bytes 4194304 | tf_op jit(solution)/shard_map/pallas_call | solution.py:491
  1.8 3.4 %collective-permute-start = (f32[72,512]{1,0:T(8,128)S(1)}, f32[72,512]{1,0:T(8,128)S(1)}, u32[]{:S(2)}, u32[]{:S(2)}) collective-permute-start(f32[72,512]{1,0:T(8,128)S(1)} %get-tuple-element.97), channel_id=1, source_target_pairs={{0,7},{1,9},{2,10},{3,4},{4,3},{5,13},{6,14},{7,0},{8,15},{9,1},{1... | collective-permute-start | bytes 442376 | tf_op jit(solution)/shard_map/ppermute | solution.py:505
  5.2 1.6 %collective-permute-start.1 = (f32[72,512]{1,0:T(8,128)S(1)}, f32[72,512]{1,0:T(8,128)S(1)}, u32[]{:S(2)}, u32[]{:S(2)}) collective-permute-start(f32[72,512]{1,0:T(8,128)S(1)} %get-tuple-element.100), channel_id=1, source_target_pairs={{0,8},{1,2},{2,1},{3,11},{4,12},{5,6},{6,5},{7,15},{8,0},{9,17},{1... | collective-permute-start | bytes 442376 | tf_op jit(solution)/shard_map/ppermute | solution.py:505
  7.3 3.2 %shard_map.87 = (f32[64,2048]{1,0:T(8,128)S(1)}, f32[64,2048]{1,0:T(8,128)S(1)}, s32[446]{0:T(512)S(4)}, f32[8,2048]{1,0:T(8,128)S(1)}, bf16[80,128,128]{2,1,0:T(8,128)(2,1)S(1)}) custom-call(s32[1,16]{1,0:T(1,128)S(4)} %get-tuple-element.89.lists, s32[5,16]{1,0:T(8,128)S(4)} %get-tuple-element.90.columns, f32[64,2048]{1,0:T(8,128)S(1)} %get-tuple-element.91.field.iterate, ...), custom_call_target="tpu_custom_call" | custom-call | flops 335544320 | bytes 4194304 | tf_op jit(solution)/shard_map/pallas_call | solution.py:491
  11.4 1.2 %collective-permute-start.4 = (f32[64,512]{1,0:T(8,128)S(1)}, f32[64,512]{1,0:T(8,128)S(1)}, u32[]{:S(2)}, u32[]{:S(2)}) collective-permute-start(f32[64,512]{1,0:T(8,128)S(1)} %get-tuple-element.107), channel_id=1, source_target_pairs={{0,7},{1,9},{2,10},{3,4},{4,3},{5,13},{6,14},{7,0},{8,15},{9,1},{1... | collective-permute-start | bytes 393224 | tf_op jit(solution)/shard_map/ppermute | solution.py:505
  12.6 2.3 %collective-permute-start.5 = (f32[64,512]{1,0:T(8,128)S(1)}, f32[64,512]{1,0:T(8,128)S(1)}, u32[]{:S(2)}, u32[]{:S(2)}) collective-permute-start(f32[64,512]{1,0:T(8,128)S(1)} %get-tuple-element.110), channel_id=1, source_target_pairs={{0,8},{1,2},{2,1},{3,11},{4,12},{5,6},{6,5},{7,15},{8,0},{9,17},{1... | collective-permute-start | bytes 393224 | tf_op jit(solution)/shard_map/ppermute | solution.py:505
  15.4 2.2 %shard_map.90 = (f32[64,2048]{1,0:T(8,128)S(1)}, f32[64,2048]{1,0:T(8,128)S(1)}, f32[64,2048]{1,0:T(8,128)S(1)}, bf16[128,2048]{1,0:T(8,128)(2,1)S(1)}, bf16[128...) custom-call(s32[446]{0:T(512)S(4)} %get-tuple-element.92.table, ...), custom_call_target="tpu_custom_call" | custom-call | flops 335544320 | bytes 4194304 | tf_op jit(solution)/shard_map/pallas_call | solution.py:491
  18.8 1.6 %collective-permute-start.8 = (f32[64,512]{1,0:T(8,128)S(1)}, f32[64,512]{1,0:T(8,128)S(1)}, u32[]{:S(2)}, u32[]{:S(2)}) collective-permute-start(f32[64,512]{1,0:T(8,128)S(1)} %get-tuple-element.119), channel_id=1, source_target_pairs={{0,7},{1,9},{2,10},{3,4},{4,3},{5,13},{6,14},{7,0},{8,15},{9,1},{1... | collective-permute-start | bytes 393224 | tf_op jit(solution)/shard_map/ppermute | solution.py:505
  20.4 2.1 %collective-permute-start.9 = (f32[64,512]{1,0:T(8,128)S(1)}, f32[64,512]{1,0:T(8,128)S(1)}, u32[]{:S(2)}, u32[]{:S(2)}) collective-permute-start(f32[64,512]{1,0:T(8,128)S(1)} %get-tuple-element.122), channel_id=1, source_target_pairs={{0,8},{1,2},{2,1},{3,11},{4,12},{5,6},{6,5},{7,15},{8,0},{9,17},{1... | collective-permute-start | bytes 393224 | tf_op jit(solution)/shard_map/ppermute | solution.py:505
  23.0 2.1 %shard_map.93 = (f32[64,2048]{1,0:T(8,128)S(1)}, f32[64,2048]{1,0:T(8,128)S(1)}, f32[64,2048]{1,0:T(8,128)S(1)}, bf16[128,2048]{1,0:T(8,128)(2,1)S(1)}, bf16[128,2048]{1,0:T(8,128)(2,1)S(1)}) custom-call(s32[446]{0:T(512)S(4)} %get-tuple-element.92.table, f32[64,2048]{1,0:T(8,128)S(1)} %get-tuple-element.113.update, ...), custom_call_target="tpu_custom_call" | custom-call | flops 335544320 | bytes 4194304 | tf_op jit(solution)/shard_map/pallas_call | solution.py:491
  26.0 1.5 %collective-permute-start.12 = (f32[64,512]{1,0:T(8,128)S(1)}, f32[64,512]{1,0:T(8,128)S(1)}, u32[]{:S(2)}, u32[]{:S(2)}) collective-permute-start(f32[64,512]{1,0:T(8,128)S(1)} %get-tuple-element.130), channel_id=1, source_target_pairs={{0,7},{1,9},{2,10},{3,4},{4,3},{5,13},{6,14},{7,0},{8,15},{9,1},{1... | collective-permute-start | bytes 393224 | tf_op jit(solution)/shard_map/ppermute | solution.py:505
  27.5 2.1 %collective-permute-start.13 = (f32[64,512]{1,0:T(8,128)S(1)}, f32[64,512]{1,0:T(8,128)S(1)}, u32[]{:S(2)}, u32[]{:S(2)}) collective-permute-start(f32[64,512]{1,0:T(8,128)S(1)} %get-tuple-element.134), channel_id=1, source_target_pairs={{0,8},{1,2},{2,1},{3,11},{4,12},{5,6},{6,5},{7,15},{8,0},{9,17},{1... | collective-permute-start | bytes 393224 | tf_op jit(solution)/shard_map/ppermute | solution.py:505
  30.1 1.5 %shard_map.96 = (f32[64,2048]{1,0:T(8,128)S(1)}, f32[64,128]{1,0:T(8,128)S(1)}, f32[64,2048]{1,0:T(8,128)S(1)}) custom-call(s32[446]{0:T(512)S(4)} %get-tuple-element.92.table, f32[64,2048]{1,0:T(8,128)S(1)} %get-tuple-element.125.update, f32[64,2048]{1,0:T(8,128)S(1)} %get-tuple-element.126.residual, f32[64,2048]{1,0:T(8,128)S(1)} %get-tuple-element.127.iterate, ...), custom_call_target="tpu_custom_call" | custom-call | flops 335544320 | bytes 4194304 | tf_op jit(solution)/shard_map/pallas_call | solution.py:491
  33.4 1.5 %collective-permute-start.19 = (f32[64,128]{1,0:T(8,128)S(1)}, f32[64,128]{1,0:T(8,128)S(1)}, u32[]{:S(2)}, u32[]{:S(2)}) collective-permute-start(f32[64,128]{1,0:T(8,128)S(1)} %get-tuple-element.137.update.iterate), channel_id=1, source_target_pairs={{0,7},{1,9},{2,10},{3,4},{4,3},{5,13},{6,14},{7,0},{8,15},{9,1},{1... | collective-permute-start | bytes 98312 | tf_op jit(solution)/shard_map/ppermute | solution.py:505
  34.8 2.1 %collective-permute-start.18 = (f32[64,128]{1,0:T(8,128)S(1)}, f32[64,128]{1,0:T(8,128)S(1)}, u32[]{:S(2)}, u32[]{:S(2)}) collective-permute-start(f32[64,128]{1,0:T(8,128)S(1)} %get-tuple-element.137.update.iterate), channel_id=1, source_target_pairs={{0,8},{1,2},{2,1},{3,11},{4,12},{5,6},{6,5},{7,15},{8,0},{9,17},{1... | collective-permute-start | bytes 98312 | tf_op jit(solution)/shard_map/ppermute | solution.py:505
  39.5 2.1 %collective-permute-start.22 = (f32[64,128]{1,0:T(8,128)S(1)}, f32[64,128]{1,0:T(8,128)S(1)}, u32[]{:S(2)}, u32[]{:S(2)}) collective-permute-start(f32[64,128]{1,0:T(8,128)S(1)} %get-tuple-element.141.update), channel_id=1, source_target_pairs={{0,8},{1,2},{2,1},{3,11},{4,12},{5,6},{6,5},{7,15},{8,0},{9,17},{1... | collective-permute-start | bytes 98312 | tf_op jit(solution)/shard_map/ppermute | solution.py:505
  44.1 1.2 %collective-permute-start.24 = (f32[64,128]{1,0:T(8,128)S(1)}, f32[64,128]{1,0:T(8,128)S(1)}, u32[]{:S(2)}, u32[]{:S(2)}) collective-permute-start(f32[64,128]{1,0:T(8,128)S(1)} %shard_map.100.correction), channel_id=1, source_target_pairs={{0,7},{1,9},{2,10},{3,4},{4,3},{5,13},{6,14},{7,0},{8,15},{9,1},{1... | collective-permute-start | bytes 98312 | tf_op jit(solution)/shard_map/ppermute | solution.py:505
  46.3 2.8 %collective-permute-start.25 = (f32[64,128]{1,0:T(8,128)S(1)}, f32[64,128]{1,0:T(8,128)S(1)}, u32[]{:S(2)}, u32[]{:S(2)}) collective-permute-start(f32[64,128]{1,0:T(8,128)S(1)} %shard_map.100.correction), channel_id=1, source_target_pairs={{0,8},{1,2},{2,1},{3,11},{4,12},{5,6},{6,5},{7,15},{8,0},{9,17},{1... | collective-permute-start | bytes 98312 | tf_op jit(solution)/shard_map/ppermute | solution.py:505
  52.5 1.7 %collective-permute-start.29 = (f32[64,512]{1,0:T(8,128)S(1)}, f32[64,512]{1,0:T(8,128)S(1)}, u32[]{:S(2)}, u32[]{:S(2)}) collective-permute-start(f32[64,512]{1,0:T(8,128)S(1)} %get-tuple-element.161), channel_id=1, source_target_pairs={{0,8},{1,2},{2,1},{3,11},{4,12},{5,6},{6,5},{7,15},{8,0},{9,17},{1... | collective-permute-start | bytes 393224 | tf_op jit(solution)/shard_map/ppermute | solution.py:505
  54.7 1.2 %shard_map.104 = (f32[64,2048]{1,0:T(8,128)S(1)}, f32[64,2048]{1,0:T(8,128)S(1)}, f32[64,2048]{1,0:T(8,128)S(1)}) custom-call(s32[446]{0:T(512)S(4)} %get-tuple-element.92.table, f32[64,2048]{1,0:T(8,128)S(1)} %get-tuple-element.153.update, f32[64,2048]{1,0:T(8,128)S(1)} %get-tuple-element.154.residual, f32[64,2048]{1,0:T(8,128)S(1)} %get-tuple-element.155.iterate, ...), custom_call_target="tpu_custom_call" | custom-call | flops 335544320 | bytes 4194304 | tf_op jit(solution)/shard_map/pallas_call | solution.py:491
  55.9 2.1 %collective-permute-done.28.refs_0_ = f32[64,512]{1,0:T(8,128)S(1)} collective-permute-done((f32[64,512]{1,0:T(8,128)S(1)}, f32[64,512]{1,0:T(8,128)S(1)}, u32[]{:S(2)}, u32[]{:S(2)}) %collective-permute-start.28) | collective-permute-done | bytes 131104 | tf_op jit(solution)/shard_map/ppermute | solution.py:505
  59.5 2.0 %collective-permute-start.33 = (f32[64,512]{1,0:T(8,128)S(1)}, f32[64,512]{1,0:T(8,128)S(1)}, u32[]{:S(2)}, u32[]{:S(2)}) collective-permute-start(f32[64,512]{1,0:T(8,128)S(1)} %get-tuple-element.172), channel_id=1, source_target_pairs={{0,8},{1,2},{2,1},{3,11},{4,12},{5,6},{6,5},{7,15},{8,0},{9,17},{1... | collective-permute-start | bytes 393224 | tf_op jit(solution)/shard_map/ppermute | solution.py:505
  62.0 1.9 %shard_map.107 = (f32[64,2048]{1,0:T(8,128)S(1)}, f32[64,2048]{1,0:T(8,128)S(1)}, f32[64,2048]{1,0:T(8,128)}) custom-call(s32[446]{0:T(512)S(4)} %get-tuple-element.92.table, f32[64,2048]{1,0:T(8,128)S(1)} %get-tuple-element.164.update, f32[64,2048]{1,0:T(8,128)S(1)} %get-tuple-element.165.residual, f32[64,2048]{1,0:T(8,128)S(1)} %get-tuple-element.166.iterate, ...), custom_call_target="tpu_custom_call" | custom-call | flops 335544320 | bytes 4194304 | tf_op jit(solution)/shard_map/pallas_call | solution.py:491
  64.5 1.3 %shard_map.109 = f32[64,2048]{1,0:T(8,128)} custom-call(s32[446]{0:T(512)S(4)} %get-tuple-element.92.table, f32[64,2048]{1,0:T(8,128)S(1)} %get-tuple-element.170.left_in, f32[64,2048]{1,0:T(8,128)S(1)} %get-tuple-element.171.new_in, f32[8,2048]{1,0:T(8,128)S(1)} %get-tuple-element.95.inverse, bf16[80,128,128]{2,1,0:T(8,128)(2,1)S(1)} %get-tuple-element.96.matrix, ...), custom_call_target="tpu_custom_call" | custom-call | flops 50331648 | bytes 4194304 | tf_op jit(solution)/shard_map/pallas_call | solution.py:491
  (72 shorter events, 19.2 us)
Async XLA Ops:
  1.8 8.7 %collective-permute-start = (f32[72,512]{1,0:T(8,128)S(1)}, f32[72,512]{1,0:T(8,128)S(1)}, u32[]{:S(2)}, u32[]{:S(2)}) collective-permute-start(f32[72,512]{1,0:T(8,128)S(1)} %get-tuple-element.97), channel_id=1, source_target_pairs={{0,7},{1,9},{2,10},{3,4},{4,3},{5,13},{6,14},{7,0},{8,15},{9,1},{1... | collective-permute-start | bytes 442376 | tf_op jit(solution)/shard_map/ppermute | solution.py:505
  5.2 5.6 %collective-permute-start.1 = (f32[72,512]{1,0:T(8,128)S(1)}, f32[72,512]{1,0:T(8,128)S(1)}, u32[]{:S(2)}, u32[]{:S(2)}) collective-permute-start(f32[72,512]{1,0:T(8,128)S(1)} %get-tuple-element.100), channel_id=1, source_target_pairs={{0,8},{1,2},{2,1},{3,11},{4,12},{5,6},{6,5},{7,15},{8,0},{9,17},{1... | collective-permute-start | bytes 442376 | tf_op jit(solution)/shard_map/ppermute | solution.py:505
  6.8 4.0 %collective-permute-start.2 = (f32[72,512]{1,0:T(8,128)S(1)}, f32[72,512]{1,0:T(8,128)S(1)}, u32[]{:S(2)}, u32[]{:S(2)}) collective-permute-start(f32[72,512]{1,0:T(8,128)S(1)} %get-tuple-element.101), channel_id=1, source_target_pairs={{0,1},{1,0},{2,3},{3,2},{4,5},{5,4},{6,7},{7,6},{8,16},{9,10},{10,... | collective-permute-start | bytes 442376 | tf_op jit(solution)/shard_map/ppermute | solution.py:505
  6.8 4.0 %collective-permute-start.3 = (f32[72,512]{1,0:T(8,128)S(1)}, f32[72,512]{1,0:T(8,128)S(1)}, u32[]{:S(2)}, u32[]{:S(2)}) collective-permute-start(f32[72,512]{1,0:T(8,128)S(1)} %get-tuple-element.102), channel_id=1, source_target_pairs={{0,1},{1,0},{2,3},{3,2},{4,5},{5,4},{6,7},{7,6},{8,9},{9,8},{10,11... | collective-permute-start | bytes 442376 | tf_op jit(solution)/shard_map/ppermute | solution.py:505
  11.4 6.2 %collective-permute-start.4 = (f32[64,512]{1,0:T(8,128)S(1)}, f32[64,512]{1,0:T(8,128)S(1)}, u32[]{:S(2)}, u32[]{:S(2)}) collective-permute-start(f32[64,512]{1,0:T(8,128)S(1)} %get-tuple-element.107), channel_id=1, source_target_pairs={{0,7},{1,9},{2,10},{3,4},{4,3},{5,13},{6,14},{7,0},{8,15},{9,1},{1... | collective-permute-start | bytes 393224 | tf_op jit(solution)/shard_map/ppermute | solution.py:505
  12.6 5.7 %collective-permute-start.5 = (f32[64,512]{1,0:T(8,128)S(1)}, f32[64,512]{1,0:T(8,128)S(1)}, u32[]{:S(2)}, u32[]{:S(2)}) collective-permute-start(f32[64,512]{1,0:T(8,128)S(1)} %get-tuple-element.110), channel_id=1, source_target_pairs={{0,8},{1,2},{2,1},{3,11},{4,12},{5,6},{6,5},{7,15},{8,0},{9,17},{1... | collective-permute-start | bytes 393224 | tf_op jit(solution)/shard_map/ppermute | solution.py:505
  18.8 6.3 %collective-permute-start.8 = (f32[64,512]{1,0:T(8,128)S(1)}, f32[64,512]{1,0:T(8,128)S(1)}, u32[]{:S(2)}, u32[]{:S(2)}) collective-permute-start(f32[64,512]{1,0:T(8,128)S(1)} %get-tuple-element.119), channel_id=1, source_target_pairs={{0,7},{1,9},{2,10},{3,4},{4,3},{5,13},{6,14},{7,0},{8,15},{9,1},{1... | collective-permute-start | bytes 393224 | tf_op jit(solution)/shard_map/ppermute | solution.py:505
  20.4 5.0 %collective-permute-start.9 = (f32[64,512]{1,0:T(8,128)S(1)}, f32[64,512]{1,0:T(8,128)S(1)}, u32[]{:S(2)}, u32[]{:S(2)}) collective-permute-start(f32[64,512]{1,0:T(8,128)S(1)} %get-tuple-element.122), channel_id=1, source_target_pairs={{0,8},{1,2},{2,1},{3,11},{4,12},{5,6},{6,5},{7,15},{8,0},{9,17},{1... | collective-permute-start | bytes 393224 | tf_op jit(solution)/shard_map/ppermute | solution.py:505
  26.0 5.6 %collective-permute-start.12 = (f32[64,512]{1,0:T(8,128)S(1)}, f32[64,512]{1,0:T(8,128)S(1)}, u32[]{:S(2)}, u32[]{:S(2)}) collective-permute-start(f32[64,512]{1,0:T(8,128)S(1)} %get-tuple-element.130), channel_id=1, source_target_pairs={{0,7},{1,9},{2,10},{3,4},{4,3},{5,13},{6,14},{7,0},{8,15},{9,1},{1... | collective-permute-start | bytes 393224 | tf_op jit(solution)/shard_map/ppermute | solution.py:505
  27.5 5.0 %collective-permute-start.13 = (f32[64,512]{1,0:T(8,128)S(1)}, f32[64,512]{1,0:T(8,128)S(1)}, u32[]{:S(2)}, u32[]{:S(2)}) collective-permute-start(f32[64,512]{1,0:T(8,128)S(1)} %get-tuple-element.134), channel_id=1, source_target_pairs={{0,8},{1,2},{2,1},{3,11},{4,12},{5,6},{6,5},{7,15},{8,0},{9,17},{1... | collective-permute-start | bytes 393224 | tf_op jit(solution)/shard_map/ppermute | solution.py:505
  33.4 4.3 %collective-permute-start.19 = (f32[64,128]{1,0:T(8,128)S(1)}, f32[64,128]{1,0:T(8,128)S(1)}, u32[]{:S(2)}, u32[]{:S(2)}) collective-permute-start(f32[64,128]{1,0:T(8,128)S(1)} %get-tuple-element.137.update.iterate), channel_id=1, source_target_pairs={{0,7},{1,9},{2,10},{3,4},{4,3},{5,13},{6,14},{7,0},{8,15},{9,1},{1... | collective-permute-start | bytes 98312 | tf_op jit(solution)/shard_map/ppermute | solution.py:505
  34.8 4.0 %collective-permute-start.18 = (f32[64,128]{1,0:T(8,128)S(1)}, f32[64,128]{1,0:T(8,128)S(1)}, u32[]{:S(2)}, u32[]{:S(2)}) collective-permute-start(f32[64,128]{1,0:T(8,128)S(1)} %get-tuple-element.137.update.iterate), channel_id=1, source_target_pairs={{0,8},{1,2},{2,1},{3,11},{4,12},{5,6},{6,5},{7,15},{8,0},{9,17},{1... | collective-permute-start | bytes 98312 | tf_op jit(solution)/shard_map/ppermute | solution.py:505
  39.1 4.3 %collective-permute-start.23 = (f32[64,128]{1,0:T(8,128)S(1)}, f32[64,128]{1,0:T(8,128)S(1)}, u32[]{:S(2)}, u32[]{:S(2)}) collective-permute-start(f32[64,128]{1,0:T(8,128)S(1)} %get-tuple-element.141.update), channel_id=1, source_target_pairs={{0,7},{1,9},{2,10},{3,4},{4,3},{5,13},{6,14},{7,0},{8,15},{9,1},{1... | collective-permute-start | bytes 98312 | tf_op jit(solution)/shard_map/ppermute | solution.py:505
  39.5 4.0 %collective-permute-start.22 = (f32[64,128]{1,0:T(8,128)S(1)}, f32[64,128]{1,0:T(8,128)S(1)}, u32[]{:S(2)}, u32[]{:S(2)}) collective-permute-start(f32[64,128]{1,0:T(8,128)S(1)} %get-tuple-element.141.update), channel_id=1, source_target_pairs={{0,8},{1,2},{2,1},{3,11},{4,12},{5,6},{6,5},{7,15},{8,0},{9,17},{1... | collective-permute-start | bytes 98312 | tf_op jit(solution)/shard_map/ppermute | solution.py:505
  44.1 5.9 %collective-permute-start.24 = (f32[64,128]{1,0:T(8,128)S(1)}, f32[64,128]{1,0:T(8,128)S(1)}, u32[]{:S(2)}, u32[]{:S(2)}) collective-permute-start(f32[64,128]{1,0:T(8,128)S(1)} %shard_map.100.correction), channel_id=1, source_target_pairs={{0,7},{1,9},{2,10},{3,4},{4,3},{5,13},{6,14},{7,0},{8,15},{9,1},{1... | collective-permute-start | bytes 98312 | tf_op jit(solution)/shard_map/ppermute | solution.py:505
  45.3 5.1 %collective-permute-start.27 = (f32[64,128]{1,0:T(8,128)S(1)}, f32[64,128]{1,0:T(8,128)S(1)}, u32[]{:S(2)}, u32[]{:S(2)}) collective-permute-start(f32[64,128]{1,0:T(8,128)S(1)} %shard_map.100.correction), channel_id=1, source_target_pairs={{0,1},{1,0},{2,3},{3,2},{4,5},{5,4},{6,7},{7,6},{8,9},{9,8},{10,11... | collective-permute-start | bytes 98312 | tf_op jit(solution)/shard_map/ppermute | solution.py:505
  46.3 4.1 %collective-permute-start.26 = (f32[64,128]{1,0:T(8,128)S(1)}, f32[64,128]{1,0:T(8,128)S(1)}, u32[]{:S(2)}, u32[]{:S(2)}) collective-permute-start(f32[64,128]{1,0:T(8,128)S(1)} %shard_map.100.correction), channel_id=1, source_target_pairs={{0,1},{1,0},{2,3},{3,2},{4,5},{5,4},{6,7},{7,6},{8,16},{9,10},{10,... | collective-permute-start | bytes 98312 | tf_op jit(solution)/shard_map/ppermute | solution.py:505
  46.3 4.7 %collective-permute-start.25 = (f32[64,128]{1,0:T(8,128)S(1)}, f32[64,128]{1,0:T(8,128)S(1)}, u32[]{:S(2)}, u32[]{:S(2)}) collective-permute-start(f32[64,128]{1,0:T(8,128)S(1)} %shard_map.100.correction), channel_id=1, source_target_pairs={{0,8},{1,2},{2,1},{3,11},{4,12},{5,6},{6,5},{7,15},{8,0},{9,17},{1... | collective-permute-start | bytes 98312 | tf_op jit(solution)/shard_map/ppermute | solution.py:505
  51.7 6.3 %collective-permute-start.28 = (f32[64,512]{1,0:T(8,128)S(1)}, f32[64,512]{1,0:T(8,128)S(1)}, u32[]{:S(2)}, u32[]{:S(2)}) collective-permute-start(f32[64,512]{1,0:T(8,128)S(1)} %get-tuple-element.158), channel_id=1, source_target_pairs={{0,7},{1,9},{2,10},{3,4},{4,3},{5,13},{6,14},{7,0},{8,15},{9,1},{1... | collective-permute-start | bytes 393224 | tf_op jit(solution)/shard_map/ppermute | solution.py:505
  52.5 5.7 %collective-permute-start.29 = (f32[64,512]{1,0:T(8,128)S(1)}, f32[64,512]{1,0:T(8,128)S(1)}, u32[]{:S(2)}, u32[]{:S(2)}) collective-permute-start(f32[64,512]{1,0:T(8,128)S(1)} %get-tuple-element.161), channel_id=1, source_target_pairs={{0,8},{1,2},{2,1},{3,11},{4,12},{5,6},{6,5},{7,15},{8,0},{9,17},{1... | collective-permute-start | bytes 393224 | tf_op jit(solution)/shard_map/ppermute | solution.py:505
  54.2 4.0 %collective-permute-start.30 = (f32[64,512]{1,0:T(8,128)S(1)}, f32[64,512]{1,0:T(8,128)S(1)}, u32[]{:S(2)}, u32[]{:S(2)}) collective-permute-start(f32[64,512]{1,0:T(8,128)S(1)} %get-tuple-element.162), channel_id=1, source_target_pairs={{0,1},{1,0},{2,3},{3,2},{4,5},{5,4},{6,7},{7,6},{8,16},{9,10},{10,... | collective-permute-start | bytes 393224 | tf_op jit(solution)/shard_map/ppermute | solution.py:505
  54.6 3.7 %collective-permute-start.31 = (f32[64,512]{1,0:T(8,128)S(1)}, f32[64,512]{1,0:T(8,128)S(1)}, u32[]{:S(2)}, u32[]{:S(2)}) collective-permute-start(f32[64,512]{1,0:T(8,128)S(1)} %get-tuple-element.163), channel_id=1, source_target_pairs={{0,1},{1,0},{2,3},{3,2},{4,5},{5,4},{6,7},{7,6},{8,9},{9,8},{10,11... | collective-permute-start | bytes 393224 | tf_op jit(solution)/shard_map/ppermute | solution.py:505
  58.8 5.4 %collective-permute-start.32 = (f32[64,512]{1,0:T(8,128)S(1)}, f32[64,512]{1,0:T(8,128)S(1)}, u32[]{:S(2)}, u32[]{:S(2)}) collective-permute-start(f32[64,512]{1,0:T(8,128)S(1)} %get-tuple-element.169), channel_id=1, source_target_pairs={{0,7},{1,9},{2,10},{3,4},{4,3},{5,13},{6,14},{7,0},{8,15},{9,1},{1... | collective-permute-start | bytes 393224 | tf_op jit(solution)/shard_map/ppermute | solution.py:505
  59.5 5.0 %collective-permute-start.33 = (f32[64,512]{1,0:T(8,128)S(1)}, f32[64,512]{1,0:T(8,128)S(1)}, u32[]{:S(2)}, u32[]{:S(2)}) collective-permute-start(f32[64,512]{1,0:T(8,128)S(1)} %get-tuple-element.172), channel_id=1, source_target_pairs={{0,8},{1,2},{2,1},{3,11},{4,12},{5,6},{6,5},{7,15},{8,0},{9,17},{1... | collective-permute-start | bytes 393224 | tf_op jit(solution)/shard_map/ppermute | solution.py:505
  (12 other events, 31.2 us)

commit v4 on v3

--- a/solution.py
+++ b/solution.py
@@ -12,7 +12,7 @@
 radius_value = 0.9
 AXES = ("span", "stream")
 STEPS = ((0,), (1, 2, 3))
-AHEAD = 2
+AHEAD = 3
 COARSE = (3, 2, 1, 0)
 CHUNK = 4
 VMEM_LIMIT = 16 * 1024 * 1024
@@ -285,9 +285,27 @@
     begin_sweep(left, update, iterate_out, inverse, new, weights, mode, onehot)
 
 
+def turn_received(table, lay, matrix, turned, size):
+    identity = jnp.where(square_mask(size), 1.0, 0.0).astype(bf16)
+
+    def group(buffer, start):
+        for i in range(CHUNK):
+            which = table[lay.entries + buffer * lay.capacity + start + i] >> 16
+            turned[which] = dot_nt(identity, matrix[which]).astype(bf16)
+
+    for buffer in range(4):
+        group(buffer, 0)
+
+        def more(c, carry, buffer=buffer):
+            group(buffer, c * CHUNK)
+            return carry
+
+        lax.fori_loop(1, (table[lay.counts + buffer] + CHUNK - 1) // CHUNK, more, 0)
+
+
 def local_and_coarse_kernel(
     table, update, residual, iterate, inverse, matrix, groups, coarse, h0, h1, h2, h3,
-    left, new, iterate_out, onehot, names, coarse_high, coarse_low, coarse_inverse, wide, brought, cells, sems, *, size, lay, weights,
+    left, new, iterate_out, turned, onehot, names, coarse_high, coarse_low, coarse_inverse, wide, brought, cells, sems, *, size, lay, weights,
 ):
     copies = [
         pltpu.make_async_copy(coarse, brought, sems.at[0]),
@@ -299,6 +317,7 @@
         table, update, residual, iterate, inverse, matrix, left, new, iterate_out, wide,
         size=size, lay=lay, weights=weights, mode="plain",
     )
+    turn_received(table, lay, matrix, turned, size)
     width = lay.slots * size
     rows = update.shape[0]
     number = lax.broadcasted_iota(i32, (size, width), 0).astype(f32)
@@ -344,18 +363,19 @@
         put_halo(wide, place, x, size)
 
 
-def entry_product(code, matrix, wide, place, lay, size):
+def entry_product(code, matrix, wide, place, lay, size, dot):
     which, row, slot = code >> 16, (code >> 8) & 255, code & 255
     at = block(place * (lay.slots + 1) + slot, size)
-    return block(row, size), halves(dot_nt(wide[:, at], matrix[which]))
-
-
-def for_received(table, lay, buffers, matrix, wide, size, use):
+    return block(row, size), halves(dot(wide[:, at], matrix[which]))
+
+
+def for_received(table, lay, buffers, matrix, wide, size, dot, use):
     def group(members):
         use(
             [
                 entry_product(
-                    table[lay.entries + buffer * lay.capacity + i], matrix, wide, place, lay, size
+                    table[lay.entries + buffer * lay.capacity + i],
+                    matrix, wide, place, lay, size, dot,
                 )
                 for place, buffer, i in members
             ]
@@ -372,7 +392,7 @@
         lax.fori_loop(1, chunks, more, 0)
 
 
-def received_kernel(table, left_in, new_in, inverse, matrix, *refs, size, lay, weights, mode, buffers, final):
+def received_kernel(table, left_in, new_in, inverse, matrix, *refs, size, lay, weights, mode, buffers, final, turned):
     refs = list(refs)
     halos, refs = refs[: len(buffers)], refs[len(buffers) :]
     rows = left_in.shape[0]
@@ -400,7 +420,7 @@
                 halves(dot_nt(stacked(product), onehot[:, at])) for at, product in found
             )
 
-    for_received(table, lay, buffers, matrix, wide, size, use)
+    for_received(table, lay, buffers, matrix, wide, size, dot_nn if turned else dot_nt, use)
     if not final or mode == "last":
         return
     if mode == "restrict":
@@ -513,6 +533,7 @@
     dims = {"size": size, "lay": lay}
 
     def received(halos, left, new, weight, mode="plain", extra=()):
+        blocks_in = matrix if turned is None else turned
         for step, buffers in enumerate(STEPS):
             final = step == len(STEPS) - 1
             outs, kept = [field, small if mode == "restrict" else field], "VV"
@@ -525,14 +546,15 @@
                 outs += [halo] * 4
             result = call(
                 received_kernel,
-                [table, left, new, inverse, matrix] + [halos[b] for b in buffers] + list(extra),
+                [table, left, new, inverse, blocks_in] + [halos[b] for b in buffers] + list(extra),
                 outs,
                 [
                     pltpu.VMEM((2 * rows, len(buffers) * (halo_width + size)), bf16),
                     pltpu.VMEM((8, width), f32),
                 ],
                 "sVV", kept, aliases, flops=flops * len(buffers) // 20,
-                weights=weight, mode=mode, buffers=buffers, final=final, **dims,
+                weights=weight, mode=mode, buffers=buffers, final=final,
+                turned=turned is not None, **dims,
             )
             left, new = result[0], result[1] if len(result) > 1 else None
         return result
@@ -560,15 +582,17 @@
         [wide_local, pltpu.VMEM(*field), pltpu.SemaphoreType.DMA((parts + 1,))],
         "ssvhh", "VVs", flops=flops, parts=parts, **dims,
     )
+    turned = None
     residual, update, *payloads = received(halos, left, new, None)
     halos = exchange(payloads)
-    left, new, iterate, onehot, names, coarse_high, coarse_low, coarse_inverse = call(
+    left, new, iterate, turned, onehot, names, coarse_high, coarse_low, coarse_inverse = call(
         local_and_coarse_kernel,
         [table, update, residual, guess, inverse, matrix, groups, coarse] + first_halos,
         [
             field,
             field,
             field,
+            (stored.shape, bf16),
             ((size, width), bf16),
             ((size, 4 * halo_width), bf16),
             ((size, 5 * size), bf16),

time: 66.5 us -> 65.7 us (0.988)
  Pallas kernels: 21.8 us -> 20.8 us
    pallas_call x24, Pallas kernels: 21.8 us -> 20.8 us  [call(): pl.pallas_call(functools.partial(kernel, **named), out_shape=[forms[c](sh...]
  transfers between devices with their start and end apart: 36 -> 36, of which waited for: 12 -> 12; matrix products, arithmetic and copies ran while one was open for 0% -> 0% of each run, Pallas kernels for 23% -> 22%
where the time goes in v4:
time: 65.7 us; the launch traced here: 65.1 us
  starting transfers between devices  37.2 us (57%)
  Pallas kernels  20.8 us (32%)
  waiting for transfers between devices  6.31 us (10%)
  between operations  0.91 us (1%)
    ppermute x36, starting transfers between devices, exchange(): return [lax.ppermute(x, AXES, perm) for x, perm in zip(payloads, perms)]  37.2 us
    pallas_call x24, Pallas kernels, call(): pl.pallas_call(functools.partial(kernel, **named), out_shape=[forms[c](sh...  20.8 us
    ppermute x36, waiting for transfers between devices, exchange(): return [lax.ppermute(x, AXES, perm) for x, perm in zip(payloads, perms)]  6.31 us
  transfers between devices with their start and end apart: 36, of which 12 were waited for; matrix products, arithmetic and copies ran while one was open for 0% of the time, Pallas kernels for 22%

profile of v4, /device:TPU:0, one launch (start us, length us, event | category | flops | bytes accessed | tf_op | source)
XLA Modules:
  0.0 65.1 jit_solution(17425933914438310411)
XLA Ops:
  0.6 1.2 %shard_map.86 = (f32[72,512]{1,0:T(8,128)S(1)}, f32[72,512]{1,0:T(8,128)S(1)}, f32[72,512]{1,0:T(8,128)S(1)}, f32[72,512]{1,0:T(8,128)S(1)}, f32[64,2048]{1,0:T(...) custom-call(f32[64,2048]{1,0:T(8,128)} %guess.1, s32[1,16]{1,0:T(1,128)} %lists.1, s32[5,16]{1,0:T(8,128)} %bitcast.8, ...), custom_call_target="tpu_custom_call" | custom-call | bytes 4194304 | tf_op jit(solution)/shard_map/pallas_call | solution.py:511
  1.8 3.4 %collective-permute-start = (f32[72,512]{1,0:T(8,128)S(1)}, f32[72,512]{1,0:T(8,128)S(1)}, u32[]{:S(2)}, u32[]{:S(2)}) collective-permute-start(f32[72,512]{1,0:T(8,128)S(1)} %get-tuple-element.98), channel_id=1, source_target_pairs={{0,7},{1,9},{2,10},{3,4},{4,3},{5,13},{6,14},{7,0},{8,15},{9,1},{1... | collective-permute-start | bytes 442376 | tf_op jit(solution)/shard_map/ppermute | solution.py:525
  5.2 1.6 %collective-permute-start.1 = (f32[72,512]{1,0:T(8,128)S(1)}, f32[72,512]{1,0:T(8,128)S(1)}, u32[]{:S(2)}, u32[]{:S(2)}) collective-permute-start(f32[72,512]{1,0:T(8,128)S(1)} %get-tuple-element.101), channel_id=1, source_target_pairs={{0,8},{1,2},{2,1},{3,11},{4,12},{5,6},{6,5},{7,15},{8,0},{9,17},{1... | collective-permute-start | bytes 442376 | tf_op jit(solution)/shard_map/ppermute | solution.py:525
  7.3 2.9 %shard_map.87 = (f32[64,2048]{1,0:T(8,128)S(1)}, f32[64,2048]{1,0:T(8,128)S(1)}, s32[446]{0:T(512)S(4)}, f32[8,2048]{1,0:T(8,128)S(1)}, bf16[80,128,128]{2,1,0:T(8,128)(2,1)S(1)}) custom-call(s32[1,16]{1,0:T(1,128)S(4)} %get-tuple-element.90.lists, s32[5,16]{1,0:T(8,128)S(4)} %get-tuple-element.91.columns, f32[64,2048]{1,0:T(8,128)S(1)} %get-tuple-element.92.field.iterate, ...), custom_call_target="tpu_custom_call" | custom-call | flops 335544320 | bytes 4194304 | tf_op jit(solution)/shard_map/pallas_call | solution.py:511
  11.1 1.6 %collective-permute-start.4 = (f32[64,512]{1,0:T(8,128)S(1)}, f32[64,512]{1,0:T(8,128)S(1)}, u32[]{:S(2)}, u32[]{:S(2)}) collective-permute-start(f32[64,512]{1,0:T(8,128)S(1)} %get-tuple-element.109), channel_id=1, source_target_pairs={{0,7},{1,9},{2,10},{3,4},{4,3},{5,13},{6,14},{7,0},{8,15},{9,1},{1... | collective-permute-start | bytes 393224 | tf_op jit(solution)/shard_map/ppermute | solution.py:525
  12.6 2.3 %collective-permute-start.5 = (f32[64,512]{1,0:T(8,128)S(1)}, f32[64,512]{1,0:T(8,128)S(1)}, u32[]{:S(2)}, u32[]{:S(2)}) collective-permute-start(f32[64,512]{1,0:T(8,128)S(1)} %get-tuple-element.112), channel_id=1, source_target_pairs={{0,8},{1,2},{2,1},{3,11},{4,12},{5,6},{6,5},{7,15},{8,0},{9,17},{1... | collective-permute-start | bytes 393224 | tf_op jit(solution)/shard_map/ppermute | solution.py:525
  15.4 2.1 %shard_map.90 = (f32[64,2048]{1,0:T(8,128)S(1)}, f32[64,2048]{1,0:T(8,128)S(1)}, f32[64,2048]{1,0:T(8,128)S(1)}, bf16[80,128,128]{2,1,0:T(8,128)(2,1)S(1)}, bf16...) custom-call(s32[446]{0:T(512)S(4)} %get-tuple-element.93.table, ...), custom_call_target="tpu_custom_call" | custom-call | flops 335544320 | bytes 4194304 | tf_op jit(solution)/shard_map/pallas_call | solution.py:511
  18.4 1.9 %collective-permute-start.8 = (f32[64,512]{1,0:T(8,128)S(1)}, f32[64,512]{1,0:T(8,128)S(1)}, u32[]{:S(2)}, u32[]{:S(2)}) collective-permute-start(f32[64,512]{1,0:T(8,128)S(1)} %get-tuple-element.121), channel_id=1, source_target_pairs={{0,7},{1,9},{2,10},{3,4},{4,3},{5,13},{6,14},{7,0},{8,15},{9,1},{1... | collective-permute-start | bytes 393224 | tf_op jit(solution)/shard_map/ppermute | solution.py:525
  20.3 2.1 %collective-permute-start.9 = (f32[64,512]{1,0:T(8,128)S(1)}, f32[64,512]{1,0:T(8,128)S(1)}, u32[]{:S(2)}, u32[]{:S(2)}) collective-permute-start(f32[64,512]{1,0:T(8,128)S(1)} %get-tuple-element.124), channel_id=1, source_target_pairs={{0,8},{1,2},{2,1},{3,11},{4,12},{5,6},{6,5},{7,15},{8,0},{9,17},{1... | collective-permute-start | bytes 393224 | tf_op jit(solution)/shard_map/ppermute | solution.py:525
  22.9 2.1 %shard_map.93 = (f32[64,2048]{1,0:T(8,128)S(1)}, f32[64,2048]{1,0:T(8,128)S(1)}, f32[64,2048]{1,0:T(8,128)S(1)}, bf16[128,2048]{1,0:T(8,128)(2,1)S(1)}, bf16[128,2048]{1,0:T(8,128)(2,1)S(1)}) custom-call(s32[446]{0:T(512)S(4)} %get-tuple-element.93.table, f32[64,2048]{1,0:T(8,128)S(1)} %get-tuple-element.115.update, ...), custom_call_target="tpu_custom_call" | custom-call | flops 335544320 | bytes 4194304 | tf_op jit(solution)/shard_map/pallas_call | solution.py:511
  25.8 1.5 %collective-permute-start.12 = (f32[64,512]{1,0:T(8,128)S(1)}, f32[64,512]{1,0:T(8,128)S(1)}, u32[]{:S(2)}, u32[]{:S(2)}) collective-permute-start(f32[64,512]{1,0:T(8,128)S(1)} %get-tuple-element.132), channel_id=1, source_target_pairs={{0,7},{1,9},{2,10},{3,4},{4,3},{5,13},{6,14},{7,0},{8,15},{9,1},{1... | collective-permute-start | bytes 393224 | tf_op jit(solution)/shard_map/ppermute | solution.py:525
  27.4 2.0 %collective-permute-start.13 = (f32[64,512]{1,0:T(8,128)S(1)}, f32[64,512]{1,0:T(8,128)S(1)}, u32[]{:S(2)}, u32[]{:S(2)}) collective-permute-start(f32[64,512]{1,0:T(8,128)S(1)} %get-tuple-element.136), channel_id=1, source_target_pairs={{0,8},{1,2},{2,1},{3,11},{4,12},{5,6},{6,5},{7,15},{8,0},{9,17},{1... | collective-permute-start | bytes 393224 | tf_op jit(solution)/shard_map/ppermute | solution.py:525
  29.9 1.5 %shard_map.96 = (f32[64,2048]{1,0:T(8,128)S(1)}, f32[64,128]{1,0:T(8,128)S(1)}, f32[64,2048]{1,0:T(8,128)S(1)}) custom-call(s32[446]{0:T(512)S(4)} %get-tuple-element.93.table, f32[64,2048]{1,0:T(8,128)S(1)} %get-tuple-element.127.update, f32[64,2048]{1,0:T(8,128)S(1)} %get-tuple-element.128.residual, f32[64,2048]{1,0:T(8,128)S(1)} %get-tuple-element.129.iterate, ...), custom_call_target="tpu_custom_call" | custom-call | flops 335544320 | bytes 4194304 | tf_op jit(solution)/shard_map/pallas_call | solution.py:511
  33.1 1.5 %collective-permute-start.19 = (f32[64,128]{1,0:T(8,128)S(1)}, f32[64,128]{1,0:T(8,128)S(1)}, u32[]{:S(2)}, u32[]{:S(2)}) collective-permute-start(f32[64,128]{1,0:T(8,128)S(1)} %get-tuple-element.139.update.iterate), channel_id=1, source_target_pairs={{0,7},{1,9},{2,10},{3,4},{4,3},{5,13},{6,14},{7,0},{8,15},{9,1},{1... | collective-permute-start | bytes 98312 | tf_op jit(solution)/shard_map/ppermute | solution.py:525
  34.6 2.1 %collective-permute-start.18 = (f32[64,128]{1,0:T(8,128)S(1)}, f32[64,128]{1,0:T(8,128)S(1)}, u32[]{:S(2)}, u32[]{:S(2)}) collective-permute-start(f32[64,128]{1,0:T(8,128)S(1)} %get-tuple-element.139.update.iterate), channel_id=1, source_target_pairs={{0,8},{1,2},{2,1},{3,11},{4,12},{5,6},{6,5},{7,15},{8,0},{9,17},{1... | collective-permute-start | bytes 98312 | tf_op jit(solution)/shard_map/ppermute | solution.py:525
  37.4 1.2 %collective-permute-done.18.h2 = f32[64,128]{1,0:T(8,128)S(1)} collective-permute-done((f32[64,128]{1,0:T(8,128)S(1)}, f32[64,128]{1,0:T(8,128)S(1)}, u32[]{:S(2)}, u32[]{:S(2)}) %collective-permute-start.18) | collective-permute-done | bytes 32800 | tf_op jit(solution)/shard_map/ppermute | solution.py:525
  39.3 2.1 %collective-permute-start.22 = (f32[64,128]{1,0:T(8,128)S(1)}, f32[64,128]{1,0:T(8,128)S(1)}, u32[]{:S(2)}, u32[]{:S(2)}) collective-permute-start(f32[64,128]{1,0:T(8,128)S(1)} %get-tuple-element.143.update), channel_id=1, source_target_pairs={{0,8},{1,2},{2,1},{3,11},{4,12},{5,6},{6,5},{7,15},{8,0},{9,17},{1... | collective-permute-start | bytes 98312 | tf_op jit(solution)/shard_map/ppermute | solution.py:525
  43.7 1.3 %collective-permute-start.24 = (f32[64,128]{1,0:T(8,128)S(1)}, f32[64,128]{1,0:T(8,128)S(1)}, u32[]{:S(2)}, u32[]{:S(2)}) collective-permute-start(f32[64,128]{1,0:T(8,128)S(1)} %shard_map.100.correction), channel_id=1, source_target_pairs={{0,7},{1,9},{2,10},{3,4},{4,3},{5,13},{6,14},{7,0},{8,15},{9,1},{1... | collective-permute-start | bytes 98312 | tf_op jit(solution)/shard_map/ppermute | solution.py:525
  45.9 2.8 %collective-permute-start.25 = (f32[64,128]{1,0:T(8,128)S(1)}, f32[64,128]{1,0:T(8,128)S(1)}, u32[]{:S(2)}, u32[]{:S(2)}) collective-permute-start(f32[64,128]{1,0:T(8,128)S(1)} %shard_map.100.correction), channel_id=1, source_target_pairs={{0,8},{1,2},{2,1},{3,11},{4,12},{5,6},{6,5},{7,15},{8,0},{9,17},{1... | collective-permute-start | bytes 98312 | tf_op jit(solution)/shard_map/ppermute | solution.py:525
  52.2 1.8 %collective-permute-start.29 = (f32[64,512]{1,0:T(8,128)S(1)}, f32[64,512]{1,0:T(8,128)S(1)}, u32[]{:S(2)}, u32[]{:S(2)}) collective-permute-start(f32[64,512]{1,0:T(8,128)S(1)} %get-tuple-element.163), channel_id=1, source_target_pairs={{0,8},{1,2},{2,1},{3,11},{4,12},{5,6},{6,5},{7,15},{8,0},{9,17},{1... | collective-permute-start | bytes 393224 | tf_op jit(solution)/shard_map/ppermute | solution.py:525
  54.4 1.2 %shard_map.104 = (f32[64,2048]{1,0:T(8,128)S(1)}, f32[64,2048]{1,0:T(8,128)S(1)}, f32[64,2048]{1,0:T(8,128)S(1)}) custom-call(s32[446]{0:T(512)S(4)} %get-tuple-element.93.table, f32[64,2048]{1,0:T(8,128)S(1)} %get-tuple-element.155.update, f32[64,2048]{1,0:T(8,128)S(1)} %get-tuple-element.156.residual, f32[64,2048]{1,0:T(8,128)S(1)} %get-tuple-element.157.iterate, ...), custom_call_target="tpu_custom_call" | custom-call | flops 335544320 | bytes 4194304 | tf_op jit(solution)/shard_map/pallas_call | solution.py:511
  55.6 1.9 %collective-permute-done.28.refs_0_ = f32[64,512]{1,0:T(8,128)S(1)} collective-permute-done((f32[64,512]{1,0:T(8,128)S(1)}, f32[64,512]{1,0:T(8,128)S(1)}, u32[]{:S(2)}, u32[]{:S(2)}) %collective-permute-start.28) | collective-permute-done | bytes 131104 | tf_op jit(solution)/shard_map/ppermute | solution.py:525
  59.0 1.9 %collective-permute-start.33 = (f32[64,512]{1,0:T(8,128)S(1)}, f32[64,512]{1,0:T(8,128)S(1)}, u32[]{:S(2)}, u32[]{:S(2)}) collective-permute-start(f32[64,512]{1,0:T(8,128)S(1)} %get-tuple-element.174), channel_id=1, source_target_pairs={{0,8},{1,2},{2,1},{3,11},{4,12},{5,6},{6,5},{7,15},{8,0},{9,17},{1... | collective-permute-start | bytes 393224 | tf_op jit(solution)/shard_map/ppermute | solution.py:525
  61.5 1.9 %shard_map.107 = (f32[64,2048]{1,0:T(8,128)S(1)}, f32[64,2048]{1,0:T(8,128)S(1)}, f32[64,2048]{1,0:T(8,128)}) custom-call(s32[446]{0:T(512)S(4)} %get-tuple-element.93.table, f32[64,2048]{1,0:T(8,128)S(1)} %get-tuple-element.166.update, f32[64,2048]{1,0:T(8,128)S(1)} %get-tuple-element.167.residual, f32[64,2048]{1,0:T(8,128)S(1)} %get-tuple-element.168.iterate, ...), custom_call_target="tpu_custom_call" | custom-call | flops 335544320 | bytes 4194304 | tf_op jit(solution)/shard_map/pallas_call | solution.py:511
  (72 shorter events, 18.3 us)
Async XLA Ops:
  1.8 8.4 %collective-permute-start = (f32[72,512]{1,0:T(8,128)S(1)}, f32[72,512]{1,0:T(8,128)S(1)}, u32[]{:S(2)}, u32[]{:S(2)}) collective-permute-start(f32[72,512]{1,0:T(8,128)S(1)} %get-tuple-element.98), channel_id=1, source_target_pairs={{0,7},{1,9},{2,10},{3,4},{4,3},{5,13},{6,14},{7,0},{8,15},{9,1},{1... | collective-permute-start | bytes 442376 | tf_op jit(solution)/shard_map/ppermute | solution.py:525
  5.2 5.2 %collective-permute-start.1 = (f32[72,512]{1,0:T(8,128)S(1)}, f32[72,512]{1,0:T(8,128)S(1)}, u32[]{:S(2)}, u32[]{:S(2)}) collective-permute-start(f32[72,512]{1,0:T(8,128)S(1)} %get-tuple-element.101), channel_id=1, source_target_pairs={{0,8},{1,2},{2,1},{3,11},{4,12},{5,6},{6,5},{7,15},{8,0},{9,17},{1... | collective-permute-start | bytes 442376 | tf_op jit(solution)/shard_map/ppermute | solution.py:525
  6.8 3.7 %collective-permute-start.2 = (f32[72,512]{1,0:T(8,128)S(1)}, f32[72,512]{1,0:T(8,128)S(1)}, u32[]{:S(2)}, u32[]{:S(2)}) collective-permute-start(f32[72,512]{1,0:T(8,128)S(1)} %get-tuple-element.102), channel_id=1, source_target_pairs={{0,1},{1,0},{2,3},{3,2},{4,5},{5,4},{6,7},{7,6},{8,16},{9,10},{10,... | collective-permute-start | bytes 442376 | tf_op jit(solution)/shard_map/ppermute | solution.py:525
  6.8 3.7 %collective-permute-start.3 = (f32[72,512]{1,0:T(8,128)S(1)}, f32[72,512]{1,0:T(8,128)S(1)}, u32[]{:S(2)}, u32[]{:S(2)}) collective-permute-start(f32[72,512]{1,0:T(8,128)S(1)} %get-tuple-element.103), channel_id=1, source_target_pairs={{0,1},{1,0},{2,3},{3,2},{4,5},{5,4},{6,7},{7,6},{8,9},{9,8},{10,11... | collective-permute-start | bytes 442376 | tf_op jit(solution)/shard_map/ppermute | solution.py:525
  11.1 6.5 %collective-permute-start.4 = (f32[64,512]{1,0:T(8,128)S(1)}, f32[64,512]{1,0:T(8,128)S(1)}, u32[]{:S(2)}, u32[]{:S(2)}) collective-permute-start(f32[64,512]{1,0:T(8,128)S(1)} %get-tuple-element.109), channel_id=1, source_target_pairs={{0,7},{1,9},{2,10},{3,4},{4,3},{5,13},{6,14},{7,0},{8,15},{9,1},{1... | collective-permute-start | bytes 393224 | tf_op jit(solution)/shard_map/ppermute | solution.py:525
  12.6 5.3 %collective-permute-start.5 = (f32[64,512]{1,0:T(8,128)S(1)}, f32[64,512]{1,0:T(8,128)S(1)}, u32[]{:S(2)}, u32[]{:S(2)}) collective-permute-start(f32[64,512]{1,0:T(8,128)S(1)} %get-tuple-element.112), channel_id=1, source_target_pairs={{0,8},{1,2},{2,1},{3,11},{4,12},{5,6},{6,5},{7,15},{8,0},{9,17},{1... | collective-permute-start | bytes 393224 | tf_op jit(solution)/shard_map/ppermute | solution.py:525
  18.4 6.6 %collective-permute-start.8 = (f32[64,512]{1,0:T(8,128)S(1)}, f32[64,512]{1,0:T(8,128)S(1)}, u32[]{:S(2)}, u32[]{:S(2)}) collective-permute-start(f32[64,512]{1,0:T(8,128)S(1)} %get-tuple-element.121), channel_id=1, source_target_pairs={{0,7},{1,9},{2,10},{3,4},{4,3},{5,13},{6,14},{7,0},{8,15},{9,1},{1... | collective-permute-start | bytes 393224 | tf_op jit(solution)/shard_map/ppermute | solution.py:525
  20.3 5.0 %collective-permute-start.9 = (f32[64,512]{1,0:T(8,128)S(1)}, f32[64,512]{1,0:T(8,128)S(1)}, u32[]{:S(2)}, u32[]{:S(2)}) collective-permute-start(f32[64,512]{1,0:T(8,128)S(1)} %get-tuple-element.124), channel_id=1, source_target_pairs={{0,8},{1,2},{2,1},{3,11},{4,12},{5,6},{6,5},{7,15},{8,0},{9,17},{1... | collective-permute-start | bytes 393224 | tf_op jit(solution)/shard_map/ppermute | solution.py:525
  25.8 5.6 %collective-permute-start.12 = (f32[64,512]{1,0:T(8,128)S(1)}, f32[64,512]{1,0:T(8,128)S(1)}, u32[]{:S(2)}, u32[]{:S(2)}) collective-permute-start(f32[64,512]{1,0:T(8,128)S(1)} %get-tuple-element.132), channel_id=1, source_target_pairs={{0,7},{1,9},{2,10},{3,4},{4,3},{5,13},{6,14},{7,0},{8,15},{9,1},{1... | collective-permute-start | bytes 393224 | tf_op jit(solution)/shard_map/ppermute | solution.py:525
  27.4 5.0 %collective-permute-start.13 = (f32[64,512]{1,0:T(8,128)S(1)}, f32[64,512]{1,0:T(8,128)S(1)}, u32[]{:S(2)}, u32[]{:S(2)}) collective-permute-start(f32[64,512]{1,0:T(8,128)S(1)} %get-tuple-element.136), channel_id=1, source_target_pairs={{0,8},{1,2},{2,1},{3,11},{4,12},{5,6},{6,5},{7,15},{8,0},{9,17},{1... | collective-permute-start | bytes 393224 | tf_op jit(solution)/shard_map/ppermute | solution.py:525
  33.1 4.3 %collective-permute-start.19 = (f32[64,128]{1,0:T(8,128)S(1)}, f32[64,128]{1,0:T(8,128)S(1)}, u32[]{:S(2)}, u32[]{:S(2)}) collective-permute-start(f32[64,128]{1,0:T(8,128)S(1)} %get-tuple-element.139.update.iterate), channel_id=1, source_target_pairs={{0,7},{1,9},{2,10},{3,4},{4,3},{5,13},{6,14},{7,0},{8,15},{9,1},{1... | collective-permute-start | bytes 98312 | tf_op jit(solution)/shard_map/ppermute | solution.py:525
  34.6 4.0 %collective-permute-start.18 = (f32[64,128]{1,0:T(8,128)S(1)}, f32[64,128]{1,0:T(8,128)S(1)}, u32[]{:S(2)}, u32[]{:S(2)}) collective-permute-start(f32[64,128]{1,0:T(8,128)S(1)} %get-tuple-element.139.update.iterate), channel_id=1, source_target_pairs={{0,8},{1,2},{2,1},{3,11},{4,12},{5,6},{6,5},{7,15},{8,0},{9,17},{1... | collective-permute-start | bytes 98312 | tf_op jit(solution)/shard_map/ppermute | solution.py:525
  38.9 4.3 %collective-permute-start.23 = (f32[64,128]{1,0:T(8,128)S(1)}, f32[64,128]{1,0:T(8,128)S(1)}, u32[]{:S(2)}, u32[]{:S(2)}) collective-permute-start(f32[64,128]{1,0:T(8,128)S(1)} %get-tuple-element.143.update), channel_id=1, source_target_pairs={{0,7},{1,9},{2,10},{3,4},{4,3},{5,13},{6,14},{7,0},{8,15},{9,1},{1... | collective-permute-start | bytes 98312 | tf_op jit(solution)/shard_map/ppermute | solution.py:525
  39.3 4.0 %collective-permute-start.22 = (f32[64,128]{1,0:T(8,128)S(1)}, f32[64,128]{1,0:T(8,128)S(1)}, u32[]{:S(2)}, u32[]{:S(2)}) collective-permute-start(f32[64,128]{1,0:T(8,128)S(1)} %get-tuple-element.143.update), channel_id=1, source_target_pairs={{0,8},{1,2},{2,1},{3,11},{4,12},{5,6},{6,5},{7,15},{8,0},{9,17},{1... | collective-permute-start | bytes 98312 | tf_op jit(solution)/shard_map/ppermute | solution.py:525
  43.7 6.0 %collective-permute-start.24 = (f32[64,128]{1,0:T(8,128)S(1)}, f32[64,128]{1,0:T(8,128)S(1)}, u32[]{:S(2)}, u32[]{:S(2)}) collective-permute-start(f32[64,128]{1,0:T(8,128)S(1)} %shard_map.100.correction), channel_id=1, source_target_pairs={{0,7},{1,9},{2,10},{3,4},{4,3},{5,13},{6,14},{7,0},{8,15},{9,1},{1... | collective-permute-start | bytes 98312 | tf_op jit(solution)/shard_map/ppermute | solution.py:525
  45.0 5.1 %collective-permute-start.27 = (f32[64,128]{1,0:T(8,128)S(1)}, f32[64,128]{1,0:T(8,128)S(1)}, u32[]{:S(2)}, u32[]{:S(2)}) collective-permute-start(f32[64,128]{1,0:T(8,128)S(1)} %shard_map.100.correction), channel_id=1, source_target_pairs={{0,1},{1,0},{2,3},{3,2},{4,5},{5,4},{6,7},{7,6},{8,9},{9,8},{10,11... | collective-permute-start | bytes 98312 | tf_op jit(solution)/shard_map/ppermute | solution.py:525
  45.9 4.2 %collective-permute-start.26 = (f32[64,128]{1,0:T(8,128)S(1)}, f32[64,128]{1,0:T(8,128)S(1)}, u32[]{:S(2)}, u32[]{:S(2)}) collective-permute-start(f32[64,128]{1,0:T(8,128)S(1)} %shard_map.100.correction), channel_id=1, source_target_pairs={{0,1},{1,0},{2,3},{3,2},{4,5},{5,4},{6,7},{7,6},{8,16},{9,10},{10,... | collective-permute-start | bytes 98312 | tf_op jit(solution)/shard_map/ppermute | solution.py:525
  45.9 4.7 %collective-permute-start.25 = (f32[64,128]{1,0:T(8,128)S(1)}, f32[64,128]{1,0:T(8,128)S(1)}, u32[]{:S(2)}, u32[]{:S(2)}) collective-permute-start(f32[64,128]{1,0:T(8,128)S(1)} %shard_map.100.correction), channel_id=1, source_target_pairs={{0,8},{1,2},{2,1},{3,11},{4,12},{5,6},{6,5},{7,15},{8,0},{9,17},{1... | collective-permute-start | bytes 98312 | tf_op jit(solution)/shard_map/ppermute | solution.py:525
  51.3 6.2 %collective-permute-start.28 = (f32[64,512]{1,0:T(8,128)S(1)}, f32[64,512]{1,0:T(8,128)S(1)}, u32[]{:S(2)}, u32[]{:S(2)}) collective-permute-start(f32[64,512]{1,0:T(8,128)S(1)} %get-tuple-element.160), channel_id=1, source_target_pairs={{0,7},{1,9},{2,10},{3,4},{4,3},{5,13},{6,14},{7,0},{8,15},{9,1},{1... | collective-permute-start | bytes 393224 | tf_op jit(solution)/shard_map/ppermute | solution.py:525
  52.2 5.6 %collective-permute-start.29 = (f32[64,512]{1,0:T(8,128)S(1)}, f32[64,512]{1,0:T(8,128)S(1)}, u32[]{:S(2)}, u32[]{:S(2)}) collective-permute-start(f32[64,512]{1,0:T(8,128)S(1)} %get-tuple-element.163), channel_id=1, source_target_pairs={{0,8},{1,2},{2,1},{3,11},{4,12},{5,6},{6,5},{7,15},{8,0},{9,17},{1... | collective-permute-start | bytes 393224 | tf_op jit(solution)/shard_map/ppermute | solution.py:525
  53.9 3.8 %collective-permute-start.30 = (f32[64,512]{1,0:T(8,128)S(1)}, f32[64,512]{1,0:T(8,128)S(1)}, u32[]{:S(2)}, u32[]{:S(2)}) collective-permute-start(f32[64,512]{1,0:T(8,128)S(1)} %get-tuple-element.164), channel_id=1, source_target_pairs={{0,1},{1,0},{2,3},{3,2},{4,5},{5,4},{6,7},{7,6},{8,16},{9,10},{10,... | collective-permute-start | bytes 393224 | tf_op jit(solution)/shard_map/ppermute | solution.py:525
  54.2 3.6 %collective-permute-start.31 = (f32[64,512]{1,0:T(8,128)S(1)}, f32[64,512]{1,0:T(8,128)S(1)}, u32[]{:S(2)}, u32[]{:S(2)}) collective-permute-start(f32[64,512]{1,0:T(8,128)S(1)} %get-tuple-element.165), channel_id=1, source_target_pairs={{0,1},{1,0},{2,3},{3,2},{4,5},{5,4},{6,7},{7,6},{8,9},{9,8},{10,11... | collective-permute-start | bytes 393224 | tf_op jit(solution)/shard_map/ppermute | solution.py:525
  58.3 5.4 %collective-permute-start.32 = (f32[64,512]{1,0:T(8,128)S(1)}, f32[64,512]{1,0:T(8,128)S(1)}, u32[]{:S(2)}, u32[]{:S(2)}) collective-permute-start(f32[64,512]{1,0:T(8,128)S(1)} %get-tuple-element.171), channel_id=1, source_target_pairs={{0,7},{1,9},{2,10},{3,4},{4,3},{5,13},{6,14},{7,0},{8,15},{9,1},{1... | collective-permute-start | bytes 393224 | tf_op jit(solution)/shard_map/ppermute | solution.py:525
  59.0 5.0 %collective-permute-start.33 = (f32[64,512]{1,0:T(8,128)S(1)}, f32[64,512]{1,0:T(8,128)S(1)}, u32[]{:S(2)}, u32[]{:S(2)}) collective-permute-start(f32[64,512]{1,0:T(8,128)S(1)} %get-tuple-element.174), channel_id=1, source_target_pairs={{0,8},{1,2},{2,1},{3,11},{4,12},{5,6},{6,5},{7,15},{8,0},{9,17},{1... | collective-permute-start | bytes 393224 | tf_op jit(solution)/shard_map/ppermute | solution.py:525
  (12 other events, 30.7 us)

commit v5 on v4

--- a/solution.py
+++ b/solution.py
@@ -12,6 +12,7 @@
 radius_value = 0.9
 AXES = ("span", "stream")
 STEPS = ((0,), (1, 2, 3))
+SPREAD_STEPS = ((0,), (3, 2, 1))
 AHEAD = 3
 COARSE = (3, 2, 1, 0)
 CHUNK = 4
@@ -534,8 +535,9 @@
 
     def received(halos, left, new, weight, mode="plain", extra=()):
         blocks_in = matrix if turned is None else turned
-        for step, buffers in enumerate(STEPS):
-            final = step == len(STEPS) - 1
+        steps = SPREAD_STEPS if mode == "spread" else STEPS
+        for step, buffers in enumerate(steps):
+            final = step == len(steps) - 1
             outs, kept = [field, small if mode == "restrict" else field], "VV"
             aliases = {1: 0, 2: 1}
             if mode == "last" and final:

time: 65.7 us -> 64.8 us (0.986)
  waiting for transfers between devices: 6.31 us -> 4.82 us
  starting transfers between devices: 37.2 us -> 38.1 us
    ppermute x36, waiting for transfers between devices: 6.31 us -> 4.82 us  [exchange(): return [lax.ppermute(x, AXES, perm) for x, perm in zip(payloads, perms)]]
    ppermute x36, starting transfers between devices: 37.2 us -> 38.1 us  [exchange(): return [lax.ppermute(x, AXES, perm) for x, perm in zip(payloads, perms)]]
  transfers between devices with their start and end apart: 36 -> 36, of which waited for: 12 -> 11; matrix products, arithmetic and copies ran while one was open for 0% -> 0% of each run, Pallas kernels for 22% -> 22%
where the time goes in v5:
time: 64.8 us; the launch traced here: 64.5 us
  starting transfers between devices  38.1 us (59%)
  Pallas kernels  20.7 us (32%)
  waiting for transfers between devices  4.82 us (7%)
  between operations  0.9 us (1%)
    ppermute x36, starting transfers between devices, exchange(): return [lax.ppermute(x, AXES, perm) for x, perm in zip(payloads, perms)]  38.1 us
    pallas_call x24, Pallas kernels, call(): pl.pallas_call(functools.partial(kernel, **named), out_shape=[forms[c](sh...  20.7 us
    ppermute x36, waiting for transfers between devices, exchange(): return [lax.ppermute(x, AXES, perm) for x, perm in zip(payloads, perms)]  4.82 us
  transfers between devices with their start and end apart: 36, of which 11 were waited for; matrix products, arithmetic and copies ran while one was open for 0% of the time, Pallas kernels for 22%

profile of v5, /device:TPU:0, one launch (start us, length us, event | category | flops | bytes accessed | tf_op | source)
XLA Modules:
  0.0 64.5 jit_solution(4846332488552690150)
XLA Ops:
  0.6 1.2 %shard_map.86 = (f32[72,512]{1,0:T(8,128)S(1)}, f32[72,512]{1,0:T(8,128)S(1)}, f32[72,512]{1,0:T(8,128)S(1)}, f32[72,512]{1,0:T(8,128)S(1)}, f32[64,2048]{1,0:T(...) custom-call(f32[64,2048]{1,0:T(8,128)} %guess.1, s32[1,16]{1,0:T(1,128)} %lists.1, s32[5,16]{1,0:T(8,128)} %bitcast.8, ...), custom_call_target="tpu_custom_call" | custom-call | bytes 4194304 | tf_op jit(solution)/shard_map/pallas_call | solution.py:512
  1.8 3.4 %collective-permute-start = (f32[72,512]{1,0:T(8,128)S(1)}, f32[72,512]{1,0:T(8,128)S(1)}, u32[]{:S(2)}, u32[]{:S(2)}) collective-permute-start(f32[72,512]{1,0:T(8,128)S(1)} %get-tuple-element.98), channel_id=1, source_target_pairs={{0,7},{1,9},{2,10},{3,4},{4,3},{5,13},{6,14},{7,0},{8,15},{9,1},{1... | collective-permute-start | bytes 442376 | tf_op jit(solution)/shard_map/ppermute | solution.py:526
  5.2 1.6 %collective-permute-start.1 = (f32[72,512]{1,0:T(8,128)S(1)}, f32[72,512]{1,0:T(8,128)S(1)}, u32[]{:S(2)}, u32[]{:S(2)}) collective-permute-start(f32[72,512]{1,0:T(8,128)S(1)} %get-tuple-element.101), channel_id=1, source_target_pairs={{0,8},{1,2},{2,1},{3,11},{4,12},{5,6},{6,5},{7,15},{8,0},{9,17},{1... | collective-permute-start | bytes 442376 | tf_op jit(solution)/shard_map/ppermute | solution.py:526
  7.3 2.9 %shard_map.87 = (f32[64,2048]{1,0:T(8,128)S(1)}, f32[64,2048]{1,0:T(8,128)S(1)}, s32[446]{0:T(512)S(4)}, f32[8,2048]{1,0:T(8,128)S(1)}, bf16[80,128,128]{2,1,0:T(8,128)(2,1)S(1)}) custom-call(s32[1,16]{1,0:T(1,128)S(4)} %get-tuple-element.90.lists, s32[5,16]{1,0:T(8,128)S(4)} %get-tuple-element.91.columns, f32[64,2048]{1,0:T(8,128)S(1)} %get-tuple-element.92.field.iterate, ...), custom_call_target="tpu_custom_call" | custom-call | flops 335544320 | bytes 4194304 | tf_op jit(solution)/shard_map/pallas_call | solution.py:512
  11.1 1.6 %collective-permute-start.4 = (f32[64,512]{1,0:T(8,128)S(1)}, f32[64,512]{1,0:T(8,128)S(1)}, u32[]{:S(2)}, u32[]{:S(2)}) collective-permute-start(f32[64,512]{1,0:T(8,128)S(1)} %get-tuple-element.109), channel_id=1, source_target_pairs={{0,7},{1,9},{2,10},{3,4},{4,3},{5,13},{6,14},{7,0},{8,15},{9,1},{1... | collective-permute-start | bytes 393224 | tf_op jit(solution)/shard_map/ppermute | solution.py:526
  12.6 2.3 %collective-permute-start.5 = (f32[64,512]{1,0:T(8,128)S(1)}, f32[64,512]{1,0:T(8,128)S(1)}, u32[]{:S(2)}, u32[]{:S(2)}) collective-permute-start(f32[64,512]{1,0:T(8,128)S(1)} %get-tuple-element.112), channel_id=1, source_target_pairs={{0,8},{1,2},{2,1},{3,11},{4,12},{5,6},{6,5},{7,15},{8,0},{9,17},{1... | collective-permute-start | bytes 393224 | tf_op jit(solution)/shard_map/ppermute | solution.py:526
  15.4 2.1 %shard_map.90 = (f32[64,2048]{1,0:T(8,128)S(1)}, f32[64,2048]{1,0:T(8,128)S(1)}, f32[64,2048]{1,0:T(8,128)S(1)}, bf16[80,128,128]{2,1,0:T(8,128)(2,1)S(1)}, bf16...) custom-call(s32[446]{0:T(512)S(4)} %get-tuple-element.93.table, ...), custom_call_target="tpu_custom_call" | custom-call | flops 335544320 | bytes 4194304 | tf_op jit(solution)/shard_map/pallas_call | solution.py:512
  18.4 1.9 %collective-permute-start.8 = (f32[64,512]{1,0:T(8,128)S(1)}, f32[64,512]{1,0:T(8,128)S(1)}, u32[]{:S(2)}, u32[]{:S(2)}) collective-permute-start(f32[64,512]{1,0:T(8,128)S(1)} %get-tuple-element.121), channel_id=1, source_target_pairs={{0,7},{1,9},{2,10},{3,4},{4,3},{5,13},{6,14},{7,0},{8,15},{9,1},{1... | collective-permute-start | bytes 393224 | tf_op jit(solution)/shard_map/ppermute | solution.py:526
  20.3 2.1 %collective-permute-start.9 = (f32[64,512]{1,0:T(8,128)S(1)}, f32[64,512]{1,0:T(8,128)S(1)}, u32[]{:S(2)}, u32[]{:S(2)}) collective-permute-start(f32[64,512]{1,0:T(8,128)S(1)} %get-tuple-element.124), channel_id=1, source_target_pairs={{0,8},{1,2},{2,1},{3,11},{4,12},{5,6},{6,5},{7,15},{8,0},{9,17},{1... | collective-permute-start | bytes 393224 | tf_op jit(solution)/shard_map/ppermute | solution.py:526
  22.9 2.1 %shard_map.93 = (f32[64,2048]{1,0:T(8,128)S(1)}, f32[64,2048]{1,0:T(8,128)S(1)}, f32[64,2048]{1,0:T(8,128)S(1)}, bf16[128,2048]{1,0:T(8,128)(2,1)S(1)}, bf16[128,2048]{1,0:T(8,128)(2,1)S(1)}) custom-call(s32[446]{0:T(512)S(4)} %get-tuple-element.93.table, f32[64,2048]{1,0:T(8,128)S(1)} %get-tuple-element.115.update, ...), custom_call_target="tpu_custom_call" | custom-call | flops 335544320 | bytes 4194304 | tf_op jit(solution)/shard_map/pallas_call | solution.py:512
  25.8 1.5 %collective-permute-start.12 = (f32[64,512]{1,0:T(8,128)S(1)}, f32[64,512]{1,0:T(8,128)S(1)}, u32[]{:S(2)}, u32[]{:S(2)}) collective-permute-start(f32[64,512]{1,0:T(8,128)S(1)} %get-tuple-element.132), channel_id=1, source_target_pairs={{0,7},{1,9},{2,10},{3,4},{4,3},{5,13},{6,14},{7,0},{8,15},{9,1},{1... | collective-permute-start | bytes 393224 | tf_op jit(solution)/shard_map/ppermute | solution.py:526
  27.3 2.0 %collective-permute-start.13 = (f32[64,512]{1,0:T(8,128)S(1)}, f32[64,512]{1,0:T(8,128)S(1)}, u32[]{:S(2)}, u32[]{:S(2)}) collective-permute-start(f32[64,512]{1,0:T(8,128)S(1)} %get-tuple-element.136), channel_id=1, source_target_pairs={{0,8},{1,2},{2,1},{3,11},{4,12},{5,6},{6,5},{7,15},{8,0},{9,17},{1... | collective-permute-start | bytes 393224 | tf_op jit(solution)/shard_map/ppermute | solution.py:526
  29.9 1.5 %shard_map.96 = (f32[64,2048]{1,0:T(8,128)S(1)}, f32[64,128]{1,0:T(8,128)S(1)}, f32[64,2048]{1,0:T(8,128)S(1)}) custom-call(s32[446]{0:T(512)S(4)} %get-tuple-element.93.table, f32[64,2048]{1,0:T(8,128)S(1)} %get-tuple-element.127.update, f32[64,2048]{1,0:T(8,128)S(1)} %get-tuple-element.128.residual, f32[64,2048]{1,0:T(8,128)S(1)} %get-tuple-element.129.iterate, ...), custom_call_target="tpu_custom_call" | custom-call | flops 335544320 | bytes 4194304 | tf_op jit(solution)/shard_map/pallas_call | solution.py:512
  33.1 1.5 %collective-permute-start.19 = (f32[64,128]{1,0:T(8,128)S(1)}, f32[64,128]{1,0:T(8,128)S(1)}, u32[]{:S(2)}, u32[]{:S(2)}) collective-permute-start(f32[64,128]{1,0:T(8,128)S(1)} %get-tuple-element.139.update.iterate), channel_id=1, source_target_pairs={{0,7},{1,9},{2,10},{3,4},{4,3},{5,13},{6,14},{7,0},{8,15},{9,1},{1... | collective-permute-start | bytes 98312 | tf_op jit(solution)/shard_map/ppermute | solution.py:526
  34.6 2.1 %collective-permute-start.18 = (f32[64,128]{1,0:T(8,128)S(1)}, f32[64,128]{1,0:T(8,128)S(1)}, u32[]{:S(2)}, u32[]{:S(2)}) collective-permute-start(f32[64,128]{1,0:T(8,128)S(1)} %get-tuple-element.139.update.iterate), channel_id=1, source_target_pairs={{0,8},{1,2},{2,1},{3,11},{4,12},{5,6},{6,5},{7,15},{8,0},{9,17},{1... | collective-permute-start | bytes 98312 | tf_op jit(solution)/shard_map/ppermute | solution.py:526
  37.4 1.2 %collective-permute-done.18.h2 = f32[64,128]{1,0:T(8,128)S(1)} collective-permute-done((f32[64,128]{1,0:T(8,128)S(1)}, f32[64,128]{1,0:T(8,128)S(1)}, u32[]{:S(2)}, u32[]{:S(2)}) %collective-permute-start.18) | collective-permute-done | bytes 32800 | tf_op jit(solution)/shard_map/ppermute | solution.py:526
  39.2 2.1 %collective-permute-start.22 = (f32[64,128]{1,0:T(8,128)S(1)}, f32[64,128]{1,0:T(8,128)S(1)}, u32[]{:S(2)}, u32[]{:S(2)}) collective-permute-start(f32[64,128]{1,0:T(8,128)S(1)} %get-tuple-element.143.update), channel_id=1, source_target_pairs={{0,8},{1,2},{2,1},{3,11},{4,12},{5,6},{6,5},{7,15},{8,0},{9,17},{1... | collective-permute-start | bytes 98312 | tf_op jit(solution)/shard_map/ppermute | solution.py:526
  43.7 1.3 %collective-permute-start.24 = (f32[64,128]{1,0:T(8,128)S(1)}, f32[64,128]{1,0:T(8,128)S(1)}, u32[]{:S(2)}, u32[]{:S(2)}) collective-permute-start(f32[64,128]{1,0:T(8,128)S(1)} %shard_map.100.correction), channel_id=1, source_target_pairs={{0,7},{1,9},{2,10},{3,4},{4,3},{5,13},{6,14},{7,0},{8,15},{9,1},{1... | collective-permute-start | bytes 98312 | tf_op jit(solution)/shard_map/ppermute | solution.py:526
  45.0 2.3 %collective-permute-start.27 = (f32[64,128]{1,0:T(8,128)S(1)}, f32[64,128]{1,0:T(8,128)S(1)}, u32[]{:S(2)}, u32[]{:S(2)}) collective-permute-start(f32[64,128]{1,0:T(8,128)S(1)} %shard_map.100.correction), channel_id=1, source_target_pairs={{0,8},{1,2},{2,1},{3,11},{4,12},{5,6},{6,5},{7,15},{8,0},{9,17},{1... | collective-permute-start | bytes 98312 | tf_op jit(solution)/shard_map/ppermute | solution.py:526
  50.9 2.0 %collective-permute-start.29 = (f32[64,512]{1,0:T(8,128)S(1)}, f32[64,512]{1,0:T(8,128)S(1)}, u32[]{:S(2)}, u32[]{:S(2)}) collective-permute-start(f32[64,512]{1,0:T(8,128)S(1)} %get-tuple-element.163), channel_id=1, source_target_pairs={{0,8},{1,2},{2,1},{3,11},{4,12},{5,6},{6,5},{7,15},{8,0},{9,17},{1... | collective-permute-start | bytes 393224 | tf_op jit(solution)/shard_map/ppermute | solution.py:526
  53.4 1.2 %shard_map.104 = (f32[64,2048]{1,0:T(8,128)S(1)}, f32[64,2048]{1,0:T(8,128)S(1)}, f32[64,2048]{1,0:T(8,128)S(1)}) custom-call(s32[446]{0:T(512)S(4)} %get-tuple-element.93.table, f32[64,2048]{1,0:T(8,128)S(1)} %get-tuple-element.155.update, f32[64,2048]{1,0:T(8,128)S(1)} %get-tuple-element.156.residual, f32[64,2048]{1,0:T(8,128)S(1)} %get-tuple-element.157.iterate, ...), custom_call_target="tpu_custom_call" | custom-call | flops 335544320 | bytes 4194304 | tf_op jit(solution)/shard_map/pallas_call | solution.py:512
  56.4 1.9 %collective-permute-start.32 = (f32[64,512]{1,0:T(8,128)S(1)}, f32[64,512]{1,0:T(8,128)S(1)}, u32[]{:S(2)}, u32[]{:S(2)}) collective-permute-start(f32[64,512]{1,0:T(8,128)S(1)} %get-tuple-element.171), channel_id=1, source_target_pairs={{0,7},{1,9},{2,10},{3,4},{4,3},{5,13},{6,14},{7,0},{8,15},{9,1},{1... | collective-permute-start | bytes 393224 | tf_op jit(solution)/shard_map/ppermute | solution.py:526
  58.3 2.2 %collective-permute-start.33 = (f32[64,512]{1,0:T(8,128)S(1)}, f32[64,512]{1,0:T(8,128)S(1)}, u32[]{:S(2)}, u32[]{:S(2)}) collective-permute-start(f32[64,512]{1,0:T(8,128)S(1)} %get-tuple-element.174), channel_id=1, source_target_pairs={{0,8},{1,2},{2,1},{3,11},{4,12},{5,6},{6,5},{7,15},{8,0},{9,17},{1... | collective-permute-start | bytes 393224 | tf_op jit(solution)/shard_map/ppermute | solution.py:526
  61.0 1.9 %shard_map.107 = (f32[64,2048]{1,0:T(8,128)S(1)}, f32[64,2048]{1,0:T(8,128)S(1)}, f32[64,2048]{1,0:T(8,128)}) custom-call(s32[446]{0:T(512)S(4)} %get-tuple-element.93.table, f32[64,2048]{1,0:T(8,128)S(1)} %get-tuple-element.166.update, f32[64,2048]{1,0:T(8,128)S(1)} %get-tuple-element.167.residual, f32[64,2048]{1,0:T(8,128)S(1)} %get-tuple-element.168.iterate, ...), custom_call_target="tpu_custom_call" | custom-call | flops 335544320 | bytes 4194304 | tf_op jit(solution)/shard_map/pallas_call | solution.py:512
  (72 shorter events, 17.9 us)
Async XLA Ops:
  1.8 8.4 %collective-permute-start = (f32[72,512]{1,0:T(8,128)S(1)}, f32[72,512]{1,0:T(8,128)S(1)}, u32[]{:S(2)}, u32[]{:S(2)}) collective-permute-start(f32[72,512]{1,0:T(8,128)S(1)} %get-tuple-element.98), channel_id=1, source_target_pairs={{0,7},{1,9},{2,10},{3,4},{4,3},{5,13},{6,14},{7,0},{8,15},{9,1},{1... | collective-permute-start | bytes 442376 | tf_op jit(solution)/shard_map/ppermute | solution.py:526
  5.2 5.2 %collective-permute-start.1 = (f32[72,512]{1,0:T(8,128)S(1)}, f32[72,512]{1,0:T(8,128)S(1)}, u32[]{:S(2)}, u32[]{:S(2)}) collective-permute-start(f32[72,512]{1,0:T(8,128)S(1)} %get-tuple-element.101), channel_id=1, source_target_pairs={{0,8},{1,2},{2,1},{3,11},{4,12},{5,6},{6,5},{7,15},{8,0},{9,17},{1... | collective-permute-start | bytes 442376 | tf_op jit(solution)/shard_map/ppermute | solution.py:526
  6.8 3.7 %collective-permute-start.2 = (f32[72,512]{1,0:T(8,128)S(1)}, f32[72,512]{1,0:T(8,128)S(1)}, u32[]{:S(2)}, u32[]{:S(2)}) collective-permute-start(f32[72,512]{1,0:T(8,128)S(1)} %get-tuple-element.102), channel_id=1, source_target_pairs={{0,1},{1,0},{2,3},{3,2},{4,5},{5,4},{6,7},{7,6},{8,16},{9,10},{10,... | collective-permute-start | bytes 442376 | tf_op jit(solution)/shard_map/ppermute | solution.py:526
  6.8 3.7 %collective-permute-start.3 = (f32[72,512]{1,0:T(8,128)S(1)}, f32[72,512]{1,0:T(8,128)S(1)}, u32[]{:S(2)}, u32[]{:S(2)}) collective-permute-start(f32[72,512]{1,0:T(8,128)S(1)} %get-tuple-element.103), channel_id=1, source_target_pairs={{0,1},{1,0},{2,3},{3,2},{4,5},{5,4},{6,7},{7,6},{8,9},{9,8},{10,11... | collective-permute-start | bytes 442376 | tf_op jit(solution)/shard_map/ppermute | solution.py:526
  11.1 6.5 %collective-permute-start.4 = (f32[64,512]{1,0:T(8,128)S(1)}, f32[64,512]{1,0:T(8,128)S(1)}, u32[]{:S(2)}, u32[]{:S(2)}) collective-permute-start(f32[64,512]{1,0:T(8,128)S(1)} %get-tuple-element.109), channel_id=1, source_target_pairs={{0,7},{1,9},{2,10},{3,4},{4,3},{5,13},{6,14},{7,0},{8,15},{9,1},{1... | collective-permute-start | bytes 393224 | tf_op jit(solution)/shard_map/ppermute | solution.py:526
  12.6 5.3 %collective-permute-start.5 = (f32[64,512]{1,0:T(8,128)S(1)}, f32[64,512]{1,0:T(8,128)S(1)}, u32[]{:S(2)}, u32[]{:S(2)}) collective-permute-start(f32[64,512]{1,0:T(8,128)S(1)} %get-tuple-element.112), channel_id=1, source_target_pairs={{0,8},{1,2},{2,1},{3,11},{4,12},{5,6},{6,5},{7,15},{8,0},{9,17},{1... | collective-permute-start | bytes 393224 | tf_op jit(solution)/shard_map/ppermute | solution.py:526
  14.9 3.1 %collective-permute-start.6 = (f32[64,512]{1,0:T(8,128)S(1)}, f32[64,512]{1,0:T(8,128)S(1)}, u32[]{:S(2)}, u32[]{:S(2)}) collective-permute-start(f32[64,512]{1,0:T(8,128)S(1)} %get-tuple-element.113), channel_id=1, source_target_pairs={{0,1},{1,0},{2,3},{3,2},{4,5},{5,4},{6,7},{7,6},{8,16},{9,10},{10,... | collective-permute-start | bytes 393224 | tf_op jit(solution)/shard_map/ppermute | solution.py:526
  14.9 3.1 %collective-permute-start.7 = (f32[64,512]{1,0:T(8,128)S(1)}, f32[64,512]{1,0:T(8,128)S(1)}, u32[]{:S(2)}, u32[]{:S(2)}) collective-permute-start(f32[64,512]{1,0:T(8,128)S(1)} %get-tuple-element.114), channel_id=1, source_target_pairs={{0,1},{1,0},{2,3},{3,2},{4,5},{5,4},{6,7},{7,6},{8,9},{9,8},{10,11... | collective-permute-start | bytes 393224 | tf_op jit(solution)/shard_map/ppermute | solution.py:526
  18.4 6.6 %collective-permute-start.8 = (f32[64,512]{1,0:T(8,128)S(1)}, f32[64,512]{1,0:T(8,128)S(1)}, u32[]{:S(2)}, u32[]{:S(2)}) collective-permute-start(f32[64,512]{1,0:T(8,128)S(1)} %get-tuple-element.121), channel_id=1, source_target_pairs={{0,7},{1,9},{2,10},{3,4},{4,3},{5,13},{6,14},{7,0},{8,15},{9,1},{1... | collective-permute-start | bytes 393224 | tf_op jit(solution)/shard_map/ppermute | solution.py:526
  20.3 5.0 %collective-permute-start.9 = (f32[64,512]{1,0:T(8,128)S(1)}, f32[64,512]{1,0:T(8,128)S(1)}, u32[]{:S(2)}, u32[]{:S(2)}) collective-permute-start(f32[64,512]{1,0:T(8,128)S(1)} %get-tuple-element.124), channel_id=1, source_target_pairs={{0,8},{1,2},{2,1},{3,11},{4,12},{5,6},{6,5},{7,15},{8,0},{9,17},{1... | collective-permute-start | bytes 393224 | tf_op jit(solution)/shard_map/ppermute | solution.py:526
  25.8 5.6 %collective-permute-start.12 = (f32[64,512]{1,0:T(8,128)S(1)}, f32[64,512]{1,0:T(8,128)S(1)}, u32[]{:S(2)}, u32[]{:S(2)}) collective-permute-start(f32[64,512]{1,0:T(8,128)S(1)} %get-tuple-element.132), channel_id=1, source_target_pairs={{0,7},{1,9},{2,10},{3,4},{4,3},{5,13},{6,14},{7,0},{8,15},{9,1},{1... | collective-permute-start | bytes 393224 | tf_op jit(solution)/shard_map/ppermute | solution.py:526
  27.3 5.0 %collective-permute-start.13 = (f32[64,512]{1,0:T(8,128)S(1)}, f32[64,512]{1,0:T(8,128)S(1)}, u32[]{:S(2)}, u32[]{:S(2)}) collective-permute-start(f32[64,512]{1,0:T(8,128)S(1)} %get-tuple-element.136), channel_id=1, source_target_pairs={{0,8},{1,2},{2,1},{3,11},{4,12},{5,6},{6,5},{7,15},{8,0},{9,17},{1... | collective-permute-start | bytes 393224 | tf_op jit(solution)/shard_map/ppermute | solution.py:526
  29.4 3.0 %collective-permute-start.14 = (f32[64,512]{1,0:T(8,128)S(1)}, f32[64,512]{1,0:T(8,128)S(1)}, u32[]{:S(2)}, u32[]{:S(2)}) collective-permute-start(f32[64,512]{1,0:T(8,128)S(1)} %get-tuple-element.137), channel_id=1, source_target_pairs={{0,1},{1,0},{2,3},{3,2},{4,5},{5,4},{6,7},{7,6},{8,16},{9,10},{10,... | collective-permute-start | bytes 393224 | tf_op jit(solution)/shard_map/ppermute | solution.py:526
  33.1 4.3 %collective-permute-start.19 = (f32[64,128]{1,0:T(8,128)S(1)}, f32[64,128]{1,0:T(8,128)S(1)}, u32[]{:S(2)}, u32[]{:S(2)}) collective-permute-start(f32[64,128]{1,0:T(8,128)S(1)} %get-tuple-element.139.update.iterate), channel_id=1, source_target_pairs={{0,7},{1,9},{2,10},{3,4},{4,3},{5,13},{6,14},{7,0},{8,15},{9,1},{1... | collective-permute-start | bytes 98312 | tf_op jit(solution)/shard_map/ppermute | solution.py:526
  34.6 4.0 %collective-permute-start.18 = (f32[64,128]{1,0:T(8,128)S(1)}, f32[64,128]{1,0:T(8,128)S(1)}, u32[]{:S(2)}, u32[]{:S(2)}) collective-permute-start(f32[64,128]{1,0:T(8,128)S(1)} %get-tuple-element.139.update.iterate), channel_id=1, source_target_pairs={{0,8},{1,2},{2,1},{3,11},{4,12},{5,6},{6,5},{7,15},{8,0},{9,17},{1... | collective-permute-start | bytes 98312 | tf_op jit(solution)/shard_map/ppermute | solution.py:526
  38.9 4.3 %collective-permute-start.23 = (f32[64,128]{1,0:T(8,128)S(1)}, f32[64,128]{1,0:T(8,128)S(1)}, u32[]{:S(2)}, u32[]{:S(2)}) collective-permute-start(f32[64,128]{1,0:T(8,128)S(1)} %get-tuple-element.143.update), channel_id=1, source_target_pairs={{0,7},{1,9},{2,10},{3,4},{4,3},{5,13},{6,14},{7,0},{8,15},{9,1},{1... | collective-permute-start | bytes 98312 | tf_op jit(solution)/shard_map/ppermute | solution.py:526
  39.2 4.0 %collective-permute-start.22 = (f32[64,128]{1,0:T(8,128)S(1)}, f32[64,128]{1,0:T(8,128)S(1)}, u32[]{:S(2)}, u32[]{:S(2)}) collective-permute-start(f32[64,128]{1,0:T(8,128)S(1)} %get-tuple-element.143.update), channel_id=1, source_target_pairs={{0,8},{1,2},{2,1},{3,11},{4,12},{5,6},{6,5},{7,15},{8,0},{9,17},{1... | collective-permute-start | bytes 98312 | tf_op jit(solution)/shard_map/ppermute | solution.py:526
  43.7 5.1 %collective-permute-start.24 = (f32[64,128]{1,0:T(8,128)S(1)}, f32[64,128]{1,0:T(8,128)S(1)}, u32[]{:S(2)}, u32[]{:S(2)}) collective-permute-start(f32[64,128]{1,0:T(8,128)S(1)} %shard_map.100.correction), channel_id=1, source_target_pairs={{0,7},{1,9},{2,10},{3,4},{4,3},{5,13},{6,14},{7,0},{8,15},{9,1},{1... | collective-permute-start | bytes 98312 | tf_op jit(solution)/shard_map/ppermute | solution.py:526
  45.0 4.2 %collective-permute-start.27 = (f32[64,128]{1,0:T(8,128)S(1)}, f32[64,128]{1,0:T(8,128)S(1)}, u32[]{:S(2)}, u32[]{:S(2)}) collective-permute-start(f32[64,128]{1,0:T(8,128)S(1)} %shard_map.100.correction), channel_id=1, source_target_pairs={{0,8},{1,2},{2,1},{3,11},{4,12},{5,6},{6,5},{7,15},{8,0},{9,17},{1... | collective-permute-start | bytes 98312 | tf_op jit(solution)/shard_map/ppermute | solution.py:526
  49.9 5.6 %collective-permute-start.28 = (f32[64,512]{1,0:T(8,128)S(1)}, f32[64,512]{1,0:T(8,128)S(1)}, u32[]{:S(2)}, u32[]{:S(2)}) collective-permute-start(f32[64,512]{1,0:T(8,128)S(1)} %get-tuple-element.160), channel_id=1, source_target_pairs={{0,7},{1,9},{2,10},{3,4},{4,3},{5,13},{6,14},{7,0},{8,15},{9,1},{1... | collective-permute-start | bytes 393224 | tf_op jit(solution)/shard_map/ppermute | solution.py:526
  50.9 5.0 %collective-permute-start.29 = (f32[64,512]{1,0:T(8,128)S(1)}, f32[64,512]{1,0:T(8,128)S(1)}, u32[]{:S(2)}, u32[]{:S(2)}) collective-permute-start(f32[64,512]{1,0:T(8,128)S(1)} %get-tuple-element.163), channel_id=1, source_target_pairs={{0,8},{1,2},{2,1},{3,11},{4,12},{5,6},{6,5},{7,15},{8,0},{9,17},{1... | collective-permute-start | bytes 393224 | tf_op jit(solution)/shard_map/ppermute | solution.py:526
  52.9 3.0 %collective-permute-start.30 = (f32[64,512]{1,0:T(8,128)S(1)}, f32[64,512]{1,0:T(8,128)S(1)}, u32[]{:S(2)}, u32[]{:S(2)}) collective-permute-start(f32[64,512]{1,0:T(8,128)S(1)} %get-tuple-element.164), channel_id=1, source_target_pairs={{0,1},{1,0},{2,3},{3,2},{4,5},{5,4},{6,7},{7,6},{8,16},{9,10},{10,... | collective-permute-start | bytes 393224 | tf_op jit(solution)/shard_map/ppermute | solution.py:526
  56.4 6.5 %collective-permute-start.32 = (f32[64,512]{1,0:T(8,128)S(1)}, f32[64,512]{1,0:T(8,128)S(1)}, u32[]{:S(2)}, u32[]{:S(2)}) collective-permute-start(f32[64,512]{1,0:T(8,128)S(1)} %get-tuple-element.171), channel_id=1, source_target_pairs={{0,7},{1,9},{2,10},{3,4},{4,3},{5,13},{6,14},{7,0},{8,15},{9,1},{1... | collective-permute-start | bytes 393224 | tf_op jit(solution)/shard_map/ppermute | solution.py:526
  58.3 5.1 %collective-permute-start.33 = (f32[64,512]{1,0:T(8,128)S(1)}, f32[64,512]{1,0:T(8,128)S(1)}, u32[]{:S(2)}, u32[]{:S(2)}) collective-permute-start(f32[64,512]{1,0:T(8,128)S(1)} %get-tuple-element.174), channel_id=1, source_target_pairs={{0,8},{1,2},{2,1},{3,11},{4,12},{5,6},{6,5},{7,15},{8,0},{9,17},{1... | collective-permute-start | bytes 393224 | tf_op jit(solution)/shard_map/ppermute | solution.py:526
  (12 other events, 27.4 us)

commit v6 on v5

--- a/solution.py
+++ b/solution.py
@@ -306,7 +306,7 @@
 
 def local_and_coarse_kernel(
     table, update, residual, iterate, inverse, matrix, groups, coarse, h0, h1, h2, h3,
-    left, new, iterate_out, turned, onehot, names, coarse_high, coarse_low, coarse_inverse, wide, brought, cells, sems, *, size, lay, weights,
+    left, new, iterate_out, turned, onehot, cells_turned, names, coarse_high, coarse_low, coarse_inverse, wide, brought, cells, sems, *, size, lay, weights,
 ):
     copies = [
         pltpu.make_async_copy(coarse, brought, sems.at[0]),
@@ -331,6 +331,10 @@
     onehot[...] = jnp.where(
         lax.broadcasted_iota(i32, onehot.shape, 0) == cells[...], 1.0, 0.0
     ).astype(bf16)
+    identity = jnp.where(square_mask(size), 1.0, 0.0).astype(bf16)
+    for g in range(lay.blocks):
+        at = slice(g * size, (g + 1) * size)
+        cells_turned[at, :] = dot_nt(identity, onehot[:, at]).astype(bf16)
     coarse_inverse[...] = jnp.broadcast_to(
         1.0 / diagonal_row(brought[0], square_mask(size)), (8, size)
     )
@@ -418,7 +422,7 @@
                 new[:, at] = new[:, at] - scaled[0:1, at] * product
         if mode == "restrict":
             new[...] = new[...] - sum(
-                halves(dot_nt(stacked(product), onehot[:, at])) for at, product in found
+                halves(dot_nn(stacked(product), onehot[at, :])) for at, product in found
             )
 
     for_received(table, lay, buffers, matrix, wide, size, dot_nn if turned else dot_nt, use)
@@ -587,7 +591,7 @@
     turned = None
     residual, update, *payloads = received(halos, left, new, None)
     halos = exchange(payloads)
-    left, new, iterate, turned, onehot, names, coarse_high, coarse_low, coarse_inverse = call(
+    left, new, iterate, turned, onehot, cells_turned, names, coarse_high, coarse_low, coarse_inverse = call(
         local_and_coarse_kernel,
         [table, update, residual, guess, inverse, matrix, groups, coarse] + first_halos,
         [
@@ -596,6 +600,7 @@
             field,
             (stored.shape, bf16),
             ((size, width), bf16),
+            ((width, size), bf16),
             ((size, 4 * halo_width), bf16),
             ((size, 5 * size), bf16),
             ((size, 5 * size), bf16),
@@ -620,7 +625,7 @@
     halos = exchange(payloads)
     left, new, iterate = local(update, residual, iterate, None, "restrict", (onehot,))
     leftover, coarse_left, c = received(
-        halos, left, new, None, "restrict", (onehot, coarse_inverse)
+        halos, left, new, None, "restrict", (cells_turned, coarse_inverse)
     )
     correction = c
     for i, weight in enumerate(weights):

time: 64.8 us -> 64.6 us (level)
  transfers between devices with their start and end apart: 36 -> 36, of which waited for: 11 -> 9; matrix products, arithmetic and copies ran while one was open for 0% -> 0% of each run, Pallas kernels for 22% -> 23%
where the time goes in v6:
time: 64.6 us; the launch traced here: 64.4 us
  starting transfers between devices  37.8 us (59%)
  Pallas kernels  21 us (33%)
  waiting for transfers between devices  4.81 us (7%)
  between operations  0.91 us (1%)
    ppermute x36, starting transfers between devices, exchange(): return [lax.ppermute(x, AXES, perm) for x, perm in zip(payloads, perms)]  37.8 us
    pallas_call x24, Pallas kernels, call(): pl.pallas_call(functools.partial(kernel, **named), out_shape=[forms[c](sh...  21 us
    ppermute x36, waiting for transfers between devices, exchange(): return [lax.ppermute(x, AXES, perm) for x, perm in zip(payloads, perms)]  4.81 us
  transfers between devices with their start and end apart: 36, of which 9 were waited for; matrix products, arithmetic and copies ran while one was open for 0% of the time, Pallas kernels for 23%

profile of v6, /device:TPU:0, one launch (start us, length us, event | category | flops | bytes accessed | tf_op | source)
XLA Modules:
  0.0 64.4 jit_solution(10237654719794480896)
XLA Ops:
  0.6 1.2 %shard_map.86 = (f32[72,512]{1,0:T(8,128)S(1)}, f32[72,512]{1,0:T(8,128)S(1)}, f32[72,512]{1,0:T(8,128)S(1)}, f32[72,512]{1,0:T(8,128)S(1)}, f32[64,2048]{1,0:T(...) custom-call(f32[64,2048]{1,0:T(8,128)} %guess.1, s32[1,16]{1,0:T(1,128)} %lists.1, s32[5,16]{1,0:T(8,128)} %bitcast.8, ...), custom_call_target="tpu_custom_call" | custom-call | bytes 4194304 | tf_op jit(solution)/shard_map/pallas_call | solution.py:516
  1.8 3.4 %collective-permute-start = (f32[72,512]{1,0:T(8,128)S(1)}, f32[72,512]{1,0:T(8,128)S(1)}, u32[]{:S(2)}, u32[]{:S(2)}) collective-permute-start(f32[72,512]{1,0:T(8,128)S(1)} %get-tuple-element.99), channel_id=1, source_target_pairs={{0,7},{1,9},{2,10},{3,4},{4,3},{5,13},{6,14},{7,0},{8,15},{9,1},{1... | collective-permute-start | bytes 442376 | tf_op jit(solution)/shard_map/ppermute | solution.py:530
  5.2 1.6 %collective-permute-start.1 = (f32[72,512]{1,0:T(8,128)S(1)}, f32[72,512]{1,0:T(8,128)S(1)}, u32[]{:S(2)}, u32[]{:S(2)}) collective-permute-start(f32[72,512]{1,0:T(8,128)S(1)} %get-tuple-element.102), channel_id=1, source_target_pairs={{0,8},{1,2},{2,1},{3,11},{4,12},{5,6},{6,5},{7,15},{8,0},{9,17},{1... | collective-permute-start | bytes 442376 | tf_op jit(solution)/shard_map/ppermute | solution.py:530
  7.3 2.9 %shard_map.87 = (f32[64,2048]{1,0:T(8,128)S(1)}, f32[64,2048]{1,0:T(8,128)S(1)}, s32[446]{0:T(512)S(4)}, f32[8,2048]{1,0:T(8,128)S(1)}, bf16[80,128,128]{2,1,0:T(8,128)(2,1)S(1)}) custom-call(s32[1,16]{1,0:T(1,128)S(4)} %get-tuple-element.91.lists, s32[5,16]{1,0:T(8,128)S(4)} %get-tuple-element.92.columns, f32[64,2048]{1,0:T(8,128)S(1)} %get-tuple-element.93.field.iterate, ...), custom_call_target="tpu_custom_call" | custom-call | flops 335544320 | bytes 4194304 | tf_op jit(solution)/shard_map/pallas_call | solution.py:516
  11.1 1.6 %collective-permute-start.4 = (f32[64,512]{1,0:T(8,128)S(1)}, f32[64,512]{1,0:T(8,128)S(1)}, u32[]{:S(2)}, u32[]{:S(2)}) collective-permute-start(f32[64,512]{1,0:T(8,128)S(1)} %get-tuple-element.110), channel_id=1, source_target_pairs={{0,7},{1,9},{2,10},{3,4},{4,3},{5,13},{6,14},{7,0},{8,15},{9,1},{1... | collective-permute-start | bytes 393224 | tf_op jit(solution)/shard_map/ppermute | solution.py:530
  12.6 2.3 %collective-permute-start.5 = (f32[64,512]{1,0:T(8,128)S(1)}, f32[64,512]{1,0:T(8,128)S(1)}, u32[]{:S(2)}, u32[]{:S(2)}) collective-permute-start(f32[64,512]{1,0:T(8,128)S(1)} %get-tuple-element.113), channel_id=1, source_target_pairs={{0,8},{1,2},{2,1},{3,11},{4,12},{5,6},{6,5},{7,15},{8,0},{9,17},{1... | collective-permute-start | bytes 393224 | tf_op jit(solution)/shard_map/ppermute | solution.py:530
  15.4 2.5 %shard_map.90 = (f32[64,2048]{1,0:T(8,128)S(1)}, f32[64,2048]{1,0:T(8,128)S(1)}, f32[64,2048]{1,0:T(8,128)S(1)}, bf16[80,128,128]{2,1,0:T(8,128)(2,1)S(1)}, bf16...) custom-call(s32[446]{0:T(512)S(4)} %get-tuple-element.94.table, ...), custom_call_target="tpu_custom_call" | custom-call | flops 335544320 | bytes 4194304 | tf_op jit(solution)/shard_map/pallas_call | solution.py:516
  18.6 1.7 %collective-permute-start.8 = (f32[64,512]{1,0:T(8,128)S(1)}, f32[64,512]{1,0:T(8,128)S(1)}, u32[]{:S(2)}, u32[]{:S(2)}) collective-permute-start(f32[64,512]{1,0:T(8,128)S(1)} %get-tuple-element.122), channel_id=1, source_target_pairs={{0,7},{1,9},{2,10},{3,4},{4,3},{5,13},{6,14},{7,0},{8,15},{9,1},{1... | collective-permute-start | bytes 393224 | tf_op jit(solution)/shard_map/ppermute | solution.py:530
  20.3 2.1 %collective-permute-start.9 = (f32[64,512]{1,0:T(8,128)S(1)}, f32[64,512]{1,0:T(8,128)S(1)}, u32[]{:S(2)}, u32[]{:S(2)}) collective-permute-start(f32[64,512]{1,0:T(8,128)S(1)} %get-tuple-element.125), channel_id=1, source_target_pairs={{0,8},{1,2},{2,1},{3,11},{4,12},{5,6},{6,5},{7,15},{8,0},{9,17},{1... | collective-permute-start | bytes 393224 | tf_op jit(solution)/shard_map/ppermute | solution.py:530
  22.9 2.1 %shard_map.93 = (f32[64,2048]{1,0:T(8,128)S(1)}, f32[64,2048]{1,0:T(8,128)S(1)}, f32[64,2048]{1,0:T(8,128)S(1)}, bf16[128,2048]{1,0:T(8,128)(2,1)S(1)}, bf16[128,2048]{1,0:T(8,128)(2,1)S(1)}) custom-call(s32[446]{0:T(512)S(4)} %get-tuple-element.94.table, f32[64,2048]{1,0:T(8,128)S(1)} %get-tuple-element.116.update, ...), custom_call_target="tpu_custom_call" | custom-call | flops 335544320 | bytes 4194304 | tf_op jit(solution)/shard_map/pallas_call | solution.py:516
  25.8 1.5 %collective-permute-start.12 = (f32[64,512]{1,0:T(8,128)S(1)}, f32[64,512]{1,0:T(8,128)S(1)}, u32[]{:S(2)}, u32[]{:S(2)}) collective-permute-start(f32[64,512]{1,0:T(8,128)S(1)} %get-tuple-element.133), channel_id=1, source_target_pairs={{0,7},{1,9},{2,10},{3,4},{4,3},{5,13},{6,14},{7,0},{8,15},{9,1},{1... | collective-permute-start | bytes 393224 | tf_op jit(solution)/shard_map/ppermute | solution.py:530
  27.3 2.0 %collective-permute-start.13 = (f32[64,512]{1,0:T(8,128)S(1)}, f32[64,512]{1,0:T(8,128)S(1)}, u32[]{:S(2)}, u32[]{:S(2)}) collective-permute-start(f32[64,512]{1,0:T(8,128)S(1)} %get-tuple-element.138), channel_id=1, source_target_pairs={{0,8},{1,2},{2,1},{3,11},{4,12},{5,6},{6,5},{7,15},{8,0},{9,17},{1... | collective-permute-start | bytes 393224 | tf_op jit(solution)/shard_map/ppermute | solution.py:530
  29.9 1.5 %shard_map.96 = (f32[64,2048]{1,0:T(8,128)S(1)}, f32[64,128]{1,0:T(8,128)S(1)}, f32[64,2048]{1,0:T(8,128)S(1)}) custom-call(s32[446]{0:T(512)S(4)} %get-tuple-element.94.table, f32[64,2048]{1,0:T(8,128)S(1)} %get-tuple-element.128.update, f32[64,2048]{1,0:T(8,128)S(1)} %get-tuple-element.129.residual, f32[64,2048]{1,0:T(8,128)S(1)} %get-tuple-element.130.iterate, ...), custom_call_target="tpu_custom_call" | custom-call | flops 335544320 | bytes 4194304 | tf_op jit(solution)/shard_map/pallas_call | solution.py:516
  32.9 1.5 %collective-permute-start.19 = (f32[64,128]{1,0:T(8,128)S(1)}, f32[64,128]{1,0:T(8,128)S(1)}, u32[]{:S(2)}, u32[]{:S(2)}) collective-permute-start(f32[64,128]{1,0:T(8,128)S(1)} %get-tuple-element.141.update.iterate), channel_id=1, source_target_pairs={{0,7},{1,9},{2,10},{3,4},{4,3},{5,13},{6,14},{7,0},{8,15},{9,1},{1... | collective-permute-start | bytes 98312 | tf_op jit(solution)/shard_map/ppermute | solution.py:530
  34.5 2.1 %collective-permute-start.18 = (f32[64,128]{1,0:T(8,128)S(1)}, f32[64,128]{1,0:T(8,128)S(1)}, u32[]{:S(2)}, u32[]{:S(2)}) collective-permute-start(f32[64,128]{1,0:T(8,128)S(1)} %get-tuple-element.141.update.iterate), channel_id=1, source_target_pairs={{0,8},{1,2},{2,1},{3,11},{4,12},{5,6},{6,5},{7,15},{8,0},{9,17},{1... | collective-permute-start | bytes 98312 | tf_op jit(solution)/shard_map/ppermute | solution.py:530
  39.1 2.1 %collective-permute-start.22 = (f32[64,128]{1,0:T(8,128)S(1)}, f32[64,128]{1,0:T(8,128)S(1)}, u32[]{:S(2)}, u32[]{:S(2)}) collective-permute-start(f32[64,128]{1,0:T(8,128)S(1)} %get-tuple-element.145.update), channel_id=1, source_target_pairs={{0,8},{1,2},{2,1},{3,11},{4,12},{5,6},{6,5},{7,15},{8,0},{9,17},{1... | collective-permute-start | bytes 98312 | tf_op jit(solution)/shard_map/ppermute | solution.py:530
  43.6 1.3 %collective-permute-start.24 = (f32[64,128]{1,0:T(8,128)S(1)}, f32[64,128]{1,0:T(8,128)S(1)}, u32[]{:S(2)}, u32[]{:S(2)}) collective-permute-start(f32[64,128]{1,0:T(8,128)S(1)} %shard_map.100.correction), channel_id=1, source_target_pairs={{0,7},{1,9},{2,10},{3,4},{4,3},{5,13},{6,14},{7,0},{8,15},{9,1},{1... | collective-permute-start | bytes 98312 | tf_op jit(solution)/shard_map/ppermute | solution.py:530
  44.9 2.3 %collective-permute-start.27 = (f32[64,128]{1,0:T(8,128)S(1)}, f32[64,128]{1,0:T(8,128)S(1)}, u32[]{:S(2)}, u32[]{:S(2)}) collective-permute-start(f32[64,128]{1,0:T(8,128)S(1)} %shard_map.100.correction), channel_id=1, source_target_pairs={{0,8},{1,2},{2,1},{3,11},{4,12},{5,6},{6,5},{7,15},{8,0},{9,17},{1... | collective-permute-start | bytes 98312 | tf_op jit(solution)/shard_map/ppermute | solution.py:530
  50.7 2.0 %collective-permute-start.29 = (f32[64,512]{1,0:T(8,128)S(1)}, f32[64,512]{1,0:T(8,128)S(1)}, u32[]{:S(2)}, u32[]{:S(2)}) collective-permute-start(f32[64,512]{1,0:T(8,128)S(1)} %get-tuple-element.165), channel_id=1, source_target_pairs={{0,8},{1,2},{2,1},{3,11},{4,12},{5,6},{6,5},{7,15},{8,0},{9,17},{1... | collective-permute-start | bytes 393224 | tf_op jit(solution)/shard_map/ppermute | solution.py:530
  53.2 1.2 %shard_map.104 = (f32[64,2048]{1,0:T(8,128)S(1)}, f32[64,2048]{1,0:T(8,128)S(1)}, f32[64,2048]{1,0:T(8,128)S(1)}) custom-call(s32[446]{0:T(512)S(4)} %get-tuple-element.94.table, f32[64,2048]{1,0:T(8,128)S(1)} %get-tuple-element.157.update, f32[64,2048]{1,0:T(8,128)S(1)} %get-tuple-element.158.residual, f32[64,2048]{1,0:T(8,128)S(1)} %get-tuple-element.159.iterate, ...), custom_call_target="tpu_custom_call" | custom-call | flops 335544320 | bytes 4194304 | tf_op jit(solution)/shard_map/pallas_call | solution.py:516
  54.3 1.2 %collective-permute-done.28.refs_0_ = f32[64,512]{1,0:T(8,128)S(1)} collective-permute-done((f32[64,512]{1,0:T(8,128)S(1)}, f32[64,512]{1,0:T(8,128)S(1)}, u32[]{:S(2)}, u32[]{:S(2)}) %collective-permute-start.28) | collective-permute-done | bytes 131104 | tf_op jit(solution)/shard_map/ppermute | solution.py:530
  56.3 1.8 %collective-permute-start.32 = (f32[64,512]{1,0:T(8,128)S(1)}, f32[64,512]{1,0:T(8,128)S(1)}, u32[]{:S(2)}, u32[]{:S(2)}) collective-permute-start(f32[64,512]{1,0:T(8,128)S(1)} %get-tuple-element.173), channel_id=1, source_target_pairs={{0,7},{1,9},{2,10},{3,4},{4,3},{5,13},{6,14},{7,0},{8,15},{9,1},{1... | collective-permute-start | bytes 393224 | tf_op jit(solution)/shard_map/ppermute | solution.py:530
  58.1 2.2 %collective-permute-start.33 = (f32[64,512]{1,0:T(8,128)S(1)}, f32[64,512]{1,0:T(8,128)S(1)}, u32[]{:S(2)}, u32[]{:S(2)}) collective-permute-start(f32[64,512]{1,0:T(8,128)S(1)} %get-tuple-element.176), channel_id=1, source_target_pairs={{0,8},{1,2},{2,1},{3,11},{4,12},{5,6},{6,5},{7,15},{8,0},{9,17},{1... | collective-permute-start | bytes 393224 | tf_op jit(solution)/shard_map/ppermute | solution.py:530
  60.8 1.9 %shard_map.107 = (f32[64,2048]{1,0:T(8,128)S(1)}, f32[64,2048]{1,0:T(8,128)S(1)}, f32[64,2048]{1,0:T(8,128)}) custom-call(s32[446]{0:T(512)S(4)} %get-tuple-element.94.table, f32[64,2048]{1,0:T(8,128)S(1)} %get-tuple-element.168.update, f32[64,2048]{1,0:T(8,128)S(1)} %get-tuple-element.169.residual, f32[64,2048]{1,0:T(8,128)S(1)} %get-tuple-element.170.iterate, ...), custom_call_target="tpu_custom_call" | custom-call | flops 335544320 | bytes 4194304 | tf_op jit(solution)/shard_map/pallas_call | solution.py:516
  (72 shorter events, 17.7 us)
Async XLA Ops:
  1.8 8.4 %collective-permute-start = (f32[72,512]{1,0:T(8,128)S(1)}, f32[72,512]{1,0:T(8,128)S(1)}, u32[]{:S(2)}, u32[]{:S(2)}) collective-permute-start(f32[72,512]{1,0:T(8,128)S(1)} %get-tuple-element.99), channel_id=1, source_target_pairs={{0,7},{1,9},{2,10},{3,4},{4,3},{5,13},{6,14},{7,0},{8,15},{9,1},{1... | collective-permute-start | bytes 442376 | tf_op jit(solution)/shard_map/ppermute | solution.py:530
  5.2 5.2 %collective-permute-start.1 = (f32[72,512]{1,0:T(8,128)S(1)}, f32[72,512]{1,0:T(8,128)S(1)}, u32[]{:S(2)}, u32[]{:S(2)}) collective-permute-start(f32[72,512]{1,0:T(8,128)S(1)} %get-tuple-element.102), channel_id=1, source_target_pairs={{0,8},{1,2},{2,1},{3,11},{4,12},{5,6},{6,5},{7,15},{8,0},{9,17},{1... | collective-permute-start | bytes 442376 | tf_op jit(solution)/shard_map/ppermute | solution.py:530
  6.8 3.7 %collective-permute-start.2 = (f32[72,512]{1,0:T(8,128)S(1)}, f32[72,512]{1,0:T(8,128)S(1)}, u32[]{:S(2)}, u32[]{:S(2)}) collective-permute-start(f32[72,512]{1,0:T(8,128)S(1)} %get-tuple-element.103), channel_id=1, source_target_pairs={{0,1},{1,0},{2,3},{3,2},{4,5},{5,4},{6,7},{7,6},{8,16},{9,10},{10,... | collective-permute-start | bytes 442376 | tf_op jit(solution)/shard_map/ppermute | solution.py:530
  6.8 3.7 %collective-permute-start.3 = (f32[72,512]{1,0:T(8,128)S(1)}, f32[72,512]{1,0:T(8,128)S(1)}, u32[]{:S(2)}, u32[]{:S(2)}) collective-permute-start(f32[72,512]{1,0:T(8,128)S(1)} %get-tuple-element.104), channel_id=1, source_target_pairs={{0,1},{1,0},{2,3},{3,2},{4,5},{5,4},{6,7},{7,6},{8,9},{9,8},{10,11... | collective-permute-start | bytes 442376 | tf_op jit(solution)/shard_map/ppermute | solution.py:530
  11.1 6.9 %collective-permute-start.4 = (f32[64,512]{1,0:T(8,128)S(1)}, f32[64,512]{1,0:T(8,128)S(1)}, u32[]{:S(2)}, u32[]{:S(2)}) collective-permute-start(f32[64,512]{1,0:T(8,128)S(1)} %get-tuple-element.110), channel_id=1, source_target_pairs={{0,7},{1,9},{2,10},{3,4},{4,3},{5,13},{6,14},{7,0},{8,15},{9,1},{1... | collective-permute-start | bytes 393224 | tf_op jit(solution)/shard_map/ppermute | solution.py:530
  12.6 5.5 %collective-permute-start.5 = (f32[64,512]{1,0:T(8,128)S(1)}, f32[64,512]{1,0:T(8,128)S(1)}, u32[]{:S(2)}, u32[]{:S(2)}) collective-permute-start(f32[64,512]{1,0:T(8,128)S(1)} %get-tuple-element.113), channel_id=1, source_target_pairs={{0,8},{1,2},{2,1},{3,11},{4,12},{5,6},{6,5},{7,15},{8,0},{9,17},{1... | collective-permute-start | bytes 393224 | tf_op jit(solution)/shard_map/ppermute | solution.py:530
  14.9 3.3 %collective-permute-start.6 = (f32[64,512]{1,0:T(8,128)S(1)}, f32[64,512]{1,0:T(8,128)S(1)}, u32[]{:S(2)}, u32[]{:S(2)}) collective-permute-start(f32[64,512]{1,0:T(8,128)S(1)} %get-tuple-element.114), channel_id=1, source_target_pairs={{0,1},{1,0},{2,3},{3,2},{4,5},{5,4},{6,7},{7,6},{8,16},{9,10},{10,... | collective-permute-start | bytes 393224 | tf_op jit(solution)/shard_map/ppermute | solution.py:530
  14.9 3.3 %collective-permute-start.7 = (f32[64,512]{1,0:T(8,128)S(1)}, f32[64,512]{1,0:T(8,128)S(1)}, u32[]{:S(2)}, u32[]{:S(2)}) collective-permute-start(f32[64,512]{1,0:T(8,128)S(1)} %get-tuple-element.115), channel_id=1, source_target_pairs={{0,1},{1,0},{2,3},{3,2},{4,5},{5,4},{6,7},{7,6},{8,9},{9,8},{10,11... | collective-permute-start | bytes 393224 | tf_op jit(solution)/shard_map/ppermute | solution.py:530
  18.6 6.4 %collective-permute-start.8 = (f32[64,512]{1,0:T(8,128)S(1)}, f32[64,512]{1,0:T(8,128)S(1)}, u32[]{:S(2)}, u32[]{:S(2)}) collective-permute-start(f32[64,512]{1,0:T(8,128)S(1)} %get-tuple-element.122), channel_id=1, source_target_pairs={{0,7},{1,9},{2,10},{3,4},{4,3},{5,13},{6,14},{7,0},{8,15},{9,1},{1... | collective-permute-start | bytes 393224 | tf_op jit(solution)/shard_map/ppermute | solution.py:530
  20.3 5.0 %collective-permute-start.9 = (f32[64,512]{1,0:T(8,128)S(1)}, f32[64,512]{1,0:T(8,128)S(1)}, u32[]{:S(2)}, u32[]{:S(2)}) collective-permute-start(f32[64,512]{1,0:T(8,128)S(1)} %get-tuple-element.125), channel_id=1, source_target_pairs={{0,8},{1,2},{2,1},{3,11},{4,12},{5,6},{6,5},{7,15},{8,0},{9,17},{1... | collective-permute-start | bytes 393224 | tf_op jit(solution)/shard_map/ppermute | solution.py:530
  25.8 5.6 %collective-permute-start.12 = (f32[64,512]{1,0:T(8,128)S(1)}, f32[64,512]{1,0:T(8,128)S(1)}, u32[]{:S(2)}, u32[]{:S(2)}) collective-permute-start(f32[64,512]{1,0:T(8,128)S(1)} %get-tuple-element.133), channel_id=1, source_target_pairs={{0,7},{1,9},{2,10},{3,4},{4,3},{5,13},{6,14},{7,0},{8,15},{9,1},{1... | collective-permute-start | bytes 393224 | tf_op jit(solution)/shard_map/ppermute | solution.py:530
  27.3 5.0 %collective-permute-start.13 = (f32[64,512]{1,0:T(8,128)S(1)}, f32[64,512]{1,0:T(8,128)S(1)}, u32[]{:S(2)}, u32[]{:S(2)}) collective-permute-start(f32[64,512]{1,0:T(8,128)S(1)} %get-tuple-element.138), channel_id=1, source_target_pairs={{0,8},{1,2},{2,1},{3,11},{4,12},{5,6},{6,5},{7,15},{8,0},{9,17},{1... | collective-permute-start | bytes 393224 | tf_op jit(solution)/shard_map/ppermute | solution.py:530
  32.9 4.3 %collective-permute-start.19 = (f32[64,128]{1,0:T(8,128)S(1)}, f32[64,128]{1,0:T(8,128)S(1)}, u32[]{:S(2)}, u32[]{:S(2)}) collective-permute-start(f32[64,128]{1,0:T(8,128)S(1)} %get-tuple-element.141.update.iterate), channel_id=1, source_target_pairs={{0,7},{1,9},{2,10},{3,4},{4,3},{5,13},{6,14},{7,0},{8,15},{9,1},{1... | collective-permute-start | bytes 98312 | tf_op jit(solution)/shard_map/ppermute | solution.py:530
  34.5 4.0 %collective-permute-start.18 = (f32[64,128]{1,0:T(8,128)S(1)}, f32[64,128]{1,0:T(8,128)S(1)}, u32[]{:S(2)}, u32[]{:S(2)}) collective-permute-start(f32[64,128]{1,0:T(8,128)S(1)} %get-tuple-element.141.update.iterate), channel_id=1, source_target_pairs={{0,8},{1,2},{2,1},{3,11},{4,12},{5,6},{6,5},{7,15},{8,0},{9,17},{1... | collective-permute-start | bytes 98312 | tf_op jit(solution)/shard_map/ppermute | solution.py:530
  38.7 4.3 %collective-permute-start.23 = (f32[64,128]{1,0:T(8,128)S(1)}, f32[64,128]{1,0:T(8,128)S(1)}, u32[]{:S(2)}, u32[]{:S(2)}) collective-permute-start(f32[64,128]{1,0:T(8,128)S(1)} %get-tuple-element.145.update), channel_id=1, source_target_pairs={{0,7},{1,9},{2,10},{3,4},{4,3},{5,13},{6,14},{7,0},{8,15},{9,1},{1... | collective-permute-start | bytes 98312 | tf_op jit(solution)/shard_map/ppermute | solution.py:530
  39.1 4.0 %collective-permute-start.22 = (f32[64,128]{1,0:T(8,128)S(1)}, f32[64,128]{1,0:T(8,128)S(1)}, u32[]{:S(2)}, u32[]{:S(2)}) collective-permute-start(f32[64,128]{1,0:T(8,128)S(1)} %get-tuple-element.145.update), channel_id=1, source_target_pairs={{0,8},{1,2},{2,1},{3,11},{4,12},{5,6},{6,5},{7,15},{8,0},{9,17},{1... | collective-permute-start | bytes 98312 | tf_op jit(solution)/shard_map/ppermute | solution.py:530
  43.6 5.1 %collective-permute-start.24 = (f32[64,128]{1,0:T(8,128)S(1)}, f32[64,128]{1,0:T(8,128)S(1)}, u32[]{:S(2)}, u32[]{:S(2)}) collective-permute-start(f32[64,128]{1,0:T(8,128)S(1)} %shard_map.100.correction), channel_id=1, source_target_pairs={{0,7},{1,9},{2,10},{3,4},{4,3},{5,13},{6,14},{7,0},{8,15},{9,1},{1... | collective-permute-start | bytes 98312 | tf_op jit(solution)/shard_map/ppermute | solution.py:530
  44.9 4.2 %collective-permute-start.27 = (f32[64,128]{1,0:T(8,128)S(1)}, f32[64,128]{1,0:T(8,128)S(1)}, u32[]{:S(2)}, u32[]{:S(2)}) collective-permute-start(f32[64,128]{1,0:T(8,128)S(1)} %shard_map.100.correction), channel_id=1, source_target_pairs={{0,8},{1,2},{2,1},{3,11},{4,12},{5,6},{6,5},{7,15},{8,0},{9,17},{1... | collective-permute-start | bytes 98312 | tf_op jit(solution)/shard_map/ppermute | solution.py:530
  49.8 5.7 %collective-permute-start.28 = (f32[64,512]{1,0:T(8,128)S(1)}, f32[64,512]{1,0:T(8,128)S(1)}, u32[]{:S(2)}, u32[]{:S(2)}) collective-permute-start(f32[64,512]{1,0:T(8,128)S(1)} %get-tuple-element.162), channel_id=1, source_target_pairs={{0,7},{1,9},{2,10},{3,4},{4,3},{5,13},{6,14},{7,0},{8,15},{9,1},{1... | collective-permute-start | bytes 393224 | tf_op jit(solution)/shard_map/ppermute | solution.py:530
  50.7 5.1 %collective-permute-start.29 = (f32[64,512]{1,0:T(8,128)S(1)}, f32[64,512]{1,0:T(8,128)S(1)}, u32[]{:S(2)}, u32[]{:S(2)}) collective-permute-start(f32[64,512]{1,0:T(8,128)S(1)} %get-tuple-element.165), channel_id=1, source_target_pairs={{0,8},{1,2},{2,1},{3,11},{4,12},{5,6},{6,5},{7,15},{8,0},{9,17},{1... | collective-permute-start | bytes 393224 | tf_op jit(solution)/shard_map/ppermute | solution.py:530
  52.7 3.1 %collective-permute-start.30 = (f32[64,512]{1,0:T(8,128)S(1)}, f32[64,512]{1,0:T(8,128)S(1)}, u32[]{:S(2)}, u32[]{:S(2)}) collective-permute-start(f32[64,512]{1,0:T(8,128)S(1)} %get-tuple-element.166), channel_id=1, source_target_pairs={{0,1},{1,0},{2,3},{3,2},{4,5},{5,4},{6,7},{7,6},{8,16},{9,10},{10,... | collective-permute-start | bytes 393224 | tf_op jit(solution)/shard_map/ppermute | solution.py:530
  52.8 3.0 %collective-permute-start.31 = (f32[64,512]{1,0:T(8,128)S(1)}, f32[64,512]{1,0:T(8,128)S(1)}, u32[]{:S(2)}, u32[]{:S(2)}) collective-permute-start(f32[64,512]{1,0:T(8,128)S(1)} %get-tuple-element.167), channel_id=1, source_target_pairs={{0,1},{1,0},{2,3},{3,2},{4,5},{5,4},{6,7},{7,6},{8,9},{9,8},{10,11... | collective-permute-start | bytes 393224 | tf_op jit(solution)/shard_map/ppermute | solution.py:530
  56.3 6.5 %collective-permute-start.32 = (f32[64,512]{1,0:T(8,128)S(1)}, f32[64,512]{1,0:T(8,128)S(1)}, u32[]{:S(2)}, u32[]{:S(2)}) collective-permute-start(f32[64,512]{1,0:T(8,128)S(1)} %get-tuple-element.173), channel_id=1, source_target_pairs={{0,7},{1,9},{2,10},{3,4},{4,3},{5,13},{6,14},{7,0},{8,15},{9,1},{1... | collective-permute-start | bytes 393224 | tf_op jit(solution)/shard_map/ppermute | solution.py:530
  58.1 5.1 %collective-permute-start.33 = (f32[64,512]{1,0:T(8,128)S(1)}, f32[64,512]{1,0:T(8,128)S(1)}, u32[]{:S(2)}, u32[]{:S(2)}) collective-permute-start(f32[64,512]{1,0:T(8,128)S(1)} %get-tuple-element.176), channel_id=1, source_target_pairs={{0,8},{1,2},{2,1},{3,11},{4,12},{5,6},{6,5},{7,15},{8,0},{9,17},{1... | collective-permute-start | bytes 393224 | tf_op jit(solution)/shard_map/ppermute | solution.py:530
  (12 other events, 27.5 us)

commit v7 on v6

--- a/solution.py
+++ b/solution.py
@@ -569,7 +569,7 @@
         return call(
             local_kernel, [table, update, residual, iterate, inverse, matrix] + list(extra),
             [field, small if mode == "restrict" else field, field],
-            [wide_local], "s", "VV", flops=flops, weights=weight, mode=mode, **dims,
+            [wide_local], "s", "VVV", flops=flops, weights=weight, mode=mode, **dims,
         )
 
     *payloads, guess, lists, columns = call(

time: 64.6 us -> 64.7 us (level)
  no operation moved by 1% of the time
where the time goes in v7:
time: 64.7 us; the launch traced here: 64.5 us
  starting transfers between devices  37.9 us (59%)
  Pallas kernels  20.9 us (32%)
  waiting for transfers between devices  4.75 us (7%)
  between operations  0.91 us (1%)
    ppermute x36, starting transfers between devices, exchange(): return [lax.ppermute(x, AXES, perm) for x, perm in zip(payloads, perms)]  37.9 us
    pallas_call x24, Pallas kernels, call(): pl.pallas_call(functools.partial(kernel, **named), out_shape=[forms[c](sh...  20.9 us
    ppermute x36, waiting for transfers between devices, exchange(): return [lax.ppermute(x, AXES, perm) for x, perm in zip(payloads, perms)]  4.75 us
  transfers between devices with their start and end apart: 36, of which 9 were waited for; matrix products, arithmetic and copies ran while one was open for 0% of the time, Pallas kernels for 23%

profile of v7, /device:TPU:0, one launch (start us, length us, event | category | flops | bytes accessed | tf_op | source)
XLA Modules:
  0.0 64.5 jit_solution(10237654719794480896)
XLA Ops:
  0.6 1.2 %shard_map.86 = (f32[72,512]{1,0:T(8,128)S(1)}, f32[72,512]{1,0:T(8,128)S(1)}, f32[72,512]{1,0:T(8,128)S(1)}, f32[72,512]{1,0:T(8,128)S(1)}, f32[64,2048]{1,0:T(...) custom-call(f32[64,2048]{1,0:T(8,128)} %guess.1, s32[1,16]{1,0:T(1,128)} %lists.1, s32[5,16]{1,0:T(8,128)} %bitcast.8, ...), custom_call_target="tpu_custom_call" | custom-call | bytes 4194304 | tf_op jit(solution)/shard_map/pallas_call | solution.py:516
  1.8 3.4 %collective-permute-start = (f32[72,512]{1,0:T(8,128)S(1)}, f32[72,512]{1,0:T(8,128)S(1)}, u32[]{:S(2)}, u32[]{:S(2)}) collective-permute-start(f32[72,512]{1,0:T(8,128)S(1)} %get-tuple-element.99), channel_id=1, source_target_pairs={{0,7},{1,9},{2,10},{3,4},{4,3},{5,13},{6,14},{7,0},{8,15},{9,1},{1... | collective-permute-start | bytes 442376 | tf_op jit(solution)/shard_map/ppermute | solution.py:530
  5.2 1.6 %collective-permute-start.1 = (f32[72,512]{1,0:T(8,128)S(1)}, f32[72,512]{1,0:T(8,128)S(1)}, u32[]{:S(2)}, u32[]{:S(2)}) collective-permute-start(f32[72,512]{1,0:T(8,128)S(1)} %get-tuple-element.102), channel_id=1, source_target_pairs={{0,8},{1,2},{2,1},{3,11},{4,12},{5,6},{6,5},{7,15},{8,0},{9,17},{1... | collective-permute-start | bytes 442376 | tf_op jit(solution)/shard_map/ppermute | solution.py:530
  7.3 2.9 %shard_map.87 = (f32[64,2048]{1,0:T(8,128)S(1)}, f32[64,2048]{1,0:T(8,128)S(1)}, s32[446]{0:T(512)S(4)}, f32[8,2048]{1,0:T(8,128)S(1)}, bf16[80,128,128]{2,1,0:T(8,128)(2,1)S(1)}) custom-call(s32[1,16]{1,0:T(1,128)S(4)} %get-tuple-element.91.lists, s32[5,16]{1,0:T(8,128)S(4)} %get-tuple-element.92.columns, f32[64,2048]{1,0:T(8,128)S(1)} %get-tuple-element.93.field.iterate, ...), custom_call_target="tpu_custom_call" | custom-call | flops 335544320 | bytes 4194304 | tf_op jit(solution)/shard_map/pallas_call | solution.py:516
  11.1 1.6 %collective-permute-start.4 = (f32[64,512]{1,0:T(8,128)S(1)}, f32[64,512]{1,0:T(8,128)S(1)}, u32[]{:S(2)}, u32[]{:S(2)}) collective-permute-start(f32[64,512]{1,0:T(8,128)S(1)} %get-tuple-element.110), channel_id=1, source_target_pairs={{0,7},{1,9},{2,10},{3,4},{4,3},{5,13},{6,14},{7,0},{8,15},{9,1},{1... | collective-permute-start | bytes 393224 | tf_op jit(solution)/shard_map/ppermute | solution.py:530
  12.6 2.3 %collective-permute-start.5 = (f32[64,512]{1,0:T(8,128)S(1)}, f32[64,512]{1,0:T(8,128)S(1)}, u32[]{:S(2)}, u32[]{:S(2)}) collective-permute-start(f32[64,512]{1,0:T(8,128)S(1)} %get-tuple-element.113), channel_id=1, source_target_pairs={{0,8},{1,2},{2,1},{3,11},{4,12},{5,6},{6,5},{7,15},{8,0},{9,17},{1... | collective-permute-start | bytes 393224 | tf_op jit(solution)/shard_map/ppermute | solution.py:530
  15.4 2.5 %shard_map.90 = (f32[64,2048]{1,0:T(8,128)S(1)}, f32[64,2048]{1,0:T(8,128)S(1)}, f32[64,2048]{1,0:T(8,128)S(1)}, bf16[80,128,128]{2,1,0:T(8,128)(2,1)S(1)}, bf16...) custom-call(s32[446]{0:T(512)S(4)} %get-tuple-element.94.table, ...), custom_call_target="tpu_custom_call" | custom-call | flops 335544320 | bytes 4194304 | tf_op jit(solution)/shard_map/pallas_call | solution.py:516
  18.6 1.7 %collective-permute-start.8 = (f32[64,512]{1,0:T(8,128)S(1)}, f32[64,512]{1,0:T(8,128)S(1)}, u32[]{:S(2)}, u32[]{:S(2)}) collective-permute-start(f32[64,512]{1,0:T(8,128)S(1)} %get-tuple-element.122), channel_id=1, source_target_pairs={{0,7},{1,9},{2,10},{3,4},{4,3},{5,13},{6,14},{7,0},{8,15},{9,1},{1... | collective-permute-start | bytes 393224 | tf_op jit(solution)/shard_map/ppermute | solution.py:530
  20.3 2.1 %collective-permute-start.9 = (f32[64,512]{1,0:T(8,128)S(1)}, f32[64,512]{1,0:T(8,128)S(1)}, u32[]{:S(2)}, u32[]{:S(2)}) collective-permute-start(f32[64,512]{1,0:T(8,128)S(1)} %get-tuple-element.125), channel_id=1, source_target_pairs={{0,8},{1,2},{2,1},{3,11},{4,12},{5,6},{6,5},{7,15},{8,0},{9,17},{1... | collective-permute-start | bytes 393224 | tf_op jit(solution)/shard_map/ppermute | solution.py:530
  22.9 2.1 %shard_map.93 = (f32[64,2048]{1,0:T(8,128)S(1)}, f32[64,2048]{1,0:T(8,128)S(1)}, f32[64,2048]{1,0:T(8,128)S(1)}, bf16[128,2048]{1,0:T(8,128)(2,1)S(1)}, bf16[128,2048]{1,0:T(8,128)(2,1)S(1)}) custom-call(s32[446]{0:T(512)S(4)} %get-tuple-element.94.table, f32[64,2048]{1,0:T(8,128)S(1)} %get-tuple-element.116.update, ...), custom_call_target="tpu_custom_call" | custom-call | flops 335544320 | bytes 4194304 | tf_op jit(solution)/shard_map/pallas_call | solution.py:516
  25.8 1.5 %collective-permute-start.12 = (f32[64,512]{1,0:T(8,128)S(1)}, f32[64,512]{1,0:T(8,128)S(1)}, u32[]{:S(2)}, u32[]{:S(2)}) collective-permute-start(f32[64,512]{1,0:T(8,128)S(1)} %get-tuple-element.133), channel_id=1, source_target_pairs={{0,7},{1,9},{2,10},{3,4},{4,3},{5,13},{6,14},{7,0},{8,15},{9,1},{1... | collective-permute-start | bytes 393224 | tf_op jit(solution)/shard_map/ppermute | solution.py:530
  27.3 2.0 %collective-permute-start.13 = (f32[64,512]{1,0:T(8,128)S(1)}, f32[64,512]{1,0:T(8,128)S(1)}, u32[]{:S(2)}, u32[]{:S(2)}) collective-permute-start(f32[64,512]{1,0:T(8,128)S(1)} %get-tuple-element.138), channel_id=1, source_target_pairs={{0,8},{1,2},{2,1},{3,11},{4,12},{5,6},{6,5},{7,15},{8,0},{9,17},{1... | collective-permute-start | bytes 393224 | tf_op jit(solution)/shard_map/ppermute | solution.py:530
  29.9 1.5 %shard_map.96 = (f32[64,2048]{1,0:T(8,128)S(1)}, f32[64,128]{1,0:T(8,128)S(1)}, f32[64,2048]{1,0:T(8,128)S(1)}) custom-call(s32[446]{0:T(512)S(4)} %get-tuple-element.94.table, f32[64,2048]{1,0:T(8,128)S(1)} %get-tuple-element.128.update, f32[64,2048]{1,0:T(8,128)S(1)} %get-tuple-element.129.residual, f32[64,2048]{1,0:T(8,128)S(1)} %get-tuple-element.130.iterate, ...), custom_call_target="tpu_custom_call" | custom-call | flops 335544320 | bytes 4194304 | tf_op jit(solution)/shard_map/pallas_call | solution.py:516
  33.0 1.5 %collective-permute-start.19 = (f32[64,128]{1,0:T(8,128)S(1)}, f32[64,128]{1,0:T(8,128)S(1)}, u32[]{:S(2)}, u32[]{:S(2)}) collective-permute-start(f32[64,128]{1,0:T(8,128)S(1)} %get-tuple-element.141.update.iterate), channel_id=1, source_target_pairs={{0,7},{1,9},{2,10},{3,4},{4,3},{5,13},{6,14},{7,0},{8,15},{9,1},{1... | collective-permute-start | bytes 98312 | tf_op jit(solution)/shard_map/ppermute | solution.py:530
  34.5 2.1 %collective-permute-start.18 = (f32[64,128]{1,0:T(8,128)S(1)}, f32[64,128]{1,0:T(8,128)S(1)}, u32[]{:S(2)}, u32[]{:S(2)}) collective-permute-start(f32[64,128]{1,0:T(8,128)S(1)} %get-tuple-element.141.update.iterate), channel_id=1, source_target_pairs={{0,8},{1,2},{2,1},{3,11},{4,12},{5,6},{6,5},{7,15},{8,0},{9,17},{1... | collective-permute-start | bytes 98312 | tf_op jit(solution)/shard_map/ppermute | solution.py:530
  37.3 1.2 %collective-permute-done.18.h2 = f32[64,128]{1,0:T(8,128)S(1)} collective-permute-done((f32[64,128]{1,0:T(8,128)S(1)}, f32[64,128]{1,0:T(8,128)S(1)}, u32[]{:S(2)}, u32[]{:S(2)}) %collective-permute-start.18) | collective-permute-done | bytes 32800 | tf_op jit(solution)/shard_map/ppermute | solution.py:530
  39.1 2.1 %collective-permute-start.22 = (f32[64,128]{1,0:T(8,128)S(1)}, f32[64,128]{1,0:T(8,128)S(1)}, u32[]{:S(2)}, u32[]{:S(2)}) collective-permute-start(f32[64,128]{1,0:T(8,128)S(1)} %get-tuple-element.145.update), channel_id=1, source_target_pairs={{0,8},{1,2},{2,1},{3,11},{4,12},{5,6},{6,5},{7,15},{8,0},{9,17},{1... | collective-permute-start | bytes 98312 | tf_op jit(solution)/shard_map/ppermute | solution.py:530
  43.7 1.2 %collective-permute-start.24 = (f32[64,128]{1,0:T(8,128)S(1)}, f32[64,128]{1,0:T(8,128)S(1)}, u32[]{:S(2)}, u32[]{:S(2)}) collective-permute-start(f32[64,128]{1,0:T(8,128)S(1)} %shard_map.100.correction), channel_id=1, source_target_pairs={{0,7},{1,9},{2,10},{3,4},{4,3},{5,13},{6,14},{7,0},{8,15},{9,1},{1... | collective-permute-start | bytes 98312 | tf_op jit(solution)/shard_map/ppermute | solution.py:530
  44.9 2.3 %collective-permute-start.27 = (f32[64,128]{1,0:T(8,128)S(1)}, f32[64,128]{1,0:T(8,128)S(1)}, u32[]{:S(2)}, u32[]{:S(2)}) collective-permute-start(f32[64,128]{1,0:T(8,128)S(1)} %shard_map.100.correction), channel_id=1, source_target_pairs={{0,8},{1,2},{2,1},{3,11},{4,12},{5,6},{6,5},{7,15},{8,0},{9,17},{1... | collective-permute-start | bytes 98312 | tf_op jit(solution)/shard_map/ppermute | solution.py:530
  50.7 2.0 %collective-permute-start.29 = (f32[64,512]{1,0:T(8,128)S(1)}, f32[64,512]{1,0:T(8,128)S(1)}, u32[]{:S(2)}, u32[]{:S(2)}) collective-permute-start(f32[64,512]{1,0:T(8,128)S(1)} %get-tuple-element.165), channel_id=1, source_target_pairs={{0,8},{1,2},{2,1},{3,11},{4,12},{5,6},{6,5},{7,15},{8,0},{9,17},{1... | collective-permute-start | bytes 393224 | tf_op jit(solution)/shard_map/ppermute | solution.py:530
  53.2 1.2 %shard_map.104 = (f32[64,2048]{1,0:T(8,128)S(1)}, f32[64,2048]{1,0:T(8,128)S(1)}, f32[64,2048]{1,0:T(8,128)S(1)}) custom-call(s32[446]{0:T(512)S(4)} %get-tuple-element.94.table, f32[64,2048]{1,0:T(8,128)S(1)} %get-tuple-element.157.update, f32[64,2048]{1,0:T(8,128)S(1)} %get-tuple-element.158.residual, f32[64,2048]{1,0:T(8,128)S(1)} %get-tuple-element.159.iterate, ...), custom_call_target="tpu_custom_call" | custom-call | flops 335544320 | bytes 4194304 | tf_op jit(solution)/shard_map/pallas_call | solution.py:516
  56.2 1.9 %collective-permute-start.32 = (f32[64,512]{1,0:T(8,128)S(1)}, f32[64,512]{1,0:T(8,128)S(1)}, u32[]{:S(2)}, u32[]{:S(2)}) collective-permute-start(f32[64,512]{1,0:T(8,128)S(1)} %get-tuple-element.173), channel_id=1, source_target_pairs={{0,7},{1,9},{2,10},{3,4},{4,3},{5,13},{6,14},{7,0},{8,15},{9,1},{1... | collective-permute-start | bytes 393224 | tf_op jit(solution)/shard_map/ppermute | solution.py:530
  58.1 2.2 %collective-permute-start.33 = (f32[64,512]{1,0:T(8,128)S(1)}, f32[64,512]{1,0:T(8,128)S(1)}, u32[]{:S(2)}, u32[]{:S(2)}) collective-permute-start(f32[64,512]{1,0:T(8,128)S(1)} %get-tuple-element.176), channel_id=1, source_target_pairs={{0,8},{1,2},{2,1},{3,11},{4,12},{5,6},{6,5},{7,15},{8,0},{9,17},{1... | collective-permute-start | bytes 393224 | tf_op jit(solution)/shard_map/ppermute | solution.py:530
  60.9 1.9 %shard_map.107 = (f32[64,2048]{1,0:T(8,128)S(1)}, f32[64,2048]{1,0:T(8,128)S(1)}, f32[64,2048]{1,0:T(8,128)}) custom-call(s32[446]{0:T(512)S(4)} %get-tuple-element.94.table, f32[64,2048]{1,0:T(8,128)S(1)} %get-tuple-element.168.update, f32[64,2048]{1,0:T(8,128)S(1)} %get-tuple-element.169.residual, f32[64,2048]{1,0:T(8,128)S(1)} %get-tuple-element.170.iterate, ...), custom_call_target="tpu_custom_call" | custom-call | flops 335544320 | bytes 4194304 | tf_op jit(solution)/shard_map/pallas_call | solution.py:516
  (72 shorter events, 17.7 us)
Async XLA Ops:
  1.8 8.4 %collective-permute-start = (f32[72,512]{1,0:T(8,128)S(1)}, f32[72,512]{1,0:T(8,128)S(1)}, u32[]{:S(2)}, u32[]{:S(2)}) collective-permute-start(f32[72,512]{1,0:T(8,128)S(1)} %get-tuple-element.99), channel_id=1, source_target_pairs={{0,7},{1,9},{2,10},{3,4},{4,3},{5,13},{6,14},{7,0},{8,15},{9,1},{1... | collective-permute-start | bytes 442376 | tf_op jit(solution)/shard_map/ppermute | solution.py:530
  5.2 5.2 %collective-permute-start.1 = (f32[72,512]{1,0:T(8,128)S(1)}, f32[72,512]{1,0:T(8,128)S(1)}, u32[]{:S(2)}, u32[]{:S(2)}) collective-permute-start(f32[72,512]{1,0:T(8,128)S(1)} %get-tuple-element.102), channel_id=1, source_target_pairs={{0,8},{1,2},{2,1},{3,11},{4,12},{5,6},{6,5},{7,15},{8,0},{9,17},{1... | collective-permute-start | bytes 442376 | tf_op jit(solution)/shard_map/ppermute | solution.py:530
  6.8 3.7 %collective-permute-start.2 = (f32[72,512]{1,0:T(8,128)S(1)}, f32[72,512]{1,0:T(8,128)S(1)}, u32[]{:S(2)}, u32[]{:S(2)}) collective-permute-start(f32[72,512]{1,0:T(8,128)S(1)} %get-tuple-element.103), channel_id=1, source_target_pairs={{0,1},{1,0},{2,3},{3,2},{4,5},{5,4},{6,7},{7,6},{8,16},{9,10},{10,... | collective-permute-start | bytes 442376 | tf_op jit(solution)/shard_map/ppermute | solution.py:530
  6.8 3.7 %collective-permute-start.3 = (f32[72,512]{1,0:T(8,128)S(1)}, f32[72,512]{1,0:T(8,128)S(1)}, u32[]{:S(2)}, u32[]{:S(2)}) collective-permute-start(f32[72,512]{1,0:T(8,128)S(1)} %get-tuple-element.104), channel_id=1, source_target_pairs={{0,1},{1,0},{2,3},{3,2},{4,5},{5,4},{6,7},{7,6},{8,9},{9,8},{10,11... | collective-permute-start | bytes 442376 | tf_op jit(solution)/shard_map/ppermute | solution.py:530
  11.1 6.8 %collective-permute-start.4 = (f32[64,512]{1,0:T(8,128)S(1)}, f32[64,512]{1,0:T(8,128)S(1)}, u32[]{:S(2)}, u32[]{:S(2)}) collective-permute-start(f32[64,512]{1,0:T(8,128)S(1)} %get-tuple-element.110), channel_id=1, source_target_pairs={{0,7},{1,9},{2,10},{3,4},{4,3},{5,13},{6,14},{7,0},{8,15},{9,1},{1... | collective-permute-start | bytes 393224 | tf_op jit(solution)/shard_map/ppermute | solution.py:530
  12.6 5.5 %collective-permute-start.5 = (f32[64,512]{1,0:T(8,128)S(1)}, f32[64,512]{1,0:T(8,128)S(1)}, u32[]{:S(2)}, u32[]{:S(2)}) collective-permute-start(f32[64,512]{1,0:T(8,128)S(1)} %get-tuple-element.113), channel_id=1, source_target_pairs={{0,8},{1,2},{2,1},{3,11},{4,12},{5,6},{6,5},{7,15},{8,0},{9,17},{1... | collective-permute-start | bytes 393224 | tf_op jit(solution)/shard_map/ppermute | solution.py:530
  14.9 3.3 %collective-permute-start.6 = (f32[64,512]{1,0:T(8,128)S(1)}, f32[64,512]{1,0:T(8,128)S(1)}, u32[]{:S(2)}, u32[]{:S(2)}) collective-permute-start(f32[64,512]{1,0:T(8,128)S(1)} %get-tuple-element.114), channel_id=1, source_target_pairs={{0,1},{1,0},{2,3},{3,2},{4,5},{5,4},{6,7},{7,6},{8,16},{9,10},{10,... | collective-permute-start | bytes 393224 | tf_op jit(solution)/shard_map/ppermute | solution.py:530
  14.9 3.3 %collective-permute-start.7 = (f32[64,512]{1,0:T(8,128)S(1)}, f32[64,512]{1,0:T(8,128)S(1)}, u32[]{:S(2)}, u32[]{:S(2)}) collective-permute-start(f32[64,512]{1,0:T(8,128)S(1)} %get-tuple-element.115), channel_id=1, source_target_pairs={{0,1},{1,0},{2,3},{3,2},{4,5},{5,4},{6,7},{7,6},{8,9},{9,8},{10,11... | collective-permute-start | bytes 393224 | tf_op jit(solution)/shard_map/ppermute | solution.py:530
  18.6 6.4 %collective-permute-start.8 = (f32[64,512]{1,0:T(8,128)S(1)}, f32[64,512]{1,0:T(8,128)S(1)}, u32[]{:S(2)}, u32[]{:S(2)}) collective-permute-start(f32[64,512]{1,0:T(8,128)S(1)} %get-tuple-element.122), channel_id=1, source_target_pairs={{0,7},{1,9},{2,10},{3,4},{4,3},{5,13},{6,14},{7,0},{8,15},{9,1},{1... | collective-permute-start | bytes 393224 | tf_op jit(solution)/shard_map/ppermute | solution.py:530
  20.3 5.0 %collective-permute-start.9 = (f32[64,512]{1,0:T(8,128)S(1)}, f32[64,512]{1,0:T(8,128)S(1)}, u32[]{:S(2)}, u32[]{:S(2)}) collective-permute-start(f32[64,512]{1,0:T(8,128)S(1)} %get-tuple-element.125), channel_id=1, source_target_pairs={{0,8},{1,2},{2,1},{3,11},{4,12},{5,6},{6,5},{7,15},{8,0},{9,17},{1... | collective-permute-start | bytes 393224 | tf_op jit(solution)/shard_map/ppermute | solution.py:530
  25.8 5.6 %collective-permute-start.12 = (f32[64,512]{1,0:T(8,128)S(1)}, f32[64,512]{1,0:T(8,128)S(1)}, u32[]{:S(2)}, u32[]{:S(2)}) collective-permute-start(f32[64,512]{1,0:T(8,128)S(1)} %get-tuple-element.133), channel_id=1, source_target_pairs={{0,7},{1,9},{2,10},{3,4},{4,3},{5,13},{6,14},{7,0},{8,15},{9,1},{1... | collective-permute-start | bytes 393224 | tf_op jit(solution)/shard_map/ppermute | solution.py:530
  27.3 5.0 %collective-permute-start.13 = (f32[64,512]{1,0:T(8,128)S(1)}, f32[64,512]{1,0:T(8,128)S(1)}, u32[]{:S(2)}, u32[]{:S(2)}) collective-permute-start(f32[64,512]{1,0:T(8,128)S(1)} %get-tuple-element.138), channel_id=1, source_target_pairs={{0,8},{1,2},{2,1},{3,11},{4,12},{5,6},{6,5},{7,15},{8,0},{9,17},{1... | collective-permute-start | bytes 393224 | tf_op jit(solution)/shard_map/ppermute | solution.py:530
  29.4 2.9 %collective-permute-start.14 = (f32[64,512]{1,0:T(8,128)S(1)}, f32[64,512]{1,0:T(8,128)S(1)}, u32[]{:S(2)}, u32[]{:S(2)}) collective-permute-start(f32[64,512]{1,0:T(8,128)S(1)} %get-tuple-element.139), channel_id=1, source_target_pairs={{0,1},{1,0},{2,3},{3,2},{4,5},{5,4},{6,7},{7,6},{8,16},{9,10},{10,... | collective-permute-start | bytes 393224 | tf_op jit(solution)/shard_map/ppermute | solution.py:530
  33.0 4.3 %collective-permute-start.19 = (f32[64,128]{1,0:T(8,128)S(1)}, f32[64,128]{1,0:T(8,128)S(1)}, u32[]{:S(2)}, u32[]{:S(2)}) collective-permute-start(f32[64,128]{1,0:T(8,128)S(1)} %get-tuple-element.141.update.iterate), channel_id=1, source_target_pairs={{0,7},{1,9},{2,10},{3,4},{4,3},{5,13},{6,14},{7,0},{8,15},{9,1},{1... | collective-permute-start | bytes 98312 | tf_op jit(solution)/shard_map/ppermute | solution.py:530
  34.5 4.0 %collective-permute-start.18 = (f32[64,128]{1,0:T(8,128)S(1)}, f32[64,128]{1,0:T(8,128)S(1)}, u32[]{:S(2)}, u32[]{:S(2)}) collective-permute-start(f32[64,128]{1,0:T(8,128)S(1)} %get-tuple-element.141.update.iterate), channel_id=1, source_target_pairs={{0,8},{1,2},{2,1},{3,11},{4,12},{5,6},{6,5},{7,15},{8,0},{9,17},{1... | collective-permute-start | bytes 98312 | tf_op jit(solution)/shard_map/ppermute | solution.py:530
  38.7 4.3 %collective-permute-start.23 = (f32[64,128]{1,0:T(8,128)S(1)}, f32[64,128]{1,0:T(8,128)S(1)}, u32[]{:S(2)}, u32[]{:S(2)}) collective-permute-start(f32[64,128]{1,0:T(8,128)S(1)} %get-tuple-element.145.update), channel_id=1, source_target_pairs={{0,7},{1,9},{2,10},{3,4},{4,3},{5,13},{6,14},{7,0},{8,15},{9,1},{1... | collective-permute-start | bytes 98312 | tf_op jit(solution)/shard_map/ppermute | solution.py:530
  39.1 4.0 %collective-permute-start.22 = (f32[64,128]{1,0:T(8,128)S(1)}, f32[64,128]{1,0:T(8,128)S(1)}, u32[]{:S(2)}, u32[]{:S(2)}) collective-permute-start(f32[64,128]{1,0:T(8,128)S(1)} %get-tuple-element.145.update), channel_id=1, source_target_pairs={{0,8},{1,2},{2,1},{3,11},{4,12},{5,6},{6,5},{7,15},{8,0},{9,17},{1... | collective-permute-start | bytes 98312 | tf_op jit(solution)/shard_map/ppermute | solution.py:530
  43.7 5.1 %collective-permute-start.24 = (f32[64,128]{1,0:T(8,128)S(1)}, f32[64,128]{1,0:T(8,128)S(1)}, u32[]{:S(2)}, u32[]{:S(2)}) collective-permute-start(f32[64,128]{1,0:T(8,128)S(1)} %shard_map.100.correction), channel_id=1, source_target_pairs={{0,7},{1,9},{2,10},{3,4},{4,3},{5,13},{6,14},{7,0},{8,15},{9,1},{1... | collective-permute-start | bytes 98312 | tf_op jit(solution)/shard_map/ppermute | solution.py:530
  44.9 4.2 %collective-permute-start.27 = (f32[64,128]{1,0:T(8,128)S(1)}, f32[64,128]{1,0:T(8,128)S(1)}, u32[]{:S(2)}, u32[]{:S(2)}) collective-permute-start(f32[64,128]{1,0:T(8,128)S(1)} %shard_map.100.correction), channel_id=1, source_target_pairs={{0,8},{1,2},{2,1},{3,11},{4,12},{5,6},{6,5},{7,15},{8,0},{9,17},{1... | collective-permute-start | bytes 98312 | tf_op jit(solution)/shard_map/ppermute | solution.py:530
  49.8 5.7 %collective-permute-start.28 = (f32[64,512]{1,0:T(8,128)S(1)}, f32[64,512]{1,0:T(8,128)S(1)}, u32[]{:S(2)}, u32[]{:S(2)}) collective-permute-start(f32[64,512]{1,0:T(8,128)S(1)} %get-tuple-element.162), channel_id=1, source_target_pairs={{0,7},{1,9},{2,10},{3,4},{4,3},{5,13},{6,14},{7,0},{8,15},{9,1},{1... | collective-permute-start | bytes 393224 | tf_op jit(solution)/shard_map/ppermute | solution.py:530
  50.7 5.0 %collective-permute-start.29 = (f32[64,512]{1,0:T(8,128)S(1)}, f32[64,512]{1,0:T(8,128)S(1)}, u32[]{:S(2)}, u32[]{:S(2)}) collective-permute-start(f32[64,512]{1,0:T(8,128)S(1)} %get-tuple-element.165), channel_id=1, source_target_pairs={{0,8},{1,2},{2,1},{3,11},{4,12},{5,6},{6,5},{7,15},{8,0},{9,17},{1... | collective-permute-start | bytes 393224 | tf_op jit(solution)/shard_map/ppermute | solution.py:530
  52.7 3.1 %collective-permute-start.30 = (f32[64,512]{1,0:T(8,128)S(1)}, f32[64,512]{1,0:T(8,128)S(1)}, u32[]{:S(2)}, u32[]{:S(2)}) collective-permute-start(f32[64,512]{1,0:T(8,128)S(1)} %get-tuple-element.166), channel_id=1, source_target_pairs={{0,1},{1,0},{2,3},{3,2},{4,5},{5,4},{6,7},{7,6},{8,16},{9,10},{10,... | collective-permute-start | bytes 393224 | tf_op jit(solution)/shard_map/ppermute | solution.py:530
  56.2 6.6 %collective-permute-start.32 = (f32[64,512]{1,0:T(8,128)S(1)}, f32[64,512]{1,0:T(8,128)S(1)}, u32[]{:S(2)}, u32[]{:S(2)}) collective-permute-start(f32[64,512]{1,0:T(8,128)S(1)} %get-tuple-element.173), channel_id=1, source_target_pairs={{0,7},{1,9},{2,10},{3,4},{4,3},{5,13},{6,14},{7,0},{8,15},{9,1},{1... | collective-permute-start | bytes 393224 | tf_op jit(solution)/shard_map/ppermute | solution.py:530
  58.1 5.2 %collective-permute-start.33 = (f32[64,512]{1,0:T(8,128)S(1)}, f32[64,512]{1,0:T(8,128)S(1)}, u32[]{:S(2)}, u32[]{:S(2)}) collective-permute-start(f32[64,512]{1,0:T(8,128)S(1)} %get-tuple-element.176), channel_id=1, source_target_pairs={{0,8},{1,2},{2,1},{3,11},{4,12},{5,6},{6,5},{7,15},{8,0},{9,17},{1... | collective-permute-start | bytes 393224 | tf_op jit(solution)/shard_map/ppermute | solution.py:530
  (12 other events, 27.6 us)
